TPU v7x, 32 devices: a whole 2x2x4 slice. The times are simulated.
32 devices in a mesh: seq: 8 (over z, y), mp: 4 (over x, core).
Axes of the slice: x: 2, y: 2, z: 4, core: 2. Of those that a mesh axis runs over, the one named last changes fastest.
Arguments:
- tokens: bfloat16 [8192, 1024], P('seq'), may hold values from -6 to 6
- text_states: bfloat16 [8, 128, 1024], replicated, may hold values from -6 to 6
- item_lengths: int32 [8], replicated, may hold values from 768 to 1280, as said below
- prompt_lengths: int32 [8], replicated, may hold values from 8 to 128, as said below
- entry_gain: float32 [1024], replicated, may hold values from 0.5 to 1.5
- entry_bias: float32 [1024], replicated, may hold values from -1 to 1
- cross_gain: float32 [1024], replicated, may hold values from 0.5 to 1.5
- cross_bias: float32 [1024], replicated, may hold values from -1 to 1
- mixer_gain: float32 [1024], replicated, may hold values from 0.5 to 1.5
- mixer_bias: float32 [1024], replicated, may hold values from -1 to 1
- query_weight: bfloat16 [1024, 1024], P(None, 'mp'), may hold values from -0.1875 to 0.1875
- key_weight: bfloat16 [1024, 1024], P(None, 'mp'), may hold values from -0.1875 to 0.1875
- value_weight: bfloat16 [1024, 1024], P(None, 'mp'), may hold values from -0.1875 to 0.1875
- merge_weight: bfloat16 [1024, 1024], P('mp'), may hold values from -0.75 to 0.75
- prompt_query: bfloat16 [1024, 1024], P(None, 'mp'), may hold values from -0.1875 to 0.1875
- prompt_key: bfloat16 [1024, 1024], P(None, 'mp'), may hold values from -0.1875 to 0.1875
- prompt_value: bfloat16 [1024, 1024], P(None, 'mp'), may hold values from -0.1875 to 0.1875
- prompt_merge: bfloat16 [1024, 1024], P('mp'), may hold values from -0.5 to 0.5
- expand_weight: bfloat16 [1024, 4096], P(None, 'mp'), may hold values from -0.1875 to 0.1875
- shrink_weight: bfloat16 [4096, 1024], P('mp'), may hold values from -0.09375 to 0.09375
- output_grad: bfloat16 [8192, 1024], P('seq'), may hold values from -6 to 6
Outputs:
- layer_output: bfloat16 [8192, 1024], P('seq')
- tokens_grad: float32 [8192, 1024], P('seq')
- text_grad: float32 [8, 128, 1024], P(None, None, 'mp')
- entry_gain_grad: float32 [1024], P('seq')
- entry_bias_grad: float32 [1024], P('seq')
- cross_gain_grad: float32 [1024], P('seq')
- cross_bias_grad: float32 [1024], P('seq')
- mixer_gain_grad: float32 [1024], P('seq')
- mixer_bias_grad: float32 [1024], P('seq')
- query_weight_grad: float32 [1024, 1024], P('seq', 'mp')
- key_weight_grad: float32 [1024, 1024], P('seq', 'mp')
- value_weight_grad: float32 [1024, 1024], P('seq', 'mp')
- merge_weight_grad: float32 [1024, 1024], P('mp', 'seq')
- prompt_query_grad: float32 [1024, 1024], P('seq', 'mp')
- prompt_key_grad: float32 [1024, 1024], P(None, 'mp')
- prompt_value_grad: float32 [1024, 1024], P(None, 'mp')
- prompt_merge_grad: float32 [1024, 1024], P('mp', 'seq')
- expand_weight_grad: float32 [1024, 4096], P('seq', 'mp')
- shrink_weight_grad: float32 [4096, 1024], P('mp', 'seq')
Inputs may be any that keep to these rules, and one draw needn't show every extreme that they name: `item_lengths`: the lengths sum to 8192; some item has exactly 1280 tokens and some exactly 768. `prompt_lengths`: some item has exactly 128 live text positions and some exactly 8.
All inputs are finite; a program needn't handle non-finite values.
Results may differ from a plain program's by a relative error of at most 0.028.
Values may be sent and summed in bfloat16 or wider, within the bound.
No kernel may reach another device: no remote copies, remote signals or barrier semaphores. Data moves between devices by JAX's collectives and lax.ppermute only.
A program may use at most 256 MiB of HBM per device.

v0:
```python
import jax
import jax.numpy as jnp
from jax import lax
from jax.sharding import PartitionSpec as P

HD = 64
ITEM_LEN = 1024


EPS = 1e-06
NEGATIVE = -1e30


def from_behind(value, axis, steps):
    count = lax.axis_size(axis)
    leading, last = (max(0, -steps), min(count, count - steps))
    return lax.ppermute(value, axis, [(source, source + steps) for source in range(leading, last)])


def layer_norm(values, gain, bias):
    average = jnp.mean(values, axis=-1, keepdims=True)
    centred = values - average
    spread = jnp.mean(centred * centred, axis=-1, keepdims=True)
    return centred * lax.rsqrt(spread + EPS) * gain + bias


def row_product(left, right):
    return lax.dot_general(
        left, right, (((0,), (0,)), ((), ())), preferred_element_type=jnp.float32
    )


def col_product(left, right):
    return lax.dot_general(
        left, right, (((1,), (1,)), ((), ())), preferred_element_type=jnp.float32
    )


def matmul(left, right):
    return jnp.dot(left, right, preferred_element_type=jnp.float32)


def model_sum(partial_sum):
    return lax.psum(partial_sum.astype(jnp.bfloat16), "mp").astype(jnp.float32)


def body(
    tokens,
    text_states,
    item_lengths,
    prompt_lengths,
    entry_gain,
    entry_bias,
    cross_gain,
    cross_bias,
    mixer_gain,
    mixer_bias,
    query_weight,
    key_weight,
    value_weight,
    merge_weight,
    prompt_query,
    prompt_key,
    prompt_value,
    prompt_merge,
    expand_weight,
    shrink_weight,
    output_grad,
):
    local_rows = tokens.shape[0]
    shards = lax.axis_size("seq")
    width = query_weight.shape[1]
    head_size = HD
    head_count = width // head_size
    score_scale = head_size ** (-0.5)
    item_count = item_lengths.shape[0]
    prompt_rows = text_states.shape[1]
    model_width = text_states.shape[2]
    longest = ITEM_LEN + ITEM_LEN // 4
    shortest = ITEM_LEN - ITEM_LEN // 4
    reach = min((longest + local_rows - 2) // local_rows, shards - 1)
    slots = min((local_rows - 2) // shortest + 2, item_count)
    window_rows = (reach + 1) * local_rows
    front_rows = reach * local_rows
    offset = lax.axis_index("seq") * local_rows
    positions = offset + jnp.arange(local_rows, dtype=jnp.int32)
    item_ends = jnp.cumsum(item_lengths)
    item_starts = item_ends - item_lengths
    item_of = jnp.sum((positions[:, None] >= item_ends[None, :]).astype(jnp.int32), axis=1)
    choose = item_of[:, None] == jnp.arange(item_count, dtype=jnp.int32)[None, :]
    start_of = jnp.sum(jnp.where(choose, item_starts[None, :], 0), axis=1)
    columns = offset - front_rows + jnp.arange(window_rows, dtype=jnp.int32)
    allowed = ((columns[None, :] <= positions[:, None]) & (columns[None, :] >= start_of[:, None]))[
        None
    ]
    residual = tokens.astype(jnp.float32)
    normed_one, entry_pull = jax.vjp(layer_norm, residual, entry_gain, entry_bias)
    hidden_one = normed_one.astype(jnp.bfloat16)
    queries = matmul(hidden_one, query_weight).astype(jnp.bfloat16)
    keys = matmul(hidden_one, key_weight).astype(jnp.bfloat16)
    value_rows = matmul(hidden_one, value_weight).astype(jnp.bfloat16)
    stacked = jnp.stack([keys, value_rows])
    pieces = [stacked]
    for step in range(1, reach + 1):
        pieces.insert(0, from_behind(stacked, "seq", step))
    window = jnp.concatenate(pieces, axis=1)
    window_keys = window[0].reshape(window_rows, head_count, head_size)
    window_values = window[1].reshape(window_rows, head_count, head_size)
    query_heads = queries.reshape(local_rows, head_count, head_size)

    def window_scores():
        return (
            jnp.einsum("qhd,khd->hqk", query_heads, window_keys, preferred_element_type=jnp.float32)
            * score_scale
        )

    def window_probs(scores, log_total):
        return jnp.where(allowed, jnp.exp(scores - log_total[:, :, None]), 0.0)

    scores = window_scores()
    masked = jnp.where(allowed, scores, NEGATIVE)
    maxima = jnp.max(masked, axis=2)
    totals = jnp.sum(jnp.where(allowed, jnp.exp(masked - maxima[:, :, None]), 0.0), axis=2)
    log_total = maxima + jnp.log(totals)
    probs = window_probs(scores, log_total)
    self_out = jnp.einsum(
        "hqk,khd->qhd",
        probs.astype(jnp.bfloat16),
        window_values,
        preferred_element_type=jnp.float32,
    )
    self_low = self_out.reshape(local_rows, width).astype(jnp.bfloat16)
    after_self = residual + model_sum(matmul(self_low, merge_weight))
    normed_two, cross_pull = jax.vjp(layer_norm, after_self, cross_gain, cross_bias)
    hidden_two = normed_two.astype(jnp.bfloat16)
    cross_queries = matmul(hidden_two, prompt_query).astype(jnp.bfloat16)
    base = jnp.minimum(item_of[0], item_count - slots)
    slot_text = lax.dynamic_slice_in_dim(text_states, base, slots, 0).reshape(
        slots * prompt_rows, model_width
    )
    slot_lengths = lax.dynamic_slice_in_dim(prompt_lengths, base, slots, 0)
    cross_keys = matmul(slot_text, prompt_key).astype(jnp.bfloat16)
    cross_values = matmul(slot_text, prompt_value).astype(jnp.bfloat16)
    key_item = base + jnp.arange(slots * prompt_rows, dtype=jnp.int32) // prompt_rows
    live = (jnp.arange(prompt_rows, dtype=jnp.int32)[None, :] < slot_lengths[:, None]).reshape(-1)
    cross_allowed = ((item_of[:, None] == key_item[None, :]) & live[None, :])[None]
    cross_query_heads = cross_queries.reshape(local_rows, head_count, head_size)
    cross_key_heads = cross_keys.reshape(-1, head_count, head_size)
    cross_value_heads = cross_values.reshape(-1, head_count, head_size)
    cross_scores = (
        jnp.einsum(
            "qhd,khd->hqk", cross_query_heads, cross_key_heads, preferred_element_type=jnp.float32
        )
        * score_scale
    )
    cross_scores = jnp.where(cross_allowed, cross_scores, NEGATIVE)
    cross_top = jnp.max(cross_scores, axis=2, keepdims=True)
    cross_unnorm = jnp.where(cross_allowed, jnp.exp(cross_scores - cross_top), 0.0)
    cross_probs = cross_unnorm / jnp.sum(cross_unnorm, axis=2, keepdims=True)
    cross_low_probs = cross_probs.astype(jnp.bfloat16)
    cross_out = (
        jnp.einsum(
            "hqk,khd->qhd", cross_low_probs, cross_value_heads, preferred_element_type=jnp.float32
        )
        .reshape(local_rows, width)
        .astype(jnp.bfloat16)
    )
    after_cross = after_self + model_sum(matmul(cross_out, prompt_merge))
    normed_three, mixer_pull = jax.vjp(layer_norm, after_cross, mixer_gain, mixer_bias)
    hidden_three = normed_three.astype(jnp.bfloat16)
    hidden_pre = matmul(hidden_three, expand_weight)
    hidden_act, gelu_pull = jax.vjp(jax.nn.gelu, hidden_pre)
    hidden_low = hidden_act.astype(jnp.bfloat16)
    layer_output = (after_cross + model_sum(matmul(hidden_low, shrink_weight))).astype(jnp.bfloat16)
    shrink_grad = row_product(hidden_low, output_grad)
    pre_grad = gelu_pull(col_product(output_grad, shrink_weight))[0].astype(jnp.bfloat16)
    expand_grad = row_product(hidden_three, pre_grad)
    three_grad = model_sum(col_product(pre_grad, expand_weight))
    mixer_part, mixer_gain_grad, mixer_bias_grad = mixer_pull(three_grad)
    cross_resid_grad = output_grad.astype(jnp.float32) + mixer_part
    cross_out_grad = cross_resid_grad.astype(jnp.bfloat16)
    merge_cross_grad = row_product(cross_out, cross_out_grad)
    cross_head_grad = (
        col_product(cross_out_grad, prompt_merge)
        .astype(jnp.bfloat16)
        .reshape(local_rows, head_count, head_size)
    )
    cross_prob_grad = jnp.einsum(
        "qhd,khd->hqk", cross_head_grad, cross_value_heads, preferred_element_type=jnp.float32
    )
    cross_row_delta = jnp.sum(cross_probs * cross_prob_grad, axis=2, keepdims=True)
    cross_score_grad = (cross_probs * (cross_prob_grad - cross_row_delta)).astype(jnp.bfloat16)
    cross_query_grad = (
        (
            jnp.einsum(
                "hqk,khd->qhd",
                cross_score_grad,
                cross_key_heads,
                preferred_element_type=jnp.float32,
            )
            * score_scale
        )
        .reshape(local_rows, width)
        .astype(jnp.bfloat16)
    )
    key_part = (
        jnp.einsum(
            "hqk,qhd->khd", cross_score_grad, cross_query_heads, preferred_element_type=jnp.float32
        )
        * score_scale
    ).reshape(slots, prompt_rows, width)
    value_part = jnp.einsum(
        "hqk,qhd->khd", cross_low_probs, cross_head_grad, preferred_element_type=jnp.float32
    ).reshape(slots, prompt_rows, width)
    placed_text = lax.dynamic_update_slice_in_dim(
        jnp.zeros((2, item_count, prompt_rows, width), jnp.float32),
        jnp.stack([key_part, value_part]),
        base,
        1,
    )
    text_sums = lax.psum(placed_text.astype(jnp.bfloat16), "seq").astype(jnp.float32)
    cross_key_grad = text_sums[0].reshape(item_count * prompt_rows, width).astype(jnp.bfloat16)
    cross_value_grad = text_sums[1].reshape(item_count * prompt_rows, width).astype(jnp.bfloat16)
    flat_text = text_states.reshape(item_count * prompt_rows, model_width)
    prompt_key_grad = row_product(flat_text, cross_key_grad)
    prompt_value_grad = row_product(flat_text, cross_value_grad)
    text_part = col_product(cross_key_grad, prompt_key) + col_product(
        cross_value_grad, prompt_value
    )
    text_grad = (
        lax.psum_scatter(text_part.astype(jnp.bfloat16), "mp", scatter_dimension=1, tiled=True)
        .astype(jnp.float32)
        .reshape(item_count, prompt_rows, -1)
    )
    query_cross_grad = row_product(hidden_two, cross_query_grad)
    two_grad = model_sum(col_product(cross_query_grad, prompt_query))
    cross_part, cross_gain_grad, cross_bias_grad = cross_pull(two_grad)
    self_resid_grad = cross_resid_grad + cross_part
    self_low_grad = self_resid_grad.astype(jnp.bfloat16)
    merge_grad = row_product(self_low, self_low_grad)
    self_head_grad = (
        col_product(self_low_grad, merge_weight)
        .astype(jnp.bfloat16)
        .reshape(local_rows, head_count, head_size)
    )
    self_delta = jnp.sum(self_head_grad.astype(jnp.float32) * self_out, axis=2).T
    back_probs = window_probs(window_scores(), log_total)
    prob_grad = jnp.einsum(
        "qhd,khd->hqk", self_head_grad, window_values, preferred_element_type=jnp.float32
    )
    score_grad = (back_probs * (prob_grad - self_delta[:, :, None])).astype(jnp.bfloat16)
    query_accum = jnp.einsum(
        "hqk,khd->qhd", score_grad, window_keys, preferred_element_type=jnp.float32
    )
    key_terms = (
        jnp.einsum("hqk,qhd->khd", score_grad, query_heads, preferred_element_type=jnp.float32)
        * score_scale
    )
    value_terms = jnp.einsum(
        "hqk,qhd->khd",
        back_probs.astype(jnp.bfloat16),
        self_head_grad,
        preferred_element_type=jnp.float32,
    )
    terms = jnp.stack(
        [key_terms.reshape(window_rows, width), value_terms.reshape(window_rows, width)]
    )
    kv_sums = terms[:, front_rows:]
    for step in range(1, reach + 1):
        lower = (reach - step) * local_rows
        kv_sums = kv_sums + from_behind(
            terms[:, lower : lower + local_rows].astype(jnp.bfloat16), "seq", -step
        ).astype(jnp.float32)
    query_grad = (query_accum * score_scale).reshape(local_rows, width).astype(jnp.bfloat16)
    key_grad = kv_sums[0].astype(jnp.bfloat16)
    value_grad = kv_sums[1].astype(jnp.bfloat16)
    query_grad_weight = row_product(hidden_one, query_grad)
    key_grad_weight = row_product(hidden_one, key_grad)
    value_grad_weight = row_product(hidden_one, value_grad)
    one_part = (
        col_product(query_grad, query_weight)
        + col_product(key_grad, key_weight)
        + col_product(value_grad, value_weight)
    )
    one_grad = model_sum(one_part)
    entry_part, entry_gain_grad, entry_bias_grad = entry_pull(one_grad)
    tokens_grad = self_resid_grad + entry_part
    summed = (
        lax.psum_scatter(
            entry_gain_grad.astype(jnp.bfloat16), "seq", scatter_dimension=0, tiled=True
        ).astype(jnp.float32),
        lax.psum_scatter(
            entry_bias_grad.astype(jnp.bfloat16), "seq", scatter_dimension=0, tiled=True
        ).astype(jnp.float32),
        lax.psum_scatter(
            cross_gain_grad.astype(jnp.bfloat16), "seq", scatter_dimension=0, tiled=True
        ).astype(jnp.float32),
        lax.psum_scatter(
            cross_bias_grad.astype(jnp.bfloat16), "seq", scatter_dimension=0, tiled=True
        ).astype(jnp.float32),
        lax.psum_scatter(
            mixer_gain_grad.astype(jnp.bfloat16), "seq", scatter_dimension=0, tiled=True
        ).astype(jnp.float32),
        lax.psum_scatter(
            mixer_bias_grad.astype(jnp.bfloat16), "seq", scatter_dimension=0, tiled=True
        ).astype(jnp.float32),
        lax.psum_scatter(
            query_grad_weight.astype(jnp.bfloat16), "seq", scatter_dimension=0, tiled=True
        ).astype(jnp.float32),
        lax.psum_scatter(
            key_grad_weight.astype(jnp.bfloat16), "seq", scatter_dimension=0, tiled=True
        ).astype(jnp.float32),
        lax.psum_scatter(
            value_grad_weight.astype(jnp.bfloat16), "seq", scatter_dimension=0, tiled=True
        ).astype(jnp.float32),
        lax.psum_scatter(
            merge_grad.astype(jnp.bfloat16), "seq", scatter_dimension=1, tiled=True
        ).astype(jnp.float32),
        lax.psum_scatter(
            query_cross_grad.astype(jnp.bfloat16), "seq", scatter_dimension=0, tiled=True
        ).astype(jnp.float32),
        lax.psum_scatter(
            merge_cross_grad.astype(jnp.bfloat16), "seq", scatter_dimension=1, tiled=True
        ).astype(jnp.float32),
        lax.psum_scatter(
            expand_grad.astype(jnp.bfloat16), "seq", scatter_dimension=0, tiled=True
        ).astype(jnp.float32),
        lax.psum_scatter(
            shrink_grad.astype(jnp.bfloat16), "seq", scatter_dimension=1, tiled=True
        ).astype(jnp.float32),
    )
    (
        entry_gain_sum,
        entry_bias_sum,
        cross_gain_sum,
        cross_bias_sum,
        mixer_gain_sum,
        mixer_bias_sum,
        query_sum,
        key_sum_w,
        value_sum_w,
        merge_sum,
        cross_query_sum,
        cross_merge_sum,
        expand_sum,
        shrink_sum,
    ) = summed
    return (
        layer_output,
        tokens_grad,
        text_grad,
        entry_gain_sum,
        entry_bias_sum,
        cross_gain_sum,
        cross_bias_sum,
        mixer_gain_sum,
        mixer_bias_sum,
        query_sum,
        key_sum_w,
        value_sum_w,
        merge_sum,
        cross_query_sum,
        prompt_key_grad,
        prompt_value_grad,
        cross_merge_sum,
        expand_sum,
        shrink_sum,
    )


def solution(mesh):
    return jax.shard_map(
        body,
        mesh=mesh,
        in_specs=(
            P("seq", None),
            P(),
            P(),
            P(),
            P(),
            P(),
            P(),
            P(),
            P(),
            P(),
            P(None, "mp"),
            P(None, "mp"),
            P(None, "mp"),
            P("mp", None),
            P(None, "mp"),
            P(None, "mp"),
            P(None, "mp"),
            P("mp", None),
            P(None, "mp"),
            P("mp", None),
            P("seq", None),
        ),
        out_specs=(
            P("seq", None),
            P("seq", None),
            P(None, None, "mp"),
            P("seq"),
            P("seq"),
            P("seq"),
            P("seq"),
            P("seq"),
            P("seq"),
            P("seq", "mp"),
            P("seq", "mp"),
            P("seq", "mp"),
            P("mp", "seq"),
            P("seq", "mp"),
            P(None, "mp"),
            P(None, "mp"),
            P("mp", "seq"),
            P("seq", "mp"),
            P("mp", "seq"),
        ),
        check_vma=False,
    )
```

profile of v0, /device:TPU:0, one launch (start us, length us, event | category | flops | bytes accessed | tf_op | source)
XLA Modules:
  0.0 1192.7 jit_solution(16131627947864065906)
XLA Ops:
  34.8 8.6 collective-permute-done.1
  55.6 20.4 %select_reduce_fusion.1 = (f32[4,1024]{1,0:T(4,128)S(1)}, f32[4,1024,3072]{2,1,0:T(8,128)}) fusion(pred[1024,3072]{1,0:T(8,128)(4,1)} %compare_and_fusion, bf16[1024,4,64]{0,2,1:T(8,128)(2,1)S(1)} %bitcast.161, bf16[3072,4,64]{0,2,1:T(8,128)(2,1)} %bitcast.168), kind=kOutput, calls=%fused_computation.4 | convolution fusion | flops 1648357376 | bytes 55590912 | tf_op jit(solution)/shard_map/qhd,khd->hqk/dot_general | solution.py:113
  76.0 24.2 %select_reduce_fusion = f32[4,1024]{1,0:T(4,128)S(1)} fusion(f32[4,1024,3072]{2,1,0:T(8,128)} %get-tuple-element.120, f32[4,1024]{1,0:T(4,128)S(1)} %get-tuple-element.119, pred[1024,3072]{1,0:T(8,128)(4,1)} %compare_and_fusion), kind=kLoop, calls=%fused_computation.3 | loop fusion | flops 62910464 | bytes 53510144 | tf_op jit(solution)/shard_map/reduce_sum | solution.py:123
  100.8 20.5 %fusion.90 = (bf16[1024,4,64]{0,2,1:T(8,128)(2,1)S(1)}, f32[1024,4,64]{0,2,1:T(8,128)}) fusion(bf16[3072,4,64]{0,2,1:T(8,128)(2,1)} %bitcast.182, f32[4,1024,3072]{2,1,0:T(8,128)} %get-tuple-element.120, f32[4,1024]{1,0:T(4,128)S(1)} %log_add_fusion, pred[1024,3072]{1,0:T(8,128)(4,1)} %compare_and_fusion), kind=kOutput, calls=%fused_computation.190 | convolution fusion | flops 1661206528 | bytes 56639488 | tf_op jit(solution)/shard_map/hqk,khd->qhd/dot_general | solution.py:126
  129.2 67.9 %all-reduce.15.cloned.1.call-done = bf16[1024,1024]{1,0:T(8,128)(2,1)} async-done(((bf16[1024,1024]{1,0:T(8,128)(2,1)}), bf16[1024,1024]{1,0:T(8,128)(2,1)}) %all-reduce.15.cloned.1.call-update) | async-done | bytes 2097168 | tf_op jit(solution)/shard_map/psum | solution.py:44
  224.6 45.0 %all-reduce.17.cloned.1.call-done = bf16[1024,1024]{1,0:T(8,128)(2,1)} async-done(((bf16[1024,1024]{1,0:T(8,128)(2,1)}), bf16[1024,1024]{1,0:T(8,128)(2,1)}) %all-reduce.17.cloned.1.call-update) | async-done | bytes 2097168 | tf_op jit(solution)/shard_map/psum | solution.py:44
  289.2 51.4 %all-reduce.19.cloned.1.call-done = bf16[1024,1024]{1,0:T(8,128)(2,1)} async-done(((bf16[1024,1024]{1,0:T(8,128)(2,1)}), bf16[1024,1024]{1,0:T(8,128)(2,1)}) %all-reduce.19.cloned.1.call-update) | async-done | bytes 2097168 | tf_op jit(solution)/shard_map/psum | solution.py:44
  368.1 11.4 dynamic_update_slice.3
  387.8 23.9 %all-reduce.21.cloned.1.call-done = bf16[1024,1024]{1,0:T(8,128)(2,1)} async-done(((bf16[1024,1024]{1,0:T(8,128)(2,1)}), bf16[1024,1024]{1,0:T(8,128)(2,1)}) %all-reduce.21.cloned.1.call-update) | async-done | bytes 2097168 | tf_op jit(solution)/shard_map/psum | solution.py:44
  428.7 30.7 %multiply_convert_fusion = bf16[4,1024,3072]{2,1,0:T(8,128)(2,1)} fusion(f32[4,1024,3072]{2,1,0:T(8,128)} %get-tuple-element.120, bf16[1024,4,64]{0,2,1:T(8,128)(2,1)S(1)} %bitcast.187, bf16[3072,4,64]{0,2,1:T(8,128)(2,1)} %bitcast.183, f32[4,1024]{1,0:T(4,128)S(1)} %bitcast.198, f32[4,1024]{1,0:T(4,128)S(1)} %copy-done.71, ...), kind=kOutput, calls=%fused_computation.1 | convolution fusion | flops 1686110208 | bytes 80773120 | tf_op jit(solution)/shard_map/qhd,khd->hqk/dot_general | solution.py:248
  459.4 13.0 %fusion.45 = bf16[4,64,1024]{2,1,0:T(8,128)(2,1)S(1)} fusion(bf16[3072,4,64]{0,2,1:T(8,128)(2,1)} %bitcast.169, bf16[4,1024,3072]{2,1,0:T(8,128)(2,1)} %multiply_convert_fusion), kind=kOutput, calls=%fused_computation.99 | convolution fusion | flops 1611137024 | bytes 27262976 | tf_op jit(solution)/shard_map/hqk,khd->qhd/dot_general | solution.py:252
  494.4 21.1 %fusion.80 = f32[4,64,3072]{2,1,0:T(8,128)} fusion(bf16[1024,4,64]{0,2,1:T(8,128)(2,1)S(1)} %bitcast.188, f32[4,1024,3072]{2,1,0:T(8,128)} %get-tuple-element.120, f32[4,1024]{1,0:T(4,128)S(1)} %copy-done.71, pred[1024,3072]{1,0:T(8,128)(4,1)} %compare_and_fusion), kind=kOutput, calls=%fused_computation.182 | convolution fusion | flops 1660944384 | bytes 57163776 | tf_op jit(solution)/shard_map/hqk,qhd->khd/dot_general | solution.py:259
  515.4 10.7 convolution_multiply_fusion
  529.8 24.4 %collective-permute-done.2 = bf16[2,1024,256]{1,2,0:T(8,128)(2,1)S(1)} collective-permute-done((bf16[2,1024,256]{1,2,0:T(8,128)(2,1)S(1)}, bf16[2,1024,256]{1,2,0:T(8,128)(2,1)S(1)}, u32[]{:S(2)}, u32[]{:S(2)}) %collective-permute-start.2) | collective-permute-done | bytes 1048608 | tf_op jit(solution)/shard_map/ppermute | solution.py:17
  554.2 25.1 %collective-permute-done.3 = bf16[2,1024,256]{1,2,0:T(8,128)(2,1)S(1)} collective-permute-done((bf16[2,1024,256]{1,2,0:T(8,128)(2,1)S(1)}, bf16[2,1024,256]{1,2,0:T(8,128)(2,1)S(1)}, u32[]{:S(2)}, u32[]{:S(2)}) %collective-permute-start.3) | collective-permute-done | bytes 1048608 | tf_op jit(solution)/shard_map/ppermute | solution.py:17
  620.3 21.0 %reduce-scatter.24.cloned.1.call-done = bf16[128,256]{1,0:T(8,128)(2,1)} async-done(((bf16[1024,256]{1,0:T(8,128)(2,1)}), bf16[128,256]{1,0:T(8,128)(2,1)}) %reduce-scatter.24.cloned.1.call-update) | async-done | bytes 65552 | tf_op jit(solution)/shard_map/reduce_scatter | solution.py:319
  642.7 63.2 %reduce-scatter.28.cloned.1.call-done = bf16[128,256]{1,0:T(8,128)(2,1)} async-done(((bf16[1024,256]{1,0:T(8,128)(2,1)}), bf16[128,256]{1,0:T(8,128)(2,1)}) %reduce-scatter.28.cloned.1.call-update) | async-done | bytes 65552
  707.5 62.7 %reduce-scatter.18.cloned.1.call-done = bf16[128,256]{1,0:T(8,128)(2,1)} async-done(((bf16[1024,256]{1,0:T(8,128)(2,1)}), bf16[128,256]{1,0:T(8,128)(2,1)}) %reduce-scatter.18.cloned.1.call-update) | async-done | bytes 65552 | tf_op jit(solution)/shard_map/reduce_scatter | solution.py:307
  771.7 69.2 %reduce-scatter.32.cloned.1.call-done = bf16[128,1024]{1,0:T(8,128)(2,1)} async-done(((bf16[1024,1024]{1,0:T(8,128)(2,1)}), bf16[128,1024]{1,0:T(8,128)(2,1)}) %reduce-scatter.32.cloned.1.call-update) | async-done | bytes 262160
  842.9 68.8 %reduce-scatter.26.cloned.1.call-done = bf16[128,1024]{1,0:T(8,128)(2,1)} async-done(((bf16[1024,1024]{1,0:T(8,128)(2,1)}), bf16[128,1024]{1,0:T(8,128)(2,1)}) %reduce-scatter.26.cloned.1.call-update) | async-done | bytes 262160 | tf_op jit(solution)/shard_map/reduce_scatter | solution.py:325
  913.5 62.7 %reduce-scatter.22.cloned.1.call-done = bf16[128,256]{1,0:T(8,128)(2,1)} async-done(((bf16[1024,256]{1,0:T(8,128)(2,1)}), bf16[128,256]{1,0:T(8,128)(2,1)}) %reduce-scatter.22.cloned.1.call-update) | async-done | bytes 65552 | tf_op jit(solution)/shard_map/reduce_scatter | solution.py:313
  977.7 62.8 %reduce-scatter.20.cloned.1.call-done = bf16[128,256]{1,0:T(8,128)(2,1)} async-done(((bf16[1024,256]{1,0:T(8,128)(2,1)}), bf16[128,256]{1,0:T(8,128)(2,1)}) %reduce-scatter.20.cloned.1.call-update) | async-done | bytes 65552 | tf_op jit(solution)/shard_map/reduce_scatter | solution.py:310
  1042.0 86.2 %all-reduce.25.cloned.1.call-done = (bf16[1024,1024]{1,0:T(8,128)(2,1)}, bf16[1024,1024]{1,0:T(8,128)(2,1)}) async-done(((bf16[1024,1024]{1,0:T(8,128)(2,1)}, bf16[1024,1024]{1,0:T(8,128)(2,1)}), (bf16[1024,1024]{1,0:T(8,128)(2,1)}, bf16[1024,1024]{1,0:T(8,128)(2,1)})) %all-reduce.25.cloned.1.call-update) | async-done | bytes 4194320 | tf_op jit(solution)/shard_map/psum | solution.py:44
  1135.7 37.1 %all-reduce.6 = (bf16[1024]{0:T(1024)(128)(2,1)S(1)}, bf16[1024]{0:T(1024)(128)(2,1)S(1)}, bf16[1024]{0:T(1024)(128)(2,1)S(1)}, bf16[1024]{0:T(1024)(128)(2,1)S(...) all-reduce(bf16[1024]{0:T(1024)(128)(2,1)S(1)} %get-tuple-element.9, ...), channel_id=3, replica_groups=mesh['seq'=8,'mp'=4] {'seq'}, use_global_device_ids=true, to_apply=%region_30.31.clone | all-reduce | flops 6144 | bytes 24576
  (337 shorter events, 244.0 us)
Async XLA Ops:
  7.2 266.7 %copy-start = (bf16[1024,1024]{1,0:T(8,128)(2,1)S(1)}, bf16[1024,1024]{1,0:T(8,128)(2,1)}, u32[]{:S(2)}) copy-start(bf16[1024,1024]{1,0:T(8,128)(2,1)} %param.39) | copy-start | bytes 6291460
  7.2 189.9 %all-reduce.15.cloned.1.call-start = ((), (), s32[]{:S(2)}) async-start(), calls=%async_computation.9 | async-start | bytes 4194304 | tf_op jit(solution)/shard_map/psum | solution.py:44
  15.8 27.6 %collective-permute-start.1 = (bf16[2,1024,256]{2,1,0:T(8,128)(2,1)}, bf16[2,1024,256]{2,1,0:T(8,128)(2,1)}, u32[]{:S(2)}, u32[]{:S(2)}) collective-permute-start(bf16[2,1024,256]{2,1,0:T(8,128)(2,1)} %pad_maximum_fusion.1), channel_id=1, source_target_pairs={{0,4},{4,8},{8,12},{12,16},{16,20},{20,24},{24,28},{1,5},{5,9},{9,... | collective-permute-start | bytes 3145736 | tf_op jit(solution)/shard_map/ppermute | solution.py:17
  21.7 25.0 %collective-permute-start = (bf16[2,1024,256]{2,1,0:T(8,128)(2,1)}, bf16[2,1024,256]{2,1,0:T(8,128)(2,1)}, u32[]{:S(2)}, u32[]{:S(2)}) collective-permute-start(bf16[2,1024,256]{2,1,0:T(8,128)(2,1)} %pad_maximum_fusion.1), channel_id=1, source_target_pairs={{0,8},{4,12},{8,16},{12,20},{16,24},{20,28},{1,9},{5,13},{9,17},{1... | collective-permute-start | bytes 3145736 | tf_op jit(solution)/shard_map/ppermute | solution.py:17
  124.2 145.4 %all-reduce.17.cloned.1.call-start = ((), (), s32[]{:S(2)}) async-start(), calls=%async_computation.10 | async-start | bytes 4194304 | tf_op jit(solution)/shard_map/psum | solution.py:44
  217.9 122.6 %all-reduce.19.cloned.1.call-start = ((), (), s32[]{:S(2)}) async-start(), calls=%async_computation.11 | async-start | bytes 4194304 | tf_op jit(solution)/shard_map/psum | solution.py:44
  289.0 122.7 %all-reduce.21.cloned.1.call-start = ((), (), s32[]{:S(2)}) async-start(), calls=%async_computation.12 | async-start | bytes 4194304 | tf_op jit(solution)/shard_map/psum | solution.py:44
  360.1 235.3 %all-reduce.23.cloned.1.call-start = ((), (), s32[]{:S(2)}) async-start(), calls=%async_computation.13 | async-start | bytes 2097152 | tf_op jit(solution)/shard_map/psum | solution.py:221
  380.5 224.5 %reduce-scatter.30.cloned.1.call-start = ((), (), s32[]{:S(2)}) async-start(), calls=%async_computation.21 | async-start | bytes 589824
  384.1 257.1 %reduce-scatter.24.cloned.1.call-start = ((), (), s32[]{:S(2)}) async-start(), calls=%async_computation.18 | async-start | bytes 589824 | tf_op jit(solution)/shard_map/reduce_scatter | solution.py:319
  387.4 318.6 %reduce-scatter.28.cloned.1.call-start = ((), (), s32[]{:S(2)}) async-start(), calls=%async_computation.20 | async-start | bytes 589824
  428.0 342.3 %reduce-scatter.18.cloned.1.call-start = ((), (), s32[]{:S(2)}) async-start(), calls=%async_computation.15 | async-start | bytes 589824 | tf_op jit(solution)/shard_map/reduce_scatter | solution.py:307
  475.8 365.1 %reduce-scatter.32.cloned.1.call-start = ((), (), s32[]{:S(2)}) async-start(), calls=%async_computation.22 | async-start | bytes 2359296
  487.0 424.7 %reduce-scatter.26.cloned.1.call-start = ((), (), s32[]{:S(2)}) async-start(), calls=%async_computation.19 | async-start | bytes 2359296 | tf_op jit(solution)/shard_map/reduce_scatter | solution.py:325
  494.3 481.9 %reduce-scatter.22.cloned.1.call-start = ((), (), s32[]{:S(2)}) async-start(), calls=%async_computation.17 | async-start | bytes 589824 | tf_op jit(solution)/shard_map/reduce_scatter | solution.py:313
  527.1 27.1 %collective-permute-start.2 = (bf16[2,1024,256]{1,2,0:T(8,128)(2,1)S(1)}, bf16[2,1024,256]{1,2,0:T(8,128)(2,1)S(1)}, u32[]{:S(2)}, u32[]{:S(2)}) collective-permute-start(bf16[2,1024,256]{1,2,0:T(8,128)(2,1)S(1)} %get-tuple-element.113), channel_id=1, source_target_pairs={{4,0},{8,4},{12,8},{16,12},{20,16},{24,20},{28,24},{5,1},{9,5},{13... | collective-permute-start | bytes 3145736 | tf_op jit(solution)/shard_map/ppermute | solution.py:17
  528.4 50.9 %collective-permute-start.3 = (bf16[2,1024,256]{1,2,0:T(8,128)(2,1)S(1)}, bf16[2,1024,256]{1,2,0:T(8,128)(2,1)S(1)}, u32[]{:S(2)}, u32[]{:S(2)}) collective-permute-start(bf16[2,1024,256]{1,2,0:T(8,128)(2,1)S(1)} %get-tuple-element.114), channel_id=1, source_target_pairs={{8,0},{12,4},{16,8},{20,12},{24,16},{28,20},{9,1},{13,5},{17,9},{2... | collective-permute-start | bytes 3145736 | tf_op jit(solution)/shard_map/ppermute | solution.py:17
  581.5 459.0 %reduce-scatter.20.cloned.1.call-start = ((), (), s32[]{:S(2)}) async-start(), calls=%async_computation.16 | async-start | bytes 589824 | tf_op jit(solution)/shard_map/reduce_scatter | solution.py:310
  590.2 538.0 %all-reduce.25.cloned.1.call-start = ((), (), s32[]{:S(2)}) async-start(), calls=%async_computation.23 | async-start | bytes 8388608 | tf_op jit(solution)/shard_map/psum | solution.py:44
  595.2 588.7 %reduce-scatter.16.cloned.1.call-start = ((), (), s32[]{:S(2)}) async-start(), calls=%async_computation.14 | async-start | bytes 2621440 | tf_op jit(solution)/shard_map/reduce_scatter | solution.py:231
  618.3 511.9 %copy-start.55 = (f32[1024]{0:T(1024)S(1)}, f32[1024]{0:T(1024)}, u32[]{:S(2)}) copy-start(f32[1024]{0:T(1024)} %copy-done.54) | copy-start | bytes 12292
  618.3 511.9 %copy-start.58 = (f32[1024]{0:T(1024)S(1)}, f32[1024]{0:T(1024)}, u32[]{:S(2)}) copy-start(f32[1024]{0:T(1024)} %param.25) | copy-start | bytes 12292
  842.0 290.9 %copy-start.64 = (f32[1024]{0:T(1024)S(1)}, f32[1024]{0:T(1024)}, u32[]{:S(2)}) copy-start(f32[1024]{0:T(1024)} %copy-done.63) | copy-start | bytes 12292
  842.0 290.9 %copy-start.60 = (f32[1024]{0:T(1024)S(1)}, f32[1024]{0:T(1024)}, u32[]{:S(2)}) copy-start(f32[1024]{0:T(1024)} %copy-done.59) | copy-start | bytes 12292
  (85 other events, 681.2 us)
Sparse Core Ops, SparseCore 0:
  124.3 72.7 all-reduce.14
  218.1 51.4 all-reduce.16
  289.1 51.4 all-reduce.18
  360.2 51.4 all-reduce.20
  415.6 78.0 all-reduce.22
  497.3 79.8 reduce-scatter.29
  580.6 60.5 reduce-scatter.23
  644.9 60.9 reduce-scatter.27
  709.3 60.9 reduce-scatter.17
  774.0 66.8 reduce-scatter.31
  844.8 66.8 reduce-scatter.25
  915.3 60.8 reduce-scatter.21
  979.6 60.9 reduce-scatter.19
  1043.5 84.6 all-reduce.24
  1130.6 31.5 reduce-scatter.15
where the time goes:
time: 1200 us; the launch traced here: 1190 us
  waiting for transfers between devices  746 us (62%)
  matrix products  221 us (18%)
  other arithmetic  102 us (8%)
  local copies, waits for them, and re-layouts  54.7 us (5%)
  blocking collectives  37.1 us (3%)
  between operations  16.8 us (1%)
  starting transfers between devices  14.2 us (1%)
    psum x5, waiting for transfers between devices, model_sum(): return lax.psum(partial_sum.astype(jnp.bfloat16), 'mp').astype(jnp.float32)  274 us
    unnamed x18, waiting for transfers between devices  133 us
    reduce_scatter x1, waiting for transfers between devices, body(): lax.psum_scatter(expand_grad.astype(jnp.bfloat16), 'seq', scatter_dimensi...  68.8 us
    reduce_scatter x1, waiting for transfers between devices, body(): lax.psum_scatter(key_grad_weight.astype(jnp.bfloat16), 'seq', scatter_dim...  62.8 us
    reduce_scatter x1, waiting for transfers between devices, body(): lax.psum_scatter(value_grad_weight.astype(jnp.bfloat16), 'seq', scatter_d...  62.7 us
    reduce_scatter x1, waiting for transfers between devices, body(): lax.psum_scatter(query_grad_weight.astype(jnp.bfloat16), 'seq', scatter_d...  62.7 us
    ppermute x4, waiting for transfers between devices, from_behind(): lax.ppermute(value, axis, [(source, source + steps) for source in range(l...  61.4 us
    unnamed x1, blocking collectives  37.1 us
  transfers between devices with their start and end apart: 19, of which 16 were waited for; matrix products, arithmetic and copies ran while one was open for 19% of the time, Pallas kernels for 0%

commit v1 on v0

v1 whole, which is shorter than its diff:
```python
import functools

import jax
import jax.numpy as jnp
from jax import lax
from jax.experimental import pallas as pl
from jax.experimental.pallas import tpu as pltpu
from jax.sharding import PartitionSpec as P

HD = 64
ITEM_LEN = 1024
EPS = 1e-06
NEGATIVE = -1e30
BF = jnp.bfloat16
F32 = jnp.float32
BLOCK = 256
SCALE = HD**-0.5
MIB = 1 << 20


def dot(left, right, ld, rd):
    return lax.dot_general(left, right, (((ld,), (rd,)), ((), ())), preferred_element_type=F32)


def nn(left, right):
    return dot(left, right, 1, 0)


def nt(left, right):
    return dot(left, right, 1, 1)


def tn(left, right):
    return dot(left, right, 0, 0)


def partner(value, step):
    count = lax.axis_size("mp")
    return lax.ppermute(value, "mp", [(rank, rank ^ step) for rank in range(count)])


def from_behind(value, axis, steps):
    count = lax.axis_size(axis)
    leading, last = (max(0, -steps), min(count, count - steps))
    return lax.ppermute(value, axis, [(source, source + steps) for source in range(leading, last)])


def whole(array):
    rank = len(array.shape)
    return pl.BlockSpec(array.shape, lambda *_: (0,) * rank)


def shaped(shape, dtype):
    return jax.ShapeDtypeStruct(shape, dtype)


def run(kernel, ids, args, outs, grid=(1,), in_specs=None, out_specs=None, scratch=(), flops=0, exps=0, vmem=40):
    in_specs = in_specs or [None] * len(args)
    out_specs = out_specs or [None] * len(outs)
    in_specs = [whole(a) if s is None else s for a, s in zip(args, in_specs)]
    out_specs = [whole(a) if s is None else s for a, s in zip(outs, out_specs)]
    moved = sum(a.size * a.dtype.itemsize for a in list(args) + list(outs))
    return pl.pallas_call(
        kernel,
        out_shape=outs,
        grid_spec=pltpu.PrefetchScalarGridSpec(
            num_scalar_prefetch=1,
            grid=grid,
            in_specs=in_specs,
            out_specs=out_specs,
            scratch_shapes=list(scratch),
        ),
        compiler_params=pltpu.CompilerParams(vmem_limit_bytes=vmem * MIB),
        cost_estimate=pl.CostEstimate(flops=flops, transcendentals=exps, bytes_accessed=moved),
    )(ids, *args)


def ln_rows(values):
    centred = values - jnp.mean(values, axis=-1, keepdims=True)
    spread = jnp.mean(centred * centred, axis=-1, keepdims=True)
    inverse = lax.rsqrt(spread + EPS)
    return centred * inverse, inverse


def ln_back(grad, gain, normed, inverse):
    scaled = grad * gain
    first = jnp.mean(scaled, axis=-1, keepdims=True)
    second = jnp.mean(scaled * normed, axis=-1, keepdims=True)
    return inverse * (scaled - first - normed * second)


def head_mask(head, heads):
    lanes = lax.broadcasted_iota(jnp.int32, (1, heads * HD), 1)
    return jnp.where(lanes // HD == head, 1.0, 0.0).astype(BF)


def by_head(rows, heads):
    return [rows * head_mask(head, heads) for head in range(heads)]


def entry_kernel(ids, tok, gain, bias, wq, wk, wv, hid, q, kv, tail):
    width = wq.shape[1]
    normed, _ = ln_rows(tok[...].astype(F32))
    hidden = (normed * gain[...] + bias[...]).astype(BF)
    hid[...] = hidden
    kv[:, :width] = nn(hidden, wk[...]).astype(BF)
    kv[:, width:] = nn(hidden, wv[...]).astype(BF)
    q[...] = (nn(hidden, wq[...]).astype(BF) * SCALE).astype(BF)

    @pl.when(pl.program_id(0) == pl.num_programs(0) - 1)
    def _():
        tail[...] = kv[...]


def prompt_kernel(ids, text, pk, pv, out):
    width = pk.shape[1]
    out[:, :width] = nn(text[0], pk[...]).astype(BF)
    out[:, width:] = nn(text[0], pv[...]).astype(BF)


def window_bias(key_base, query_base, begin):
    shape = (BLOCK, BLOCK)
    key = key_base + lax.broadcasted_iota(jnp.int32, shape, 0)
    query = query_base + lax.broadcasted_iota(jnp.int32, shape, 1)
    return jnp.where((key <= query) & (key >= begin), 0.0, NEGATIVE).astype(F32)


def attend_block(keys, values_t, queries, bias, top, total, acc):
    for head, query in enumerate(queries):
        scores = nt(keys, query) + bias
        before = top[head : head + 1, :]
        after = jnp.maximum(before, jnp.max(scores, axis=0, keepdims=True))
        fade = jnp.exp(before - after)
        unnorm = jnp.exp(scores - after)
        total[head : head + 1, :] = total[head : head + 1, :] * fade + jnp.sum(unnorm, axis=0, keepdims=True)
        acc[head] = acc[head] * fade + nn(values_t[head * HD : (head + 1) * HD, :], unnorm.astype(BF))
        top[head : head + 1, :] = after


def attend_local_kernel(ids, q, kv, begin, acc_o, top_o, total_o, vt, acc, top, total):
    step = pl.program_id(0)
    width = q.shape[1]
    heads = width // HD
    blocks = kv.shape[0] // BLOCK

    @pl.when(step == 0)
    def _():
        for b in range(blocks):
            vt[b] = kv[b * BLOCK : (b + 1) * BLOCK, width:].T

    queries = by_head(q[...], heads)
    top[...] = jnp.full_like(top, NEGATIVE)
    total[...] = jnp.zeros_like(total)
    acc[...] = jnp.zeros_like(acc)
    low = lax.shift_right_logical(jnp.maximum(ids[8 + step], 0), 8)

    @pl.loop(low, step + 1)
    def _(b):
        row = pl.multiple_of(b * BLOCK, BLOCK)
        bias = window_bias(row, step * BLOCK, begin[...])
        attend_block(kv[pl.ds(row, BLOCK), :width], vt[b], queries, bias, top, total, acc)

    acc_o[0] = acc[...]
    top_o[0] = top[...]
    total_o[0] = total[...]


def attend_remote_kernel(ids, q, kv, tail, begin, acc_i, top_i, total_i, out, low_out, lse, vt, acc, top, total):
    step = pl.program_id(0)
    width = q.shape[1]
    heads = width // HD
    blocks = kv.shape[0] // BLOCK

    @pl.when(step == 0)
    def _():
        vt[0] = tail[:, width:].T
        for b in range(blocks):
            vt[b + 1] = kv[b * BLOCK : (b + 1) * BLOCK, width:].T

    queries = by_head(q[...], heads)
    acc[...] = acc_i[0]
    top[...] = top_i[0]
    total[...] = total_i[0]
    span = (blocks + 1) * BLOCK
    low = lax.shift_right_logical(jnp.maximum(ids[8 + step] + span, 0), 8)

    def bias_of(b):
        return window_bias(b * BLOCK - span, step * BLOCK, begin[...])

    @pl.when(low == 0)
    def _():
        attend_block(tail[:, :width], vt[0], queries, bias_of(0), top, total, acc)

    @pl.loop(jnp.maximum(low, 1), blocks + 1)
    def _(b):
        row = pl.multiple_of((b - 1) * BLOCK, BLOCK)
        attend_block(kv[pl.ds(row, BLOCK), :width], vt[b], queries, bias_of(b), top, total, acc)

    lse[0] = top[...] + jnp.log(total[...])
    stacked = jnp.concatenate([acc[h] * (1.0 / total[h : h + 1, :]) for h in range(heads)], axis=0)
    rows = stacked.T
    out[0] = rows
    low_out[0] = rows.astype(BF)


def back_block(keys, values, keys_t, queries, grads, bias, lse, delta, dq):
    key_sum = value_sum = None
    for head, (query, grad) in enumerate(zip(queries, grads)):
        row = slice(head, head + 1)
        probs = jnp.exp(nt(keys, query) + bias - lse[row, :])
        score_grad = (probs * (nt(values, grad) - delta[row, :])).astype(BF)
        low_probs = probs.astype(BF)
        key_term = nn(score_grad, query)
        value_term = nn(low_probs, grad)
        key_sum = key_term if key_sum is None else key_sum + key_term
        value_sum = value_term if value_sum is None else value_sum + value_term
        dq[head] += nn(keys_t[head * HD : (head + 1) * HD, :], score_grad)
    return key_sum, value_sum


def back_remote_kernel(ids, q, kv, tail, begin, grad, out, lse, dkv_o, dtail_o, dq_o, delta_o, kt, dkv, dq):
    step = pl.program_id(0)
    width = q.shape[1]
    heads = width // HD
    blocks = kv.shape[0] // BLOCK

    @pl.when(step == 0)
    def _():
        dkv[...] = jnp.zeros_like(dkv)
        kt[0] = tail[:, :width].T
        for b in range(blocks):
            kt[b + 1] = kv[b * BLOCK : (b + 1) * BLOCK, :width].T

    products = (grad[0].astype(F32) * out[0]).T
    for head in range(heads):
        delta_o[0, head : head + 1, :] = jnp.sum(products[head * HD : (head + 1) * HD, :], axis=0, keepdims=True)
    dq[...] = jnp.zeros_like(dq)
    span = (blocks + 1) * BLOCK
    low = lax.shift_right_logical(jnp.maximum(ids[8 + step] + span, 0), 8)

    @pl.when(low <= blocks)
    def _():
        queries = by_head(q[...], heads)
        grads = by_head(grad[0], heads)

        def one(b, pair):
            bias = window_bias(b * BLOCK - span, step * BLOCK, begin[...])
            key_sum, value_sum = back_block(
                pair[:, :width], pair[:, width:], kt[b], queries, grads, bias, lse.at[0], delta_o.at[0], dq
            )
            dkv[b, :, :width] += key_sum
            dkv[b, :, width:] += value_sum

        @pl.when(low == 0)
        def _():
            one(0, tail[...])

        @pl.loop(jnp.maximum(low, 1), blocks + 1)
        def _(b):
            row = pl.multiple_of((b - 1) * BLOCK, BLOCK)
            one(b, kv[pl.ds(row, BLOCK), :])

    dq_o[0] = dq[...]

    @pl.when(step == pl.num_programs(0) - 1)
    def _():
        dtail_o[...] = dkv[0].astype(BF)
        for b in range(blocks):
            dkv_o[b * BLOCK : (b + 1) * BLOCK, :] = dkv[b + 1].astype(BF)


def back_local_kernel(ids, q, kv, begin, grad, lse, delta, dq_i, dkv_o, dq_o, kt, dkv, dq):
    step = pl.program_id(0)
    width = q.shape[1]
    heads = width // HD
    blocks = kv.shape[0] // BLOCK

    @pl.when(step == 0)
    def _():
        dkv[...] = jnp.zeros_like(dkv)
        for b in range(blocks):
            kt[b] = kv[b * BLOCK : (b + 1) * BLOCK, :width].T

    dq[...] = dq_i[0]
    queries = by_head(q[...], heads)
    grads = by_head(grad[0], heads)
    low = lax.shift_right_logical(jnp.maximum(ids[8 + step], 0), 8)

    @pl.loop(low, step + 1)
    def _(b):
        row = pl.multiple_of(b * BLOCK, BLOCK)
        pair = kv[pl.ds(row, BLOCK), :]
        bias = window_bias(row, step * BLOCK, begin[...])
        key_sum, value_sum = back_block(
            pair[:, :width], pair[:, width:], kt[b], queries, grads, bias, lse.at[0], delta.at[0], dq
        )
        dkv[b, :, :width] += key_sum
        dkv[b, :, width:] += value_sum

    stacked = jnp.concatenate([dq[h] for h in range(heads)], axis=0)
    dq_o[...] = (stacked.T * SCALE).astype(BF)

    @pl.when(step == pl.num_programs(0) - 1)
    def _():
        for b in range(blocks):
            dkv_o[b * BLOCK : (b + 1) * BLOCK, :] = dkv[b]


def cross_bias(ids, prompt_rows, rows):
    shape = (2 * prompt_rows, rows)
    key = lax.broadcasted_iota(jnp.int32, shape, 0)
    query = lax.broadcasted_iota(jnp.int32, shape, 1)
    key_slot = lax.shift_right_logical(key, prompt_rows.bit_length() - 1)
    query_slot = jnp.where(query >= ids[4], 1, 0)
    limit = jnp.where(key_slot == 1, prompt_rows + ids[6], ids[5])
    return jnp.where((key_slot == query_slot) & (key < limit), 0.0, NEGATIVE).astype(F32)


def cross_kernel(ids, tok, low, *refs):
    packs, pairs = refs[:4], refs[4:8]
    gain2, bias2, gain3, bias3 = refs[8:12]
    after_self_o, two_o, q_o, stat_o, out_o, after_o, three_o = refs[12:]
    rows = tok.shape[0]
    width = packs[0].shape[0] // 3
    heads = width // HD
    rank = ids[1]
    prompt_rows = pairs[0].shape[0] // 3
    after = tok[...].astype(F32)
    for d in range(4):
        after = after + nn(low[rank ^ d], packs[d][:width, :])
    after_self_o[...] = after
    normed, _ = ln_rows(after)
    hidden = (normed * gain2[...] + bias2[...]).astype(BF)
    two_o[...] = hidden
    bias = cross_bias(ids, prompt_rows, rows)
    first = pl.multiple_of(ids[3], prompt_rows)
    for d in range(4):
        columns = slice(d * width, (d + 1) * width)
        query_rows = (nt(hidden, packs[d][width : 2 * width, :]).astype(BF) * SCALE).astype(BF)
        q_o[:, columns] = query_rows
        keys = pairs[d][pl.ds(first, 2 * prompt_rows), :width]
        values_t = pairs[d][pl.ds(first, 2 * prompt_rows), width:].T
        parts = []
        for head, query in enumerate(by_head(query_rows, heads)):
            scores = nt(keys, query) + bias
            top = jnp.max(scores, axis=0, keepdims=True)
            unnorm = jnp.exp(scores - top)
            total = jnp.sum(unnorm, axis=0, keepdims=True)
            stat_o[d * heads + head : d * heads + head + 1, :] = top + jnp.log(total)
            part = nn(values_t[head * HD : (head + 1) * HD, :], unnorm.astype(BF))
            parts.append(part * (1.0 / total))
        out_o[:, columns] = jnp.concatenate(parts, axis=0).T.astype(BF)
    after = after_self_o[...]
    for d in range(4):
        after = after + nn(out_o[:, d * width : (d + 1) * width], packs[d][2 * width :, :])
    after_o[...] = after
    normed, _ = ln_rows(after)
    three_o[...] = (normed * gain3[...] + bias3[...]).astype(BF)


def cross_back_kernel(ids, kept, sent, crossed, og, after, after_self, q, stat, *refs):
    packs, pairs = refs[:4], refs[4:8]
    gain2, gain3 = refs[8:10]
    cog_o, cqg_o, slg_o, resid_o, shg_o, keep_o, send_o, norms_o = refs[10:]
    rows, model = after.shape
    width = packs[0].shape[0] // 3
    heads = width // HD
    rank = ids[1]
    prompt_rows = pairs[0].shape[0] // 3
    grad = kept[...].astype(F32) + sent[...].astype(F32) + crossed[...].astype(F32)
    normed, inverse = ln_rows(after[...])
    norms_o[0:1, :] = jnp.sum(grad * normed, axis=0, keepdims=True)
    norms_o[1:2, :] = jnp.sum(grad, axis=0, keepdims=True)
    resid = og[...].astype(F32) + ln_back(grad, gain3[...], normed, inverse)
    low_resid = resid.astype(BF)
    cog_o[...] = low_resid
    bias = cross_bias(ids, prompt_rows, rows)
    first = pl.multiple_of(ids[3], prompt_rows)
    keep_o[...] = jnp.zeros_like(keep_o)
    send_o[...] = jnp.zeros_like(send_o)
    for d in range(4):
        columns = slice(d * width, (d + 1) * width)
        head_grad = nt(low_resid, packs[d][2 * width :, :]).astype(BF)
        keys = pairs[d][pl.ds(first, 2 * prompt_rows), :width]
        values = pairs[d][pl.ds(first, 2 * prompt_rows), width:]
        keys_t = keys.T
        key_sum = value_sum = None
        parts = []
        for head, (query, out_grad) in enumerate(zip(by_head(q[:, columns], heads), by_head(head_grad, heads))):
            row = slice(d * heads + head, d * heads + head + 1)
            probs = jnp.exp(nt(keys, query) + bias - stat[row, :])
            prob_grad = nt(values, out_grad)
            delta = jnp.sum(probs * prob_grad, axis=0, keepdims=True)
            score_grad = (probs * (prob_grad - delta)).astype(BF)
            key_term = nn(score_grad, query)
            value_term = nn(probs.astype(BF), out_grad)
            key_sum = key_term if key_sum is None else key_sum + key_term
            value_sum = value_term if value_sum is None else value_sum + value_term
            parts.append(nn(keys_t[head * HD : (head + 1) * HD, :], score_grad))
        cqg_o[:, columns] = (jnp.concatenate(parts, axis=0).T * SCALE).astype(BF)
        target = keep_o if d % 2 == 0 else send_o
        target[d // 2, pl.ds(first, 2 * prompt_rows), :width] = key_sum.astype(BF)
        target[d // 2, pl.ds(first, 2 * prompt_rows), width:] = value_sum.astype(BF)
    two_grad = None
    for d in range(4):
        term = nn(cqg_o[:, d * width : (d + 1) * width], packs[d][width : 2 * width, :])
        two_grad = term if two_grad is None else two_grad + term
    normed, inverse = ln_rows(after_self[...])
    norms_o[2:3, :] = jnp.sum(two_grad * normed, axis=0, keepdims=True)
    norms_o[3:4, :] = jnp.sum(two_grad, axis=0, keepdims=True)
    resid = resid + ln_back(two_grad, gain2[...], normed, inverse)
    resid_o[...] = resid
    low_resid = resid.astype(BF)
    slg_o[...] = low_resid
    for d in range(4):
        shg_o[rank ^ d] = nt(low_resid, packs[d][:width, :]).astype(BF)


def feed_kernel(ids, h_a, h_b, dh_a, dh_b, expand, shrink, *refs):
    outs, accs = refs[:8], refs[8:]
    last = pl.num_programs(0) - 1
    c = 0.7978845608028654
    for side, (h, dh) in enumerate(((h_a, dh_a), (h_b, dh_b))):
        low_o, pre_o, out_o, three_o = outs[4 * side : 4 * side + 4]
        out_s, three_s = accs[2 * side : 2 * side + 2]
        v = nn(h[...], expand[...])
        square = v * v
        t = jnp.tanh(c * v * (1.0 + 0.044715 * square))
        half = 0.5 * (1.0 + t)
        low = (v * half).astype(BF)
        slope = half + 0.5 * v * (1.0 - t * t) * (c * (1.0 + 3 * 0.044715 * square))
        pre = (dh[...].astype(F32) * slope).astype(BF)
        low_o[...] = low
        pre_o[...] = pre
        out_part = nn(low, shrink[...])
        three_part = nt(pre, expand[...])

        @pl.when(pl.program_id(0) == 0)
        def _():
            out_s[...] = out_part
            three_s[...] = three_part

        @pl.when(pl.program_id(0) > 0)
        def _():
            out_s[...] += out_part
            three_s[...] += three_part

        @pl.when(pl.program_id(0) == last)
        def _():
            out_o[...] = out_s[...].astype(BF)
            three_o[...] = three_s[...].astype(BF)


def feed(ids, base, h_a, h_b, dh, expand, shrink):
    rows, model = h_a.shape
    hidden = expand.shape[1]
    chunk = 256
    row_block = lambda d: pl.BlockSpec((rows, chunk), lambda j, s: (s[1] ^ d, j))
    column = pl.BlockSpec((rows, chunk), lambda j, s: (0, j))
    full = pl.BlockSpec((rows, model), lambda j, s: (0, 0))
    return run(
        feed_kernel,
        ids,
        (h_a, h_b, dh, dh, expand, shrink),
        [shaped((rows, hidden), BF), shaped((rows, hidden), BF), shaped((rows, model), BF), shaped((rows, model), BF)] * 2,
        grid=(hidden // chunk,),
        in_specs=[
            full,
            full,
            row_block(base),
            row_block(base + 1),
            pl.BlockSpec((model, chunk), lambda j, s: (0, j)),
            pl.BlockSpec((chunk, model), lambda j, s: (j, 0)),
        ],
        out_specs=[column, column, full, full] * 2,
        scratch=[pltpu.VMEM((rows, model), F32)] * 4,
        flops=2 * 2 * 3 * rows * model * hidden,
        exps=2 * rows * hidden,
    )


def feed_weights_kernel(ids, *refs):
    threes, pres, lows = refs[:4], refs[4:8], refs[8:12]
    og, out, turned = refs[12:]
    step = pl.program_id(0)
    half = pl.num_programs(0) // 2
    rank = ids[1]
    rows = threes[0].shape[0]

    @pl.when(step == 0)
    def _():
        for d in range(4):
            turned[:, d * rows : (d + 1) * rows] = threes[d][...].T

    @pl.when(step == half)
    def _():
        for d in range(4):
            turned[:, d * rows : (d + 1) * rows] = og[pl.ds(pl.multiple_of((rank ^ d) * rows, rows), rows), :].T

    @pl.when(step < half)
    def _():
        out[...] = nn(turned[...], jnp.concatenate([p[...] for p in pres], axis=0)).astype(BF)

    @pl.when(step >= half)
    def _():
        out[...] = nn(turned[...], jnp.concatenate([p[...] for p in lows], axis=0)).astype(BF)


def feed_weights(ids, threes, pres, lows, og):
    rows, model = threes[0].shape
    hidden = pres[0].shape[1]
    chunk = 256
    half = hidden // chunk
    front = pl.BlockSpec((rows, chunk), lambda j, s: (0, jnp.minimum(j, half - 1)))
    back = pl.BlockSpec((rows, chunk), lambda j, s: (0, jnp.maximum(j - half, 0)))
    return run(
        feed_weights_kernel,
        ids,
        (*threes, *pres, *lows, og),
        [shaped((model, 2 * hidden), BF)],
        grid=(2 * half,),
        in_specs=[None] * 4 + [front] * 4 + [back] * 4 + [None],
        out_specs=[pl.BlockSpec((model, chunk), lambda j, s: (0, j))],
        scratch=[pltpu.VMEM((model, 4 * rows), BF)],
        flops=2 * 2 * 4 * rows * model * hidden,
    )[0]


def head_weights_kernel(ids, two, cqg, cog, crossed, slg, low, keep, send, turned):
    step = pl.program_id(0)
    rank = ids[1]
    width = low.shape[2]

    @pl.when(step == 0)
    def _():
        turned[0] = two[...].T
        turned[1] = cog[...].T
        turned[2] = slg[...].T

    for side, out in enumerate((keep, send)):
        columns = pl.ds(pl.multiple_of((2 * step + side) * width, width), width)
        out[0, :, :width] = nn(turned[0], cqg[:, columns]).astype(BF)
        out[0, :, width : 2 * width] = nn(turned[1], crossed[:, columns]).astype(BF)
        out[0, :, 2 * width :] = nn(turned[2], low[rank ^ (2 * step + side)]).astype(BF)


def key_sum_kernel(ids, dkv, near, far, hid, dq, wq, wk, wv, gain, bias, kvg_o, keep, send, norms):
    rows, width2 = dkv.shape
    width = width2 // 2
    quarter = rows // 4
    rank = ids[1]
    kvg_o[: rows - BLOCK, :] = (dkv[: rows - BLOCK, :] + near[: rows - BLOCK, :].astype(F32)).astype(BF)
    kvg_o[rows - BLOCK :, :] = (
        dkv[rows - BLOCK :, :] + near[rows - BLOCK :, :].astype(F32) + far[...].astype(F32)
    ).astype(BF)
    product = total = None
    for d in (1, 3, 2, 0):
        own = pl.ds(pl.multiple_of((rank ^ d) * quarter, quarter), quarter)
        part = (
            nt(dq[own, :], wq[...]) + nt(kvg_o[own, :width], wk[...]) + nt(kvg_o[own, width:], wv[...])
        )
        hidden = hid[own, :].astype(F32)
        term = jnp.sum(part * hidden, axis=0, keepdims=True)
        plain = jnp.sum(part, axis=0, keepdims=True)
        product = term if product is None else product + term
        total = plain if total is None else total + plain
        target = keep if d % 2 == 0 else send
        target[d // 2] = part.astype(BF)
    norms[0:1, :] = (product - bias[...] * total) / gain[...]
    norms[1:2, :] = total


def entry_back_kernel(ids, keep, sent, crossed, tok, gain, resid, out):
    grad = keep[0].astype(F32) + sent[0].astype(F32) + crossed[...].astype(F32)
    normed, inverse = ln_rows(tok[...].astype(F32))
    out[...] = (resid[...] + ln_back(grad, gain[...], normed, inverse)).astype(BF)


def assemble_kernel(ids, *refs):
    out = refs[4]
    for d in range(4):

        @pl.when(pl.program_id(0) == ids[1] ^ d)
        def _():
            out[...] = refs[d][...].astype(out.dtype)


def assemble(ids, pieces, dtype):
    rows, model = pieces[0].shape
    return run(
        assemble_kernel,
        ids,
        pieces,
        [shaped((4 * rows, model), dtype)],
        grid=(4,),
        out_specs=[pl.BlockSpec((rows, model), lambda i, s: (i, 0))],
    )[0]


def gather(own):
    across = partner(own, 2)
    near = partner(own, 1)
    return own, near, across, partner(across, 1)


def sum_rows(blocks):
    return jnp.sum(blocks.astype(F32), axis=0)


def body(
    tokens,
    text_states,
    item_lengths,
    prompt_lengths,
    entry_gain,
    entry_bias,
    cross_gain,
    cross_bias_,
    mixer_gain,
    mixer_bias,
    query_weight,
    key_weight,
    value_weight,
    merge_weight,
    prompt_query,
    prompt_key,
    prompt_value,
    prompt_merge,
    expand_weight,
    shrink_weight,
    output_grad,
):
    rows, model = tokens.shape
    shards = lax.axis_size("seq")
    ranks = lax.axis_size("mp")
    width = query_weight.shape[1]
    heads = width // HD
    items, prompt_rows = text_states.shape[:2]
    quarter = rows // ranks
    steps = rows // BLOCK
    hidden_units = expand_weight.shape[1]
    assert ranks == 4 and quarter == BLOCK

    rank = lax.axis_index("mp")
    offset = lax.axis_index("seq") * rows
    ends = jnp.cumsum(item_lengths)
    starts = ends - item_lengths
    positions = jnp.arange(rows, dtype=jnp.int32) + offset

    def begin_of(where):
        return jnp.max(jnp.where(starts[None, :] <= where[:, None], starts[None, :], 0), axis=1)

    begin = (begin_of(positions) - offset)[None, :]
    lows = begin_of(offset + BLOCK * jnp.arange(steps, dtype=jnp.int32)) - offset
    base = jnp.minimum(jnp.sum((ends <= offset).astype(jnp.int32)), items - 3)
    own_first = offset + rank * quarter
    own_base = jnp.minimum(jnp.sum((ends <= own_first).astype(jnp.int32)), items - 2)
    numbers = jnp.arange(items, dtype=jnp.int32)

    def at(values, index):
        return jnp.sum(jnp.where(numbers == index, values, 0))

    ids = jnp.stack(
        [
            lax.axis_index("seq"),
            rank,
            base,
            (own_base - base) * prompt_rows,
            at(ends, own_base) - own_first,
            at(prompt_lengths, own_base),
            at(prompt_lengths, own_base + 1),
            jnp.zeros_like(rank),
        ]
    )
    ids = jnp.concatenate([ids, lows]).astype(jnp.int32)

    row = lambda vector: vector.reshape(1, -1)
    own_rows = lambda columns: pl.BlockSpec((quarter, columns), lambda *g: (g[-1][1], 0))

    block_rows = lambda columns: pl.BlockSpec((BLOCK, columns), lambda i, s: (i, 0))
    hidden_one, q, kv, kv_tail = run(
        entry_kernel,
        ids,
        (tokens, row(entry_gain), row(entry_bias), query_weight, key_weight, value_weight),
        [shaped((rows, model), BF), shaped((rows, width), BF), shaped((rows, 2 * width), BF), shaped((BLOCK, 2 * width), BF)],
        grid=(steps,),
        in_specs=[block_rows(model)] + [None] * 5,
        out_specs=[block_rows(model), block_rows(width), block_rows(2 * width), None],
        flops=6 * rows * model * width,
    )
    kv_near = from_behind(kv, "seq", 1)
    kv_far = from_behind(kv_tail, "seq", 2)

    pack = jnp.concatenate([merge_weight, prompt_query.T, prompt_merge], axis=0)
    pair = run(
        prompt_kernel,
        ids,
        (text_states, prompt_key, prompt_value),
        [shaped((3 * prompt_rows, 2 * width), BF)],
        grid=(3,),
        in_specs=[pl.BlockSpec((1, prompt_rows, model), lambda i, s: (s[2] + i, 0, 0)), None, None],
        out_specs=[pl.BlockSpec((prompt_rows, 2 * width), lambda i, s: (i, 0))],
        flops=4 * 3 * prompt_rows * model * width,
    )[0]
    packs = gather(pack)
    pairs = gather(pair)
    hidden_grad = nt(output_grad, shrink_weight).astype(BF)

    state = [shaped((steps, heads, HD, BLOCK), F32), shaped((steps, heads, BLOCK), F32), shaped((steps, heads, BLOCK), F32)]
    state_specs = [
        pl.BlockSpec((1, heads, HD, BLOCK), lambda i, s: (i, 0, 0, 0)),
        pl.BlockSpec((1, heads, BLOCK), lambda i, s: (i, 0, 0)),
        pl.BlockSpec((1, heads, BLOCK), lambda i, s: (i, 0, 0)),
    ]
    state_scratch = [pltpu.VMEM((heads, HD, BLOCK), F32), pltpu.VMEM((heads, BLOCK), F32), pltpu.VMEM((heads, BLOCK), F32)]
    q_spec = block_rows(width)
    begin_spec = pl.BlockSpec((1, BLOCK), lambda i, s: (0, i))
    piece_spec = pl.BlockSpec((1, BLOCK, width), lambda i, s: (i, 0, 0))
    turned = lambda blocks: pltpu.VMEM((blocks, width, BLOCK), BF)
    pair_flops = 2 * heads * BLOCK * BLOCK * width
    acc, top, total = run(
        attend_local_kernel,
        ids,
        (q, kv, begin),
        state,
        grid=(steps,),
        in_specs=[q_spec, None, begin_spec],
        out_specs=state_specs,
        scratch=[turned(steps)] + state_scratch,
        flops=2 * pair_flops * 10,
        exps=heads * BLOCK * BLOCK * 10,
    )
    self_out, self_low, lse = run(
        attend_remote_kernel,
        ids,
        (q, kv_near, kv_far, begin, acc, top, total),
        [shaped((steps, BLOCK, width), F32), shaped((steps, BLOCK, width), BF), shaped((steps, heads, BLOCK), F32)],
        grid=(steps,),
        in_specs=[q_spec, None, None, begin_spec] + state_specs,
        out_specs=[piece_spec, piece_spec, state_specs[1]],
        scratch=[turned(steps + 1)] + state_scratch,
        flops=2 * pair_flops * 10,
        exps=heads * BLOCK * BLOCK * 10,
    )
    low_rows = lax.all_to_all(self_low, "mp", 0, 0)

    wide = lambda dtype: shaped((quarter, model), dtype)
    stat_shape = shaped((ranks * heads, quarter), F32)
    norms = (row(cross_gain), row(cross_bias_), row(mixer_gain), row(mixer_bias))
    after_self, hidden_two, cross_q, stat, cross_out, after_cross, hidden_three = run(
        cross_kernel,
        ids,
        (tokens, low_rows, *packs, *pairs, *norms),
        [wide(F32), wide(BF), wide(BF), stat_shape, wide(BF), wide(F32), wide(BF)],
        in_specs=[own_rows(model)] + [None] * 13,
        flops=6 * quarter * model * model + 4 * ranks * pair_flops,
        exps=ranks * heads * BLOCK * BLOCK,
    )

    threes = gather(hidden_three)
    low0, pre0, out0, part0, low1, pre1, out1, part1 = feed(ids, 0, threes[0], threes[1], hidden_grad, expand_weight, shrink_weight)
    low2, pre2, out2, part2, low3, pre3, out3, part3 = feed(ids, 2, threes[2], threes[3], hidden_grad, expand_weight, shrink_weight)
    sent1 = partner(part1, 1)
    across = partner((part2.astype(F32) + partner(part3, 1).astype(F32)).astype(BF), 2)

    feed_grads = feed_weights(ids, threes, (pre0, pre1, pre2, pre3), (low0, low1, low2, low3), output_grad)
    feed_sum = lax.psum_scatter(feed_grads, "seq", scatter_dimension=0, tiled=True)

    pair_out = shaped((2, 3 * prompt_rows, 2 * width), BF)
    cog, cqg, slg, resid, shg, pair_keep, pair_send, norm_grads = run(
        cross_back_kernel,
        ids,
        (part0, sent1, across, output_grad, after_cross, after_self, cross_q, stat, *packs, *pairs, norms[0], norms[2]),
        [wide(BF), wide(BF), wide(BF), wide(F32), shaped((ranks, quarter, width), BF), pair_out, pair_out, shaped((4, model), F32)],
        in_specs=[None] * 3 + [own_rows(model)] + [None] * 14,
        flops=6 * quarter * model * model + 10 * ranks * pair_flops,
        exps=ranks * heads * BLOCK * BLOCK,
        vmem=48,
    )
    self_grad = lax.all_to_all(shg, "mp", 0, 0)

    out_across = partner((out2.astype(F32) + partner(out3, 1).astype(F32)).astype(BF), 2)
    out_rows = (
        after_cross + out0.astype(F32) + partner(out1, 1).astype(F32) + out_across.astype(F32)
    ).astype(BF)
    layer_output = assemble(ids, gather(out_rows), BF)

    pieces = shaped((2, model, 3 * width), BF)
    piece_out = pl.BlockSpec((1, model, 3 * width), lambda i, s: (i, 0, 0))
    head_keep, head_send = run(
        head_weights_kernel,
        ids,
        (hidden_two, cqg, cog, cross_out, slg, low_rows),
        [pieces, pieces],
        grid=(2,),
        out_specs=[piece_out, piece_out],
        scratch=[pltpu.VMEM((3, model, quarter), BF)],
        flops=6 * quarter * model * model,
    )

    def over_ranks(keep, send):
        sent = partner(send, 1).astype(F32) + keep.astype(F32)
        return (sent[0] + partner(sent[1].astype(BF), 2).astype(F32)).astype(BF)

    def over_shards(blocks):
        return sum_rows(lax.all_to_all(blocks.reshape(shards, -1, blocks.shape[-1]), "seq", 0, 0))

    head_sum = over_shards(over_ranks(head_keep, head_send))

    pair_sum = over_ranks(pair_keep, pair_send).reshape(3, prompt_rows, 2 * width)
    placed = lax.dynamic_update_slice_in_dim(jnp.zeros((items, prompt_rows, 2 * width), BF), pair_sum, base, 0)
    own_pair = over_shards(placed.reshape(items * prompt_rows, 2 * width)).astype(BF)
    pair_grad = lax.all_gather(own_pair, "seq", axis=0, tiled=True)
    flat_text = text_states.reshape(items * prompt_rows, model)
    prompt_grads = tn(flat_text, pair_grad)
    text_part = nt(own_pair[:, :width], prompt_key) + nt(own_pair[:, width:], prompt_value)
    text_blocks = jnp.swapaxes(text_part.astype(BF).reshape(-1, ranks, width), 0, 1)
    text_own = sum_rows(lax.all_to_all(text_blocks, "mp", 0, 0)).astype(BF)
    text_grad = lax.all_gather(text_own, "seq", axis=0, tiled=True).astype(F32).reshape(items, prompt_rows, width)

    lse_spec = state_specs[1]
    stat4 = shaped((steps, heads, BLOCK), F32)
    dkv_near, dkv_far, dq_part, delta = run(
        back_remote_kernel,
        ids,
        (q, kv_near, kv_far, begin, self_grad, self_out, lse),
        [shaped((rows, 2 * width), BF), shaped((BLOCK, 2 * width), BF), state[0], stat4],
        grid=(steps,),
        in_specs=[q_spec, None, None, begin_spec, piece_spec, piece_spec, lse_spec],
        out_specs=[None, None, state_specs[0], lse_spec],
        scratch=[turned(steps + 1), pltpu.VMEM((steps + 1, BLOCK, 2 * width), F32), state_scratch[0]],
        flops=5 * pair_flops * 10,
        exps=heads * BLOCK * BLOCK * 10,
    )
    from_near = from_behind(dkv_near, "seq", -1)
    from_far = from_behind(dkv_far, "seq", -2)
    dkv, dq = run(
        back_local_kernel,
        ids,
        (q, kv, begin, self_grad, lse, delta, dq_part),
        [shaped((rows, 2 * width), F32), shaped((rows, width), BF)],
        grid=(steps,),
        in_specs=[q_spec, None, begin_spec, piece_spec, lse_spec, lse_spec, state_specs[0]],
        out_specs=[None, q_spec],
        scratch=[turned(steps), pltpu.VMEM((steps, BLOCK, 2 * width), F32), state_scratch[0]],
        flops=5 * pair_flops * 10,
        exps=heads * BLOCK * BLOCK * 10,
    )

    two_quarters = shaped((2, quarter, model), BF)
    kvg, one_keep, one_send, entry_norms = run(
        key_sum_kernel,
        ids,
        (dkv, from_near, from_far, hidden_one, dq, query_weight, key_weight, value_weight, row(entry_gain), row(entry_bias)),
        [shaped((rows, 2 * width), BF), two_quarters, two_quarters, shaped((2, model), F32)],
        flops=6 * rows * model * width,
    )
    one_sent = partner(one_send, 1)
    one_across = partner((one_keep[1].astype(F32) + one_sent[1].astype(F32)).astype(BF), 2)
    grad_rows = run(
        entry_back_kernel,
        ids,
        (one_keep, one_sent, one_across, tokens, row(entry_gain), resid),
        [wide(BF)],
        in_specs=[None] * 3 + [own_rows(model)] + [None] * 2,
    )[0]
    tokens_grad = assemble(ids, gather(grad_rows), F32)

    entry_grads = jnp.concatenate([tn(hidden_one, dq), tn(hidden_one, kvg)], axis=1).astype(BF)
    entry_sum = over_shards(entry_grads)

    norm_rows = jnp.concatenate([entry_norms, norm_grads[2:4], norm_grads[0:2], jnp.zeros((2, model), F32)])
    norm_blocks = jnp.swapaxes(norm_rows.reshape(8, shards, model // shards), 0, 1)
    norm_sum = jnp.sum(lax.all_to_all(norm_blocks, "seq", 0, 0), axis=0)
    norm_sum = norm_sum + partner(norm_sum, 1)
    norm_sum = norm_sum + partner(norm_sum, 2)

    cut = lambda array, index: array[:, index * width : (index + 1) * width]
    feed_sum = feed_sum.astype(F32)
    return (
        layer_output,
        tokens_grad,
        text_grad,
        norm_sum[0],
        norm_sum[1],
        norm_sum[2],
        norm_sum[3],
        norm_sum[4],
        norm_sum[5],
        cut(entry_sum, 0),
        cut(entry_sum, 1),
        cut(entry_sum, 2),
        cut(head_sum, 2).T,
        cut(head_sum, 0),
        prompt_grads[:, :width],
        prompt_grads[:, width:],
        cut(head_sum, 1).T,
        feed_sum[:, :hidden_units],
        feed_sum[:, hidden_units:].T,
    )


def solution(mesh):
    seq, mp, both = P("seq", None), P("mp", None), P(None, "mp")
    return jax.shard_map(
        body,
        mesh=mesh,
        in_specs=(seq,) + (P(),) * 9 + (both,) * 3 + (mp,) + (both,) * 3 + (mp, both, mp, seq),
        out_specs=(
            (seq, seq, P(None, None, "mp"))
            + (P("seq"),) * 6
            + (P("seq", "mp"),) * 3
            + (P("mp", "seq"), P("seq", "mp"), both, both, P("mp", "seq"), P("seq", "mp"), P("mp", "seq"))
        ),
        check_vma=False,
    )
```

time: 1200 us -> 540 us (0.45)
  waiting for transfers between devices: 746 us -> 186 us
  matrix products: 221 us -> 12.4 us
  Pallas kernels: 0 us -> 113 us
  other arithmetic: 102 us -> 25.3 us
  starting transfers between devices: 14.2 us -> 51.2 us
  blocking collectives: 37.1 us -> 66.9 us
    reduce_scatter x6 -> x1, waiting for transfers between devices: 278 us -> 0.01 us  [body(): lax.psum_scatter(feed_grads, 'seq', scatter_dimension=0, tiled=True)]
    psum x6 -> x0, waiting for transfers between devices: 274 us -> none  [the longest x5 274 us: model_sum(): return lax.psum(partial_sum.astype(jnp.bfloat16), 'mp').astype(jnp.float32)]
    dot_general x41 -> x6, matrix products: 215 us -> 12.4 us  [dot(): lax.dot_general(left, right, (((ld,), (rd,)), ((), ())), preferred_elemen...]
    unnamed x18 -> x2, waiting for transfers between devices: 133 us -> 0.03 us
    ppermute x0 -> x29, waiting for transfers between devices: none -> 126 us  [partner(): lax.ppermute(value, 'mp', [(rank, rank ^ step) for rank in range(count)])]
    pallas_call x0 -> x16, Pallas kernels: none -> 113 us  [run(): pl.pallas_call(kernel, out_shape=outs, grid_spec=pltpu.PrefetchScalarGrid...]
    reduce_sum x18 -> x7, other arithmetic: 63 us -> 6.73 us  [the longest x4 5.41 us: sum_rows(): return jnp.sum(blocks.astype(F32), axis=0)]
    unnamed x1 -> x0, blocking collectives: 37.1 us -> none
  transfers between devices with their start and end apart: 19 -> 41, of which waited for: 16 -> 14; matrix products, arithmetic and copies ran while one was open for 19% -> 7% of each run, Pallas kernels for 0% -> 16%
where the time goes in v1:
time: 540 us; the launch traced here: 534 us
  waiting for transfers between devices  186 us (34%)
  Pallas kernels  113 us (21%)
  blocking collectives  66.9 us (12%)
  local copies, waits for them, and re-layouts  61.3 us (11%)
  starting transfers between devices  51.2 us (9%)
  other arithmetic  25.3 us (5%)
  between operations  17.2 us (3%)
  matrix products  12.4 us (2%)
    ppermute x29, waiting for transfers between devices, partner(): lax.ppermute(value, 'mp', [(rank, rank ^ step) for rank in range(count)])  126 us
    pallas_call x16, Pallas kernels, run(): pl.pallas_call(kernel, out_shape=outs, grid_spec=pltpu.PrefetchScalarGrid...  113 us
    unnamed x182, local copies, waits for them, and re-layouts  55.8 us
    ppermute x4, waiting for transfers between devices, from_behind(): lax.ppermute(value, axis, [(source, source + steps) for source in range(l...  47.2 us
    all_to_all x1, blocking collectives, over_shards(): lax.all_to_all(blocks.reshape(shards, -1, blocks.shape[-1]), 'seq', 0, 0)  35.4 us
    all_gather x1, blocking collectives, body(): lax.all_gather(text_own, 'seq', axis=0, tiled=True).astype(F32)  31.4 us
    ppermute x29, starting transfers between devices, partner(): lax.ppermute(value, 'mp', [(rank, rank ^ step) for rank in range(count)])  17.1 us
    dot_general x6, matrix products, dot(): lax.dot_general(left, right, (((ld,), (rd,)), ((), ())), preferred_elemen...  12.4 us
  transfers between devices with their start and end apart: 41, of which 14 were waited for; matrix products, arithmetic and copies ran while one was open for 7% of the time, Pallas kernels for 16%

profile of v1, /device:TPU:0, one launch (start us, length us, event | category | flops | bytes accessed | tf_op | source)
XLA Modules:
  0.0 533.6 jit_solution(16600730931899021615)
XLA Ops:
  21.7 4.0 shard_map.348
  30.6 18.1 %collective-permute-done.3.refs_2_ = bf16[768,1024]{1,0:T(8,128)(2,1)} collective-permute-done((bf16[768,1024]{1,0:T(8,128)(2,1)}, bf16[768,1024]{1,0:T(8,128)(2,1)}, u32[]{:S(2)}, u32[]{:S(2)}) %collective-permute-start.3) | collective-permute-done | bytes 1572896 | tf_op jit(solution)/shard_map/ppermute | solution.py:39
  55.7 11.9 %shard_map.349 = (f32[4,4,64,256]{3,2,1,0:T(8,128)S(1)}, f32[4,4,256]{2,1,0:T(4,128)S(1)}, f32[4,4,256]{2,1,0:T(4,128)S(1)}) custom-call(s32[12]{0:T(128)S(1)} %concatenate.18.ids, bf16[1024,256]{1,0:T(8,128)(2,1)S(1)} %get-tuple-element.72.q, bf16[1024,512]{1,0:T(8,128)(2,1)S(1)} %get-tuple-element.73.kv, s32[1,1024]{1,0:T(1,128)S(1)} %bitcast.93), custom_call_target="tpu_custom_call" | custom-call | flops 2684354560 | bytes 2658304 | tf_op jit(solution)/shard_map/pallas_call | solution.py:63
  75.8 8.5 %all-to-all-done.low = bf16[4,256,256]{2,1,0:T(8,128)(2,1)S(1)} async-done(((bf16[4,256,256]{2,1,0:T(8,128)(2,1)}), bf16[4,256,256]{2,1,0:T(8,128)(2,1)S(1)}, u32[]{:S(2)}, u32[]{:S(2)}) %all-to-all-start) | async-done | bytes 524320 | tf_op jit(solution)/shard_map/all_to_all | solution.py:745
  84.4 10.8 %shard_map.352 = (f32[256,1024]{1,0:T(8,128)S(1)}, bf16[256,1024]{1,0:T(8,128)(2,1)S(1)}, bf16[256,1024]{1,0:T(8,128)(2,1)S(1)}, f32[16,256]{1,0:T(8,128)S(1)}, ...) custom-call(s32[12]{0:T(128)S(1)} %concatenate.18.ids, ...), custom_call_target="tpu_custom_call" | custom-call | flops 3758096384 | bytes 14712832 | tf_op jit(solution)/shard_map/pallas_call | solution.py:63
  96.7 13.1 %collective-permute-done.10.h_a.refs_2_ = bf16[256,1024]{1,0:T(8,128)(2,1)S(1)} collective-permute-done((bf16[256,1024]{1,0:T(8,128)(2,1)S(1)}, bf16[256,1024]{1,0:T(8,128)(2,1)S(1)}, u32[]{:S(2)}, u32[]{:S(2)}) %collective-permute-start.10) | collective-permute-done | bytes 524320 | tf_op jit(solution)/shard_map/ppermute | solution.py:39
  112.8 12.1 %shard_map.354 = (bf16[256,1024]{1,0:T(8,128)(2,1)S(1)}, bf16[256,1024]{1,0:T(8,128)(2,1)S(1)}, bf16[256,1024]{1,0:T(8,128)(2,1)S(1)}, bf16[256,1024]{1,0:T(8,12...) custom-call(s32[12]{0:T(128)S(1)} %concatenate.18.ids, ...), custom_call_target="tpu_custom_call" | custom-call | flops 3221225472 | bytes 13631488 | tf_op jit(solution)/shard_map/pallas_call | solution.py:63
  128.9 11.5 %shard_map.353 = (bf16[256,1024]{1,0:T(8,128)(2,1)S(1)}, bf16[256,1024]{1,0:T(8,128)(2,1)S(1)}, bf16[256,1024]{1,0:T(8,128)(2,1)S(1)}, bf16[256,1024]{1,0:T(8,12...) custom-call(s32[12]{0:T(128)S(1)} %concatenate.18.ids, ...), custom_call_target="tpu_custom_call" | custom-call | flops 3221225472 | bytes 13631488 | tf_op jit(solution)/shard_map/pallas_call | solution.py:63
  144.1 13.0 %collective-permute-done.19.crossed = bf16[256,1024]{1,0:T(8,128)(2,1)S(1)} collective-permute-done((bf16[256,1024]{1,0:T(8,128)(2,1)S(1)}, bf16[256,1024]{1,0:T(8,128)(2,1)S(1)}, u32[]{:S(2)}, u32[]{:S(2)}) %collective-permute-start.19) | collective-permute-done | bytes 524320 | tf_op jit(solution)/shard_map/ppermute | solution.py:39
  157.1 14.6 %shard_map.356 = (bf16[256,1024]{1,0:T(8,128)(2,1)S(1)}, bf16[256,1024]{1,0:T(8,128)(2,1)S(1)}, bf16[256,1024]{1,0:T(8,128)(2,1)S(1)}, f32[256,1024]{1,0:T(8,128...) custom-call(s32[12]{0:T(128)S(1)} %concatenate.18.ids, ...), custom_call_target="tpu_custom_call" | custom-call | flops 6979321856 | bytes 18915328 | tf_op jit(solution)/shard_map/pallas_call | solution.py:63
  180.0 10.6 %collective-permute-done.28 = bf16[384,512]{1,0:T(8,128)(2,1)} collective-permute-done((bf16[384,512]{1,0:T(8,128)(2,1)S(1)}, bf16[384,512]{1,0:T(8,128)(2,1)}, u32[]{:S(2)}, u32[]{:S(2)}) %collective-permute-start.28) | collective-permute-done | bytes 393248 | tf_op jit(solution)/shard_map/ppermute | solution.py:39
  192.1 35.4 %all_to_all.35 = bf16[8,128,512]{2,1,0:T(8,128)(2,1)} all-to-all(bf16[8,128,512]{2,1,0:T(8,128)(2,1)S(1)} %constant_dynamic-update-slice_fusion), channel_id=1, replica_groups=mesh['seq'=8,'mp'=4] {'seq'}, dimensions={0} | all-to-all | bytes 2097152 | tf_op jit(solution)/shard_map/all_to_all | solution.py:806
  247.4 9.3 %shard_map.363 = bf16[1024,2048]{1,0:T(8,128)(2,1)S(1)} custom-call(s32[12]{0:T(128)S(1)} %concatenate.18.ids, bf16[256,1024]{1,0:T(8,128)(2,1)S(1)} %copy-done.40, bf16[256,1024]{1,0:T(8,128)(2,1)S(1)} %copy-done.46, bf16[256,1024]{1,0:T(8,128)(2,1)S(1)} %copy-done.42, bf16[256,1024]{1,0:T(8,128)(2,1)S(1)} %copy-done.44, bf16[256,1024]{1,0:T(8,128)(2,1)S(1)} %copy-done.65, ...), custom_call_target="tpu_custom_call" | custom-call | flops 4294967296 | bytes 12582912 | tf_op jit(solution)/shard_map/pallas_call | solution.py:63
  264.0 4.2 shard_map.362
  278.1 14.5 %shard_map.358 = (f32[1024,512]{1,0:T(8,128)S(1)}, bf16[1024,256]{1,0:T(8,128)(2,1)S(1)}) custom-call(s32[12]{0:T(128)S(1)} %concatenate.18.ids, bf16[1024,256]{1,0:T(8,128)(2,1)S(1)} %copy-done.52, bf16[1024,512]{1,0:T(8,128)(2,1)S(1)} %copy-done.31, s32[1,1024]{1,0:T(1,128)S(1)} %bitcast.96, bf16[4,256,256]{2,1,0:T(8,128)(2,1)S(1)} %all-to-all-done.1.grad, ...), custom_call_target="tpu_custom_call" | custom-call | flops 6710886400 | bytes 5804032 | tf_op jit(solution)/shard_map/pallas_call | solution.py:63
  294.3 47.2 %collective-permute-done.21.far = bf16[256,512]{1,0:T(8,128)(2,1)S(1)} collective-permute-done((bf16[256,512]{1,0:T(8,128)(2,1)S(1)}, bf16[256,512]{1,0:T(8,128)(2,1)S(1)}, u32[]{:S(2)}, u32[]{:S(2)}) %collective-permute-start.21) | collective-permute-done | bytes 262176 | tf_op jit(solution)/shard_map/ppermute | solution.py:45
  366.8 4.3 all-to-all-start.5
  378.9 43.3 %collective-permute-done.13 = bf16[256,1024]{1,0:T(8,128)(2,1)S(1)} collective-permute-done((bf16[256,1024]{1,0:T(8,128)(2,1)S(1)}, bf16[256,1024]{1,0:T(8,128)(2,1)S(1)}, u32[]{:S(2)}, u32[]{:S(2)}) %collective-permute-start.13) | collective-permute-done | bytes 524320 | tf_op jit(solution)/shard_map/ppermute | solution.py:39
  428.9 5.6 %all-to-all-start.6 = ((bf16[8,128,768]{2,1,0:T(8,128)(2,1)}), bf16[8,128,768]{2,1,0:T(8,128)(2,1)}, u32[]{:S(2)}, u32[]{:S(2)}) async-start(bf16[8,128,768]{2,1,0:T(8,128)(2,1)} %bitcast.103), calls=%async_computation.6 | async-start | bytes 3145728 | tf_op jit(solution)/shard_map/all_to_all | solution.py:806
  434.5 12.9 %collective-permute-done.23.crossed = bf16[256,1024]{1,0:T(8,128)(2,1)} collective-permute-done((bf16[256,1024]{1,0:T(8,128)(2,1)}, bf16[256,1024]{1,0:T(8,128)(2,1)}, u32[]{:S(2)}, u32[]{:S(2)}) %collective-permute-start.23) | collective-permute-done | bytes 524320 | tf_op jit(solution)/shard_map/ppermute | solution.py:39
  456.8 10.2 %collective-permute-done.25.refs_2_ = bf16[256,1024]{1,0:T(8,128)(2,1)S(1)} collective-permute-done((bf16[256,1024]{1,0:T(8,128)(2,1)}, bf16[256,1024]{1,0:T(8,128)(2,1)S(1)}, u32[]{:S(2)}, u32[]{:S(2)}) %collective-permute-start.25) | collective-permute-done | bytes 524320 | tf_op jit(solution)/shard_map/ppermute | solution.py:39
  470.7 3.9 shard_map.355
  475.2 31.4 %all_gather.6 = bf16[1024,256]{1,0:T(8,128)(2,1)S(1)} all-gather(bf16[128,256]{1,0:T(8,128)(2,1)S(1)} %reduce_sum.102), channel_id=1, replica_groups=mesh['seq'=8,'mp'=4] {'seq'}, dimensions={0}, use_global_device_ids=true | all-gather | bytes 589824 | tf_op jit(solution)/shard_map/all_gather | solution.py:819
  507.7 4.2 shard_map.361
  (310 shorter events, 161.6 us)
Async XLA Ops:
  11.1 37.6 %collective-permute-start.3 = (bf16[768,1024]{1,0:T(8,128)(2,1)}, bf16[768,1024]{1,0:T(8,128)(2,1)}, u32[]{:S(2)}, u32[]{:S(2)}) collective-permute-start(bf16[768,1024]{1,0:T(8,128)(2,1)} %pad_maximum_fusion.refs_0_), channel_id=1, source_target_pairs={{0,2},{1,3},{2,0},{3,1},{4,6},{5,7},{6,4},{7,5},{8,10},{9,11},{10,... | collective-permute-start | bytes 4718600 | tf_op jit(solution)/shard_map/ppermute | solution.py:39
  27.1 41.2 %collective-permute-start = (bf16[1024,512]{1,0:T(8,128)(2,1)S(1)}, bf16[1024,512]{1,0:T(8,128)(2,1)S(1)}, u32[]{:S(2)}, u32[]{:S(2)}) collective-permute-start(bf16[1024,512]{1,0:T(8,128)(2,1)S(1)} %get-tuple-element.73.kv), channel_id=1, source_target_pairs={{0,4},{4,8},{8,12},{12,16},{16,20},{20,24},{24,28},{1,5},{5,9},{9,... | collective-permute-start | bytes 3145736 | tf_op jit(solution)/shard_map/ppermute | solution.py:45
  30.5 53.8 %collective-permute-start.2 = (bf16[768,1024]{1,0:T(8,128)(2,1)}, bf16[768,1024]{1,0:T(8,128)(2,1)}, u32[]{:S(2)}, u32[]{:S(2)}) collective-permute-start(bf16[768,1024]{1,0:T(8,128)(2,1)} %pad_maximum_fusion.refs_0_), channel_id=1, source_target_pairs={{0,1},{1,0},{2,3},{3,2},{4,5},{5,4},{6,7},{7,6},{8,9},{9,8},{10,11... | collective-permute-start | bytes 4718600 | tf_op jit(solution)/shard_map/ppermute | solution.py:39
  48.7 35.6 %collective-permute-start.4 = (bf16[768,1024]{1,0:T(8,128)(2,1)}, bf16[768,1024]{1,0:T(8,128)(2,1)}, u32[]{:S(2)}, u32[]{:S(2)}) collective-permute-start(bf16[768,1024]{1,0:T(8,128)(2,1)} %collective-permute-done.3.refs_2_), channel_id=1, source_target_pairs={{0,1},{1,0},{2,3},{3,2},{4,5},{5,4},{6,7},{7,6},{8,9},{9,8},{10,11... | collective-permute-start | bytes 4718600 | tf_op jit(solution)/shard_map/ppermute | solution.py:39
  48.7 19.0 %collective-permute-start.1 = (bf16[256,512]{1,0:T(8,128)(2,1)S(1)}, bf16[256,512]{1,0:T(8,128)(2,1)S(1)}, u32[]{:S(2)}, u32[]{:S(2)}) collective-permute-start(bf16[256,512]{1,0:T(8,128)(2,1)S(1)} %get-tuple-element.74), channel_id=1, source_target_pairs={{0,8},{4,12},{8,16},{12,20},{16,24},{20,28},{1,9},{5,13},{9,17},{1... | collective-permute-start | bytes 786440 | tf_op jit(solution)/shard_map/ppermute | solution.py:45
  75.5 438.8 %all-gather.2.cloned.1.call-start = ((), (), s32[]{:S(2)}) async-start(), calls=%async_computation.8 | async-start | bytes 1179648 | tf_op jit(solution)/shard_map/all_gather | solution.py:813
  112.2 16.7 %collective-permute-start.8 = (bf16[256,1024]{1,0:T(8,128)(2,1)S(1)}, bf16[256,1024]{1,0:T(8,128)(2,1)S(1)}, u32[]{:S(2)}, u32[]{:S(2)}) collective-permute-start(bf16[256,1024]{1,0:T(8,128)(2,1)S(1)} %get-tuple-element.80.h_a.refs_0_), channel_id=1, source_target_pairs={{0,1},{1,0},{2,3},{3,2},{4,5},{5,4},{6,7},{7,6},{8,9},{9,8},{10,11... | collective-permute-start | bytes 1572872 | tf_op jit(solution)/shard_map/ppermute | solution.py:39
  229.7 146.4 %collective-permute-start.12 = (bf16[256,1024]{1,0:T(8,128)(2,1)}, bf16[256,1024]{1,0:T(8,128)(2,1)}, u32[]{:S(2)}, u32[]{:S(2)}) collective-permute-start(bf16[256,1024]{1,0:T(8,128)(2,1)} %get-tuple-element.84), channel_id=1, source_target_pairs={{0,1},{1,0},{2,3},{3,2},{4,5},{5,4},{6,7},{7,6},{8,9},{9,8},{10,11... | collective-permute-start | bytes 1572872 | tf_op jit(solution)/shard_map/ppermute | solution.py:39
  229.7 40.5 %all-to-all-start.1 = ((bf16[4,256,256]{2,1,0:T(8,128)(2,1)}), bf16[4,256,256]{2,1,0:T(8,128)(2,1)S(1)}, u32[]{:S(2)}, u32[]{:S(2)}) async-start(bf16[4,256,256]{2,1,0:T(8,128)(2,1)} %get-tuple-element.92), calls=%async_computation.1 | async-start | bytes 1048576 | tf_op jit(solution)/shard_map/all_to_all | solution.py:780
  233.2 286.4 %reduce-scatter.2.cloned.1.call-start = ((), (), s32[]{:S(2)}) async-start(), calls=%async_computation.9 | async-start | bytes 4718592 | tf_op jit(solution)/shard_map/reduce_scatter | solution.py:767
  269.8 101.4 %collective-permute-start.31 = (bf16[2,1024,768]{2,1,0:T(8,128)(2,1)}, bf16[2,1024,768]{2,1,0:T(8,128)(2,1)}, u32[]{:S(2)}, u32[]{:S(2)}) collective-permute-start(bf16[2,1024,768]{2,1,0:T(8,128)(2,1)} %get-tuple-element.115), channel_id=1, source_target_pairs={{0,1},{1,0},{2,3},{3,2},{4,5},{5,4},{6,7},{7,6},{8,9},{9,8},{10,11... | collective-permute-start | bytes 9437192 | tf_op jit(solution)/shard_map/ppermute | solution.py:39
  275.5 66.0 %collective-permute-start.20 = (bf16[1024,512]{1,0:T(8,128)(2,1)S(1)}, bf16[1024,512]{1,0:T(8,128)(2,1)S(1)}, u32[]{:S(2)}, u32[]{:S(2)}) collective-permute-start(bf16[1024,512]{1,0:T(8,128)(2,1)S(1)} %get-tuple-element.98), channel_id=1, source_target_pairs={{4,0},{8,4},{12,8},{16,12},{20,16},{24,20},{28,24},{5,1},{9,5},{13... | collective-permute-start | bytes 3145736 | tf_op jit(solution)/shard_map/ppermute | solution.py:45
  276.8 64.7 %collective-permute-start.21 = (bf16[256,512]{1,0:T(8,128)(2,1)S(1)}, bf16[256,512]{1,0:T(8,128)(2,1)S(1)}, u32[]{:S(2)}, u32[]{:S(2)}) collective-permute-start(bf16[256,512]{1,0:T(8,128)(2,1)S(1)} %get-tuple-element.99), channel_id=1, source_target_pairs={{8,0},{12,4},{16,8},{20,12},{24,16},{28,20},{9,1},{13,5},{17,9},{2... | collective-permute-start | bytes 786440 | tf_op jit(solution)/shard_map/ppermute | solution.py:45
  366.8 62.1 %all-to-all-start.5 = ((bf16[8,128,768]{2,1,0:T(8,128)(2,1)}), bf16[8,128,768]{2,1,0:T(8,128)(2,1)}, u32[]{:S(2)}, u32[]{:S(2)}) async-start(bf16[8,128,768]{2,1,0:T(8,128)(2,1)} %pad_maximum_fusion.1), calls=%async_computation.5 | async-start | bytes 3145728 | tf_op jit(solution)/shard_map/all_to_all | solution.py:806
  375.0 52.3 %collective-permute-start.32 = (bf16[1024,768]{1,0:T(8,128)(2,1)S(1)}, bf16[1024,768]{1,0:T(8,128)(2,1)S(1)}, u32[]{:S(2)}, u32[]{:S(2)}) collective-permute-start(bf16[1024,768]{1,0:T(8,128)(2,1)S(1)} %fusion.2), channel_id=1, source_target_pairs={{0,2},{1,3},{2,0},{3,1},{4,6},{5,7},{6,4},{7,5},{8,10},{9,11},{10,... | collective-permute-start | bytes 4718600 | tf_op jit(solution)/shard_map/ppermute | solution.py:39
  376.0 48.3 %collective-permute-start.22 = (bf16[2,256,1024]{2,1,0:T(8,128)(2,1)S(1)}, bf16[2,256,1024]{2,1,0:T(8,128)(2,1)S(1)}, u32[]{:S(2)}, u32[]{:S(2)}) collective-permute-start(bf16[2,256,1024]{2,1,0:T(8,128)(2,1)S(1)} %copy-done.35), channel_id=1, source_target_pairs={{0,1},{1,0},{2,3},{3,2},{4,5},{5,4},{6,7},{7,6},{8,9},{9,8},{10,11... | collective-permute-start | bytes 3145736 | tf_op jit(solution)/shard_map/ppermute | solution.py:39
  377.4 44.8 %collective-permute-start.13 = (bf16[256,1024]{1,0:T(8,128)(2,1)S(1)}, bf16[256,1024]{1,0:T(8,128)(2,1)S(1)}, u32[]{:S(2)}, u32[]{:S(2)}) collective-permute-start(bf16[256,1024]{1,0:T(8,128)(2,1)S(1)} %add_convert_fusion.3), channel_id=1, source_target_pairs={{0,2},{1,3},{2,0},{3,1},{4,6},{5,7},{6,4},{7,5},{8,10},{9,11},{10,... | collective-permute-start | bytes 1572872 | tf_op jit(solution)/shard_map/ppermute | solution.py:39
  423.3 33.0 %collective-permute-start.15 = (bf16[256,1024]{1,0:T(8,128)(2,1)}, bf16[256,1024]{1,0:T(8,128)(2,1)}, u32[]{:S(2)}, u32[]{:S(2)}) collective-permute-start(bf16[256,1024]{1,0:T(8,128)(2,1)} %add_convert_fusion.2.refs_0_), channel_id=1, source_target_pairs={{0,2},{1,3},{2,0},{3,1},{4,6},{5,7},{6,4},{7,5},{8,10},{9,11},{10,... | collective-permute-start | bytes 1572872 | tf_op jit(solution)/shard_map/ppermute | solution.py:39
  426.3 21.1 %collective-permute-start.23 = (bf16[256,1024]{1,0:T(8,128)(2,1)}, bf16[256,1024]{1,0:T(8,128)(2,1)}, u32[]{:S(2)}, u32[]{:S(2)}) collective-permute-start(bf16[256,1024]{1,0:T(8,128)(2,1)} %fusion.6), channel_id=1, source_target_pairs={{0,2},{1,3},{2,0},{3,1},{4,6},{5,7},{6,4},{7,5},{8,10},{9,11},{10,... | collective-permute-start | bytes 1572872 | tf_op jit(solution)/shard_map/ppermute | solution.py:39
  428.9 93.8 %all-to-all-start.6 = ((bf16[8,128,768]{2,1,0:T(8,128)(2,1)}), bf16[8,128,768]{2,1,0:T(8,128)(2,1)}, u32[]{:S(2)}, u32[]{:S(2)}) async-start(bf16[8,128,768]{2,1,0:T(8,128)(2,1)} %bitcast.103), calls=%async_computation.6 | async-start | bytes 3145728 | tf_op jit(solution)/shard_map/all_to_all | solution.py:806
  456.3 14.4 %collective-permute-start.14 = (bf16[256,1024]{1,0:T(8,128)(2,1)}, bf16[256,1024]{1,0:T(8,128)(2,1)}, u32[]{:S(2)}, u32[]{:S(2)}) collective-permute-start(bf16[256,1024]{1,0:T(8,128)(2,1)} %add_convert_fusion.2.refs_0_), channel_id=1, source_target_pairs={{0,1},{1,0},{2,3},{3,2},{4,5},{5,4},{6,7},{7,6},{8,9},{9,8},{10,11... | collective-permute-start | bytes 1572872 | tf_op jit(solution)/shard_map/ppermute | solution.py:39
  456.3 14.4 %collective-permute-start.16 = (bf16[256,1024]{1,0:T(8,128)(2,1)}, bf16[256,1024]{1,0:T(8,128)(2,1)}, u32[]{:S(2)}, u32[]{:S(2)}) collective-permute-start(bf16[256,1024]{1,0:T(8,128)(2,1)} %collective-permute-done.15.refs_2_), channel_id=1, source_target_pairs={{0,1},{1,0},{2,3},{3,2},{4,5},{5,4},{6,7},{7,6},{8,9},{9,8},{10,11... | collective-permute-start | bytes 1572872 | tf_op jit(solution)/shard_map/ppermute | solution.py:39
  456.8 50.9 %collective-permute-start.24 = (bf16[256,1024]{1,0:T(8,128)(2,1)}, bf16[256,1024]{1,0:T(8,128)(2,1)S(1)}, u32[]{:S(2)}, u32[]{:S(2)}) collective-permute-start(bf16[256,1024]{1,0:T(8,128)(2,1)} %shard_map.360.refs_0_), channel_id=1, source_target_pairs={{0,1},{1,0},{2,3},{3,2},{4,5},{5,4},{6,7},{7,6},{8,9},{9,8},{10,11... | collective-permute-start | bytes 1572872 | tf_op jit(solution)/shard_map/ppermute | solution.py:39
  467.0 40.7 %collective-permute-start.26 = (bf16[256,1024]{1,0:T(8,128)(2,1)S(1)}, bf16[256,1024]{1,0:T(8,128)(2,1)}, u32[]{:S(2)}, u32[]{:S(2)}) collective-permute-start(bf16[256,1024]{1,0:T(8,128)(2,1)S(1)} %collective-permute-done.25.refs_2_), channel_id=1, source_target_pairs={{0,1},{1,0},{2,3},{3,2},{4,5},{5,4},{6,7},{7,6},{8,9},{9,8},{10,11... | collective-permute-start | bytes 1572872 | tf_op jit(solution)/shard_map/ppermute | solution.py:39
  (105 other events, 1014.8 us)
Sparse Core Ops, SparseCore 0:
  229.7 38.3 all-gather.1
  271.7 121.8 reduce-scatter.1

commit v2 on v1

--- a/solution.py
+++ b/solution.py
@@ -39,10 +39,36 @@
     return lax.ppermute(value, "mp", [(rank, rank ^ step) for rank in range(count)])
 
 
-def from_behind(value, axis, steps):
-    count = lax.axis_size(axis)
+SEQ = ("far", "near")
+
+
+def from_behind(value, steps):
+    count = lax.axis_size("far") * lax.axis_size("near")
     leading, last = (max(0, -steps), min(count, count - steps))
-    return lax.ppermute(value, axis, [(source, source + steps) for source in range(leading, last)])
+    return lax.ppermute(value, SEQ, [(source, source + steps) for source in range(leading, last)])
+
+
+def other_near(value):
+    return lax.ppermute(value, "near", [(0, 1), (1, 0)])
+
+
+def over_shards(blocks):
+    far = lax.axis_size("far")
+    parts = blocks.reshape(far, 2, -1, blocks.shape[-1])
+    own = lax.axis_index("near")
+    sent = other_near(lax.dynamic_index_in_dim(parts, 1 - own, 1, keepdims=False))
+    kept = lax.dynamic_index_in_dim(parts, own, 1, keepdims=False)
+    half = (kept.astype(F32) + sent.astype(F32)).astype(BF)
+    return sum_rows(lax.all_to_all(half, "far", 0, 0))
+
+
+def from_shards(own):
+    far = lax.axis_size("far")
+    mine = lax.all_to_all(jnp.broadcast_to(own[None], (far, *own.shape)), "far", 0, 0)
+    other = other_near(mine)
+    first = lax.axis_index("near") == 0
+    both = jnp.stack([jnp.where(first, mine, other), jnp.where(first, other, mine)], axis=1)
+    return both.reshape(-1, own.shape[-1])
 
 
 def whole(array):
@@ -54,25 +80,30 @@
     return jax.ShapeDtypeStruct(shape, dtype)
 
 
-def run(kernel, ids, args, outs, grid=(1,), in_specs=None, out_specs=None, scratch=(), flops=0, exps=0, vmem=40):
+def run(kernel, ids, args, outs, grid=(1,), in_specs=None, out_specs=None, scratch=(), micros=1, vmem=40):
     in_specs = in_specs or [None] * len(args)
     out_specs = out_specs or [None] * len(outs)
     in_specs = [whole(a) if s is None else s for a, s in zip(args, in_specs)]
     out_specs = [whole(a) if s is None else s for a, s in zip(outs, out_specs)]
     moved = sum(a.size * a.dtype.itemsize for a in list(args) + list(outs))
+    prefetch = () if ids is None else (ids,)
     return pl.pallas_call(
-        kernel,
+        functools.partial(kernel, None) if ids is None else kernel,
         out_shape=outs,
         grid_spec=pltpu.PrefetchScalarGridSpec(
-            num_scalar_prefetch=1,
+            num_scalar_prefetch=len(prefetch),
             grid=grid,
             in_specs=in_specs,
             out_specs=out_specs,
             scratch_shapes=list(scratch),
         ),
         compiler_params=pltpu.CompilerParams(vmem_limit_bytes=vmem * MIB),
-        cost_estimate=pl.CostEstimate(flops=flops, transcendentals=exps, bytes_accessed=moved),
-    )(ids, *args)
+        cost_estimate=pl.CostEstimate(flops=int(micros * 1e6), transcendentals=0, bytes_accessed=1000),
+    )(*prefetch, *args)
+
+
+def after(value, *others):
+    return lax.optimization_barrier((value, *others))[0]
 
 
 def ln_rows(values):
@@ -98,8 +129,47 @@
     return [rows * head_mask(head, heads) for head in range(heads)]
 
 
-def entry_kernel(ids, tok, gain, bias, wq, wk, wv, hid, q, kv, tail):
+def layout_kernel(rows, lens, prompts, place, ids, begin):
+    items = lens.shape[0]
+    offset = place[0] * rows
+    own_first = offset + place[1] * (rows // 4)
+    positions = offset + lax.broadcasted_iota(jnp.int32, (1, rows), 1)
+    found = jnp.zeros((1, rows), jnp.int32)
+    lows = [jnp.int32(0)] * (rows // BLOCK)
+    begun = base = own_base = jnp.int32(0)
+    for item in range(items):
+        found = jnp.where(positions >= begun, begun, found)
+        lows = [jnp.where(offset + block * BLOCK >= begun, begun, low) for block, low in enumerate(lows)]
+        begun = begun + lens[item]
+        base = base + jnp.where(begun <= offset, 1, 0)
+        own_base = own_base + jnp.where(begun <= own_first, 1, 0)
+    begin[...] = found - offset
+    base = jnp.minimum(base, items - 3)
+    own_base = jnp.minimum(own_base, items - 2)
+    begun = bound = jnp.int32(0)
+    for item in range(items):
+        begun = begun + lens[item]
+        bound = jnp.where(own_base == item, begun, bound)
+    ids[0] = place[0]
+    ids[1] = place[1]
+    ids[2] = base
+    ids[3] = (own_base - base) * 128
+    ids[4] = bound - own_first
+    ids[5] = prompts[own_base]
+    ids[6] = prompts[own_base + 1]
+    ids[7] = 0
+    for block, low in enumerate(lows):
+        ids[8 + block] = low - offset
+
+
+def entry_kernel(ids, tok, gain, bias, wq, wk, wv, merge, pq, pm, hid, q, kv, tail, pack):
     width = wq.shape[1]
+    for part, source in enumerate((merge, pq, pm)):
+
+        @pl.when(pl.program_id(0) == part)
+        def _():
+            pack[part * width : (part + 1) * width, :] = source[...].T if part == 1 else source[...]
+
     normed, _ = ln_rows(tok[...].astype(F32))
     hidden = (normed * gain[...] + bias[...]).astype(BF)
     hid[...] = hidden
@@ -361,7 +431,7 @@
 def cross_back_kernel(ids, kept, sent, crossed, og, after, after_self, q, stat, *refs):
     packs, pairs = refs[:4], refs[4:8]
     gain2, gain3 = refs[8:10]
-    cog_o, cqg_o, slg_o, resid_o, shg_o, keep_o, send_o, norms_o = refs[10:]
+    cog_o, cqg_o, slg_o, resid_o, shg_o, keep0_o, keep1_o, send_o, norms_o = refs[10:]
     rows, model = after.shape
     width = packs[0].shape[0] // 3
     heads = width // HD
@@ -376,7 +446,8 @@
     cog_o[...] = low_resid
     bias = cross_bias(ids, prompt_rows, rows)
     first = pl.multiple_of(ids[3], prompt_rows)
-    keep_o[...] = jnp.zeros_like(keep_o)
+    keep0_o[...] = jnp.zeros_like(keep0_o)
+    keep1_o[...] = jnp.zeros_like(keep1_o)
     send_o[...] = jnp.zeros_like(send_o)
     for d in range(4):
         columns = slice(d * width, (d + 1) * width)
@@ -398,9 +469,9 @@
             value_sum = value_term if value_sum is None else value_sum + value_term
             parts.append(nn(keys_t[head * HD : (head + 1) * HD, :], score_grad))
         cqg_o[:, columns] = (jnp.concatenate(parts, axis=0).T * SCALE).astype(BF)
-        target = keep_o if d % 2 == 0 else send_o
-        target[d // 2, pl.ds(first, 2 * prompt_rows), :width] = key_sum.astype(BF)
-        target[d // 2, pl.ds(first, 2 * prompt_rows), width:] = value_sum.astype(BF)
+        target = (keep0_o, send_o.at[0], keep1_o, send_o.at[1])[d]
+        target[pl.ds(first, 2 * prompt_rows), :width] = key_sum.astype(BF)
+        target[pl.ds(first, 2 * prompt_rows), width:] = value_sum.astype(BF)
     two_grad = None
     for d in range(4):
         term = nn(cqg_o[:, d * width : (d + 1) * width], packs[d][width : 2 * width, :])
@@ -474,8 +545,7 @@
         ],
         out_specs=[column, column, full, full] * 2,
         scratch=[pltpu.VMEM((rows, model), F32)] * 4,
-        flops=2 * 2 * 3 * rows * model * hidden,
-        exps=2 * rows * hidden,
+        micros=12,
     )
 
 
@@ -522,29 +592,22 @@
         in_specs=[None] * 4 + [front] * 4 + [back] * 4 + [None],
         out_specs=[pl.BlockSpec((model, chunk), lambda j, s: (0, j))],
         scratch=[pltpu.VMEM((model, 4 * rows), BF)],
-        flops=2 * 2 * 4 * rows * model * hidden,
+        micros=9,
     )[0]
 
 
-def head_weights_kernel(ids, two, cqg, cog, crossed, slg, low, keep, send, turned):
-    step = pl.program_id(0)
+def head_weights_kernel(ids, two, cqg, cog, crossed, slg, low, keep0, keep1, send):
     rank = ids[1]
     width = low.shape[2]
-
-    @pl.when(step == 0)
-    def _():
-        turned[0] = two[...].T
-        turned[1] = cog[...].T
-        turned[2] = slg[...].T
-
-    for side, out in enumerate((keep, send)):
-        columns = pl.ds(pl.multiple_of((2 * step + side) * width, width), width)
-        out[0, :, :width] = nn(turned[0], cqg[:, columns]).astype(BF)
-        out[0, :, width : 2 * width] = nn(turned[1], crossed[:, columns]).astype(BF)
-        out[0, :, 2 * width :] = nn(turned[2], low[rank ^ (2 * step + side)]).astype(BF)
-
-
-def key_sum_kernel(ids, dkv, near, far, hid, dq, wq, wk, wv, gain, bias, kvg_o, keep, send, norms):
+    two_t, cog_t, slg_t = two[...].T, cog[...].T, slg[...].T
+    for d, out in enumerate((keep0, send.at[0], keep1, send.at[1])):
+        columns = slice(d * width, (d + 1) * width)
+        out[:, :width] = nn(two_t, cqg[:, columns]).astype(BF)
+        out[:, width : 2 * width] = nn(cog_t, crossed[:, columns]).astype(BF)
+        out[:, 2 * width :] = nn(slg_t, low[rank ^ d]).astype(BF)
+
+
+def key_sum_kernel(ids, dkv, near, far, hid, dq, wq, wk, wv, gain, bias, kvg_o, keep0, keep1, send, norms):
     rows, width2 = dkv.shape
     width = width2 // 2
     quarter = rows // 4
@@ -564,14 +627,13 @@
         plain = jnp.sum(part, axis=0, keepdims=True)
         product = term if product is None else product + term
         total = plain if total is None else total + plain
-        target = keep if d % 2 == 0 else send
-        target[d // 2] = part.astype(BF)
+        (keep0, send.at[0], keep1, send.at[1])[d][...] = part.astype(BF)
     norms[0:1, :] = (product - bias[...] * total) / gain[...]
     norms[1:2, :] = total
 
 
 def entry_back_kernel(ids, keep, sent, crossed, tok, gain, resid, out):
-    grad = keep[0].astype(F32) + sent[0].astype(F32) + crossed[...].astype(F32)
+    grad = keep[...].astype(F32) + sent[0].astype(F32) + crossed[...].astype(F32)
     normed, inverse = ln_rows(tok[...].astype(F32))
     out[...] = (resid[...] + ln_back(grad, gain[...], normed, inverse)).astype(BF)
 
@@ -594,6 +656,7 @@
         [shaped((4 * rows, model), dtype)],
         grid=(4,),
         out_specs=[pl.BlockSpec((rows, model), lambda i, s: (i, 0))],
+        micros=4,
     )[0]
 
 
@@ -631,7 +694,6 @@
     output_grad,
 ):
     rows, model = tokens.shape
-    shards = lax.axis_size("seq")
     ranks = lax.axis_size("mp")
     width = query_weight.shape[1]
     heads = width // HD
@@ -639,72 +701,55 @@
     quarter = rows // ranks
     steps = rows // BLOCK
     hidden_units = expand_weight.shape[1]
-    assert ranks == 4 and quarter == BLOCK
-
-    rank = lax.axis_index("mp")
-    offset = lax.axis_index("seq") * rows
-    ends = jnp.cumsum(item_lengths)
-    starts = ends - item_lengths
-    positions = jnp.arange(rows, dtype=jnp.int32) + offset
-
-    def begin_of(where):
-        return jnp.max(jnp.where(starts[None, :] <= where[:, None], starts[None, :], 0), axis=1)
-
-    begin = (begin_of(positions) - offset)[None, :]
-    lows = begin_of(offset + BLOCK * jnp.arange(steps, dtype=jnp.int32)) - offset
-    base = jnp.minimum(jnp.sum((ends <= offset).astype(jnp.int32)), items - 3)
-    own_first = offset + rank * quarter
-    own_base = jnp.minimum(jnp.sum((ends <= own_first).astype(jnp.int32)), items - 2)
-    numbers = jnp.arange(items, dtype=jnp.int32)
-
-    def at(values, index):
-        return jnp.sum(jnp.where(numbers == index, values, 0))
-
-    ids = jnp.stack(
-        [
-            lax.axis_index("seq"),
-            rank,
-            base,
-            (own_base - base) * prompt_rows,
-            at(ends, own_base) - own_first,
-            at(prompt_lengths, own_base),
-            at(prompt_lengths, own_base + 1),
-            jnp.zeros_like(rank),
-        ]
-    )
-    ids = jnp.concatenate([ids, lows]).astype(jnp.int32)
+    shards = lax.axis_size("far") * lax.axis_size("near")
+    assert ranks == 4 and quarter == BLOCK and prompt_rows == 128 and items % shards == 0
+
+    place = jnp.stack([lax.axis_index(SEQ), lax.axis_index("mp")]).astype(jnp.int32)
+    scalars = pl.BlockSpec(memory_space=pltpu.SMEM)
+    ids, begin = pl.pallas_call(
+        functools.partial(layout_kernel, rows),
+        out_shape=[shaped((8 + steps,), jnp.int32), shaped((1, rows), jnp.int32)],
+        in_specs=[scalars] * 3,
+        out_specs=[scalars, pl.BlockSpec(memory_space=pltpu.VMEM)],
+    )(item_lengths, prompt_lengths, place)
+    base = ids[2]
 
     row = lambda vector: vector.reshape(1, -1)
     own_rows = lambda columns: pl.BlockSpec((quarter, columns), lambda *g: (g[-1][1], 0))
 
-    block_rows = lambda columns: pl.BlockSpec((BLOCK, columns), lambda i, s: (i, 0))
-    hidden_one, q, kv, kv_tail = run(
+    block_rows = lambda columns: pl.BlockSpec((BLOCK, columns), lambda i, *s: (i, 0))
+    hidden_one, q, kv, kv_tail, pack = run(
         entry_kernel,
-        ids,
-        (tokens, row(entry_gain), row(entry_bias), query_weight, key_weight, value_weight),
-        [shaped((rows, model), BF), shaped((rows, width), BF), shaped((rows, 2 * width), BF), shaped((BLOCK, 2 * width), BF)],
+        None,
+        (tokens, row(entry_gain), row(entry_bias), query_weight, key_weight, value_weight, merge_weight, prompt_query, prompt_merge),
+        [
+            shaped((rows, model), BF),
+            shaped((rows, width), BF),
+            shaped((rows, 2 * width), BF),
+            shaped((BLOCK, 2 * width), BF),
+            shaped((3 * width, model), BF),
+        ],
         grid=(steps,),
-        in_specs=[block_rows(model)] + [None] * 5,
-        out_specs=[block_rows(model), block_rows(width), block_rows(2 * width), None],
-        flops=6 * rows * model * width,
-    )
-    kv_near = from_behind(kv, "seq", 1)
-    kv_far = from_behind(kv_tail, "seq", 2)
-
-    pack = jnp.concatenate([merge_weight, prompt_query.T, prompt_merge], axis=0)
+        in_specs=[block_rows(model)] + [None] * 8,
+        out_specs=[block_rows(model), block_rows(width), block_rows(2 * width), None, None],
+        micros=5,
+    )
+    kv_near = from_behind(kv, 1)
+    kv_far = from_behind(kv_tail, 2)
+
     pair = run(
         prompt_kernel,
         ids,
-        (text_states, prompt_key, prompt_value),
+        (after(text_states, kv), prompt_key, prompt_value),
         [shaped((3 * prompt_rows, 2 * width), BF)],
         grid=(3,),
         in_specs=[pl.BlockSpec((1, prompt_rows, model), lambda i, s: (s[2] + i, 0, 0)), None, None],
         out_specs=[pl.BlockSpec((prompt_rows, 2 * width), lambda i, s: (i, 0))],
-        flops=4 * 3 * prompt_rows * model * width,
+        micros=1.5,
     )[0]
-    packs = gather(pack)
-    pairs = gather(pair)
-    hidden_grad = nt(output_grad, shrink_weight).astype(BF)
+    pack_near, pack_across = partner(pack, 1), partner(pack, 2)
+    pair_near, pair_across = partner(pair, 1), partner(after(pair, pack), 2)
+    hidden_grad = nt(after(output_grad, kv, pack), shrink_weight).astype(BF)
 
     state = [shaped((steps, heads, HD, BLOCK), F32), shaped((steps, heads, BLOCK), F32), shaped((steps, heads, BLOCK), F32)]
     state_specs = [
@@ -717,19 +762,18 @@
     begin_spec = pl.BlockSpec((1, BLOCK), lambda i, s: (0, i))
     piece_spec = pl.BlockSpec((1, BLOCK, width), lambda i, s: (i, 0, 0))
     turned = lambda blocks: pltpu.VMEM((blocks, width, BLOCK), BF)
-    pair_flops = 2 * heads * BLOCK * BLOCK * width
     acc, top, total = run(
         attend_local_kernel,
         ids,
-        (q, kv, begin),
+        (after(q, pack, pair), kv, begin),
         state,
         grid=(steps,),
         in_specs=[q_spec, None, begin_spec],
         out_specs=state_specs,
         scratch=[turned(steps)] + state_scratch,
-        flops=2 * pair_flops * 10,
-        exps=heads * BLOCK * BLOCK * 10,
-    )
+        micros=12,
+    )
+    kv_near, kv_far = lax.optimization_barrier((kv_near, kv_far, acc, hidden_grad))[:2]
     self_out, self_low, lse = run(
         attend_remote_kernel,
         ids,
@@ -739,10 +783,12 @@
         in_specs=[q_spec, None, None, begin_spec] + state_specs,
         out_specs=[piece_spec, piece_spec, state_specs[1]],
         scratch=[turned(steps + 1)] + state_scratch,
-        flops=2 * pair_flops * 10,
-        exps=heads * BLOCK * BLOCK * 10,
+        micros=10,
     )
     low_rows = lax.all_to_all(self_low, "mp", 0, 0)
+    pack_across, pair_across = lax.optimization_barrier((pack_across, pair_across, self_low))[:2]
+    packs = (pack, pack_near, pack_across, partner(pack_across, 1))
+    pairs = (pair, pair_near, pair_across, partner(pair_across, 1))
 
     wide = lambda dtype: shaped((quarter, model), dtype)
     stat_shape = shaped((ranks * heads, quarter), F32)
@@ -753,70 +799,60 @@
         (tokens, low_rows, *packs, *pairs, *norms),
         [wide(F32), wide(BF), wide(BF), stat_shape, wide(BF), wide(F32), wide(BF)],
         in_specs=[own_rows(model)] + [None] * 13,
-        flops=6 * quarter * model * model + 4 * ranks * pair_flops,
-        exps=ranks * heads * BLOCK * BLOCK,
-    )
-
-    threes = gather(hidden_three)
-    low0, pre0, out0, part0, low1, pre1, out1, part1 = feed(ids, 0, threes[0], threes[1], hidden_grad, expand_weight, shrink_weight)
-    low2, pre2, out2, part2, low3, pre3, out3, part3 = feed(ids, 2, threes[2], threes[3], hidden_grad, expand_weight, shrink_weight)
-    sent1 = partner(part1, 1)
-    across = partner((part2.astype(F32) + partner(part3, 1).astype(F32)).astype(BF), 2)
-
-    feed_grads = feed_weights(ids, threes, (pre0, pre1, pre2, pre3), (low0, low1, low2, low3), output_grad)
-    feed_sum = lax.psum_scatter(feed_grads, "seq", scatter_dimension=0, tiled=True)
-
-    pair_out = shaped((2, 3 * prompt_rows, 2 * width), BF)
-    cog, cqg, slg, resid, shg, pair_keep, pair_send, norm_grads = run(
+        micros=11,
+    )
+
+    three_near, three_across = partner(hidden_three, 1), partner(hidden_three, 2)
+    low0, pre0, out0, part0, low1, pre1, out1, part1 = feed(
+        ids, 0, hidden_three, three_near, hidden_grad, expand_weight, shrink_weight
+    )
+    three_across = after(three_across, part1)
+    threes = (hidden_three, three_near, three_across, partner(three_across, 1))
+    sent1, out_sent1 = partner(part1, 1), partner(out1, 1)
+    low2, pre2, out2, part2, low3, pre3, out3, part3 = feed(
+        ids, 2, threes[2], threes[3], hidden_grad, expand_weight, shrink_weight
+    )
+    partial = (part2.astype(F32) + partner(part3, 1).astype(F32)).astype(BF)
+    across = partner(partial, 2)
+    out_partial = (out2.astype(F32) + partner(after(out3, partial), 1).astype(F32)).astype(BF)
+    feed_grads = feed_weights(ids, threes, (pre0, pre1, pre2, pre3), (low0, low1, low2, low3), after(output_grad, partial))
+    feed_sum = lax.psum_scatter(feed_grads, SEQ, scatter_dimension=0, tiled=True)
+    across = after(across, feed_grads, out_partial)
+    out_across = partner(after(out_partial, across), 2)
+
+    pair_out = shaped((3 * prompt_rows, 2 * width), BF)
+    cog, cqg, slg, resid, shg, pair_keep0, pair_keep1, pair_send, norm_grads = run(
         cross_back_kernel,
         ids,
         (part0, sent1, across, output_grad, after_cross, after_self, cross_q, stat, *packs, *pairs, norms[0], norms[2]),
-        [wide(BF), wide(BF), wide(BF), wide(F32), shaped((ranks, quarter, width), BF), pair_out, pair_out, shaped((4, model), F32)],
+        [wide(BF), wide(BF), wide(BF), wide(F32), shaped((ranks, quarter, width), BF)]
+        + [pair_out, pair_out, shaped((2, *pair_out.shape), BF), shaped((4, model), F32)],
         in_specs=[None] * 3 + [own_rows(model)] + [None] * 14,
-        flops=6 * quarter * model * model + 10 * ranks * pair_flops,
-        exps=ranks * heads * BLOCK * BLOCK,
+        micros=15,
         vmem=48,
     )
     self_grad = lax.all_to_all(shg, "mp", 0, 0)
 
-    out_across = partner((out2.astype(F32) + partner(out3, 1).astype(F32)).astype(BF), 2)
-    out_rows = (
-        after_cross + out0.astype(F32) + partner(out1, 1).astype(F32) + out_across.astype(F32)
-    ).astype(BF)
-    layer_output = assemble(ids, gather(out_rows), BF)
-
-    pieces = shaped((2, model, 3 * width), BF)
-    piece_out = pl.BlockSpec((1, model, 3 * width), lambda i, s: (i, 0, 0))
-    head_keep, head_send = run(
+    pieces = shaped((model, 3 * width), BF)
+    head_keep0, head_keep1, head_send = run(
         head_weights_kernel,
         ids,
         (hidden_two, cqg, cog, cross_out, slg, low_rows),
-        [pieces, pieces],
-        grid=(2,),
-        out_specs=[piece_out, piece_out],
-        scratch=[pltpu.VMEM((3, model, quarter), BF)],
-        flops=6 * quarter * model * model,
-    )
-
-    def over_ranks(keep, send):
-        sent = partner(send, 1).astype(F32) + keep.astype(F32)
-        return (sent[0] + partner(sent[1].astype(BF), 2).astype(F32)).astype(BF)
-
-    def over_shards(blocks):
-        return sum_rows(lax.all_to_all(blocks.reshape(shards, -1, blocks.shape[-1]), "seq", 0, 0))
-
-    head_sum = over_shards(over_ranks(head_keep, head_send))
-
-    pair_sum = over_ranks(pair_keep, pair_send).reshape(3, prompt_rows, 2 * width)
-    placed = lax.dynamic_update_slice_in_dim(jnp.zeros((items, prompt_rows, 2 * width), BF), pair_sum, base, 0)
-    own_pair = over_shards(placed.reshape(items * prompt_rows, 2 * width)).astype(BF)
-    pair_grad = lax.all_gather(own_pair, "seq", axis=0, tiled=True)
-    flat_text = text_states.reshape(items * prompt_rows, model)
-    prompt_grads = tn(flat_text, pair_grad)
-    text_part = nt(own_pair[:, :width], prompt_key) + nt(own_pair[:, width:], prompt_value)
-    text_blocks = jnp.swapaxes(text_part.astype(BF).reshape(-1, ranks, width), 0, 1)
-    text_own = sum_rows(lax.all_to_all(text_blocks, "mp", 0, 0)).astype(BF)
-    text_grad = lax.all_gather(text_own, "seq", axis=0, tiled=True).astype(F32).reshape(items, prompt_rows, width)
+        [pieces, pieces, shaped((2, *pieces.shape), BF)],
+        micros=4,
+    )
+
+    def added(*terms):
+        total = terms[0].astype(F32)
+        for term in terms[1:]:
+            total = total + term.astype(F32)
+        return total.astype(BF)
+
+    pair_sent, head_sent = partner(pair_send, 1), partner(head_send, 1)
+    pair_half = added(pair_keep1, pair_sent[1])
+    self_grad = after(self_grad, head_keep0, pair_half)
+    pair_across = partner(after(pair_half, self_grad), 2)
+    head_across = partner(after(added(head_keep1, head_sent[1]), self_grad), 2)
 
     lse_spec = state_specs[1]
     stat4 = shaped((steps, heads, BLOCK), F32)
@@ -829,11 +865,17 @@
         in_specs=[q_spec, None, None, begin_spec, piece_spec, piece_spec, lse_spec],
         out_specs=[None, None, state_specs[0], lse_spec],
         scratch=[turned(steps + 1), pltpu.VMEM((steps + 1, BLOCK, 2 * width), F32), state_scratch[0]],
-        flops=5 * pair_flops * 10,
-        exps=heads * BLOCK * BLOCK * 10,
-    )
-    from_near = from_behind(dkv_near, "seq", -1)
-    from_far = from_behind(dkv_far, "seq", -2)
+        micros=10,
+    )
+    from_near = from_behind(dkv_near, -1)
+    from_far = from_behind(dkv_far, -2)
+
+    pair_sum = added(pair_keep0, pair_sent[0], pair_across).reshape(3, prompt_rows, 2 * width)
+    placed = lax.dynamic_update_slice_in_dim(jnp.zeros((items, prompt_rows, 2 * width), BF), pair_sum, base, 0)
+    placed = after(placed, dkv_near).reshape(items * prompt_rows, 2 * width)
+    dq_part = after(dq_part, placed)
+    own_pair = over_shards(placed).astype(BF)
+
     dkv, dq = run(
         back_local_kernel,
         ids,
@@ -843,35 +885,48 @@
         in_specs=[q_spec, None, begin_spec, piece_spec, lse_spec, lse_spec, state_specs[0]],
         out_specs=[None, q_spec],
         scratch=[turned(steps), pltpu.VMEM((steps, BLOCK, 2 * width), F32), state_scratch[0]],
-        flops=5 * pair_flops * 10,
-        exps=heads * BLOCK * BLOCK * 10,
-    )
-
-    two_quarters = shaped((2, quarter, model), BF)
-    kvg, one_keep, one_send, entry_norms = run(
+        micros=14,
+    )
+    text_part = nt(own_pair[:, :width], prompt_key) + nt(own_pair[:, width:], prompt_value)
+    text_blocks = jnp.swapaxes(text_part.astype(BF).reshape(-1, ranks, width), 0, 1)
+    text_own = sum_rows(lax.all_to_all(text_blocks, "mp", 0, 0)).astype(BF)
+
+    head_rows = added(head_keep0, head_sent[0], head_across)
+    out_rows = added(after_cross, out0, out_sent1, out_across)
+    layer_output = assemble(ids, gather(after(out_rows, head_rows)), BF)
+
+    from_near, from_far = lax.optimization_barrier((from_near, from_far, dq))[:2]
+    quarter_out = shaped((quarter, model), BF)
+    kvg, one_keep0, one_keep1, one_send, entry_norms = run(
         key_sum_kernel,
         ids,
         (dkv, from_near, from_far, hidden_one, dq, query_weight, key_weight, value_weight, row(entry_gain), row(entry_bias)),
-        [shaped((rows, 2 * width), BF), two_quarters, two_quarters, shaped((2, model), F32)],
-        flops=6 * rows * model * width,
+        [shaped((rows, 2 * width), BF), quarter_out, quarter_out, shaped((2, *quarter_out.shape), BF), shaped((2, model), F32)],
+        micros=3,
     )
     one_sent = partner(one_send, 1)
-    one_across = partner((one_keep[1].astype(F32) + one_sent[1].astype(F32)).astype(BF), 2)
+    one_across = partner(added(one_keep1, one_sent[1]), 2)
+    head_sum = over_shards(after(head_rows, from_near, from_far))
+    entry_grads = jnp.concatenate([tn(hidden_one, dq), tn(hidden_one, kvg)], axis=1).astype(BF)
+    one_across = after(one_across, entry_grads)
+    entry_sum = over_shards(entry_grads)
     grad_rows = run(
         entry_back_kernel,
         ids,
-        (one_keep, one_sent, one_across, tokens, row(entry_gain), resid),
+        (one_keep0, one_sent, one_across, tokens, row(entry_gain), resid),
         [wide(BF)],
         in_specs=[None] * 3 + [own_rows(model)] + [None] * 2,
+        micros=3,
     )[0]
     tokens_grad = assemble(ids, gather(grad_rows), F32)
 
-    entry_grads = jnp.concatenate([tn(hidden_one, dq), tn(hidden_one, kvg)], axis=1).astype(BF)
-    entry_sum = over_shards(entry_grads)
-
-    norm_rows = jnp.concatenate([entry_norms, norm_grads[2:4], norm_grads[0:2], jnp.zeros((2, model), F32)])
+    prompt_all = from_shards(jnp.concatenate([own_pair, text_own], axis=1))
+    prompt_grads = tn(text_states.reshape(items * prompt_rows, model), prompt_all[:, : 2 * width])
+    text_grad = prompt_all[:, 2 * width :].astype(F32).reshape(items, prompt_rows, width)
+
+    norm_rows = jnp.concatenate([after(entry_norms, one_across), norm_grads[2:4], norm_grads[0:2], jnp.zeros((2, model), F32)])
     norm_blocks = jnp.swapaxes(norm_rows.reshape(8, shards, model // shards), 0, 1)
-    norm_sum = jnp.sum(lax.all_to_all(norm_blocks, "seq", 0, 0), axis=0)
+    norm_sum = jnp.sum(lax.all_to_all(norm_blocks, SEQ, 0, 0), axis=0)
     norm_sum = norm_sum + partner(norm_sum, 1)
     norm_sum = norm_sum + partner(norm_sum, 2)
 
@@ -901,16 +956,18 @@
 
 
 def solution(mesh):
-    seq, mp, both = P("seq", None), P("mp", None), P(None, "mp")
+    shards = mesh.shape["seq"]
+    mesh = jax.sharding.Mesh(mesh.devices.reshape(shards // 2, 2, mesh.shape["mp"]), (*SEQ, "mp"))
+    seq, mp, both = P(SEQ, None), P("mp", None), P(None, "mp")
     return jax.shard_map(
         body,
         mesh=mesh,
         in_specs=(seq,) + (P(),) * 9 + (both,) * 3 + (mp,) + (both,) * 3 + (mp, both, mp, seq),
         out_specs=(
             (seq, seq, P(None, None, "mp"))
-            + (P("seq"),) * 6
-            + (P("seq", "mp"),) * 3
-            + (P("mp", "seq"), P("seq", "mp"), both, both, P("mp", "seq"), P("seq", "mp"), P("mp", "seq"))
+            + (P(SEQ),) * 6
+            + (P(SEQ, "mp"),) * 3
+            + (P("mp", SEQ), P(SEQ, "mp"), both, both, P("mp", SEQ), P(SEQ, "mp"), P("mp", SEQ))
         ),
         check_vma=False,
     )

time: 540 us -> 418 us (0.77)
  waiting for transfers between devices: 186 us -> 102 us
  blocking collectives: 66.9 us -> 0 us
  starting transfers between devices: 51.2 us -> 71.6 us
  other arithmetic: 25.3 us -> 32.5 us
    ppermute x29, waiting for transfers between devices: 126 us -> 31.7 us  [partner(): lax.ppermute(value, 'mp', [(rank, rank ^ step) for rank in range(count)])]
    all_to_all x1 -> x0, blocking collectives: 35.4 us -> none  [over_shards(): lax.all_to_all(blocks.reshape(shards, -1, blocks.shape[-1]), 'seq', 0, 0)]
    all_gather x1 -> x0, blocking collectives: 31.4 us -> none  [body(): lax.all_gather(text_own, 'seq', axis=0, tiled=True).astype(F32)]
    convert_element_type x6 -> x11, other arithmetic: 6.45 us -> 20.8 us  [the longest x6 12.3 us: added(): return total.astype(BF)]
    all_to_all x3 -> x5, starting transfers between devices: 13.4 us -> 24.7 us  [the longest x3 15.5 us: over_shards(): return sum_rows(lax.all_to_all(half, 'far', 0, 0))]
    ppermute x4 -> x8, starting transfers between devices: 9.8 us -> 20 us  [the longest x4 10.3 us: from_behind(): lax.ppermute(value, SEQ, [(source, source + steps) for source in range(le...]
    ppermute x4 -> x8, waiting for transfers between devices: 47.2 us -> 55 us  [the longest x4 55 us: other_near(): return lax.ppermute(value, 'near', [(0, 1), (1, 0)])]
    unnamed x182 -> x179, local copies, waits for them, and re-layouts: 55.8 us -> 50.8 us
  transfers between devices with their start and end apart: 41 -> 46, of which waited for: 14 -> 15; matrix products, arithmetic and copies ran while one was open for 7% -> 13% of each run, Pallas kernels for 16% -> 18%
where the time goes in v2:
time: 418 us; the launch traced here: 410 us
  Pallas kernels  118 us (28%)
  waiting for transfers between devices  102 us (24%)
  starting transfers between devices  71.6 us (17%)
  local copies, waits for them, and re-layouts  59 us (14%)
  other arithmetic  32.5 us (8%)
  between operations  17.3 us (4%)
  matrix products  9.32 us (2%)
    pallas_call x16, Pallas kernels, run(): pl.pallas_call(functools.partial(kernel, None) if ids is None else kernel...  117 us
    ppermute x4, waiting for transfers between devices, other_near(): return lax.ppermute(value, 'near', [(0, 1), (1, 0)])  55 us
    unnamed x179, local copies, waits for them, and re-layouts  50.8 us
    ppermute x29, waiting for transfers between devices, partner(): lax.ppermute(value, 'mp', [(rank, rank ^ step) for rank in range(count)])  31.7 us
    all_to_all x3, starting transfers between devices, over_shards(): return sum_rows(lax.all_to_all(half, 'far', 0, 0))  15.5 us
    ppermute x29, starting transfers between devices, partner(): lax.ppermute(value, 'mp', [(rank, rank ^ step) for rank in range(count)])  14.7 us
    convert_element_type x6, other arithmetic, added(): return total.astype(BF)  12.3 us
    ppermute x4, starting transfers between devices, from_behind(): lax.ppermute(value, SEQ, [(source, source + steps) for source in range(le...  10.3 us
  transfers between devices with their start and end apart: 46, of which 15 were waited for; matrix products, arithmetic and copies ran while one was open for 13% of the time, Pallas kernels for 18%

profile of v2, /device:TPU:0, one launch (start us, length us, event | category | flops | bytes accessed | tf_op | source)
XLA Modules:
  0.0 410.2 jit_solution(17445875377550190189)
XLA Ops:
  16.4 5.1 %shard_map.349 = (bf16[1024,1024]{1,0:T(8,128)(2,1)S(1)}, bf16[1024,256]{1,0:T(8,128)(2,1)S(1)}, bf16[1024,512]{1,0:T(8,128)(2,1)}, bf16[256,512]{1,0:T(8,128)(2,1)}, bf16[768,1024]{1,0:T(8,128)(2,1)}) custom-call(bf16[1024,1024]{1,0:T(8,128)(2,1)S(1)} %copy-done, f32[1,1024]{1,0:T(1,128)S(1)} %bitcast.109, f32[1,1024]{1,0:T(1,128)S(1)} %bitcast.116, ...), custom_call_target="tpu_custom_call" | custom-call | flops 5000000 | bytes 1000 | tf_op jit(solution)/shard_map/pallas_call | solution.py:90
  25.8 4.4 %collective-permute-start = (bf16[1024,512]{1,0:T(8,128)(2,1)}, bf16[1024,512]{1,0:T(8,128)(2,1)}, u32[]{:S(2)}, u32[]{:S(2)}) collective-permute-start(bf16[1024,512]{1,0:T(8,128)(2,1)} %get-tuple-element.102.kv), channel_id=1, source_target_pairs={{0,4},{4,8},{8,12},{12,16},{16,20},{20,24},{24,28},{1,5},{5,9},{9,... | collective-permute-start | bytes 3145736 | tf_op jit(solution)/shard_map/ppermute | solution.py:48
  39.3 4.6 %convolution_convert_fusion.dh_a.dh_b = bf16[1024,1024]{1,0:T(8,128)(2,1)S(1)} fusion(bf16[1024,1024]{1,0:T(8,128)(2,1)} %og.1, bf16[1024,1024]{1,0:T(8,128)(2,1)} %shrink.3), kind=kOutput, calls=%fused_computation.7 | convolution fusion | flops 2148532224 | bytes 6291456 | tf_op jit(solution)/shard_map/dot_general | solution.py:22
  43.9 13.2 %shard_map.351 = (f32[4,4,64,256]{3,2,1,0:T(8,128)S(1)}, f32[4,4,256]{2,1,0:T(4,128)S(1)}, f32[4,4,256]{2,1,0:T(4,128)S(1)}) custom-call(s32[12]{0:T(128)S(1)} %copy-done.64, bf16[1024,256]{1,0:T(8,128)(2,1)S(1)} %get-tuple-element.106.q, bf16[1024,512]{1,0:T(8,128)(2,1)} %get-tuple-element.102.kv, s32[1,1024]{1,0:T(1,128)S(1)} %copy-done.67), custom_call_target="tpu_custom_call" | custom-call | flops 12000000 | bytes 1000 | tf_op jit(solution)/shard_map/pallas_call | solution.py:90
  62.4 6.5 %collective-permute-done.4.refs_6_ = bf16[384,512]{1,0:T(8,128)(2,1)} collective-permute-done((bf16[384,512]{1,0:T(8,128)(2,1)S(1)}, bf16[384,512]{1,0:T(8,128)(2,1)}, u32[]{:S(2)}, u32[]{:S(2)}) %collective-permute-start.4) | collective-permute-done | bytes 393248 | tf_op jit(solution)/shard_map/ppermute | solution.py:39
  73.9 8.3 %all-to-all-done.low = bf16[4,256,256]{2,1,0:T(8,128)(2,1)S(1)} async-done(((bf16[4,256,256]{2,1,0:T(8,128)(2,1)}), bf16[4,256,256]{2,1,0:T(8,128)(2,1)S(1)}, u32[]{:S(2)}, u32[]{:S(2)}) %all-to-all-start) | async-done | bytes 524320 | tf_op jit(solution)/shard_map/all_to_all | solution.py:788
  83.6 10.8 %shard_map.353 = (f32[256,1024]{1,0:T(8,128)S(1)}, bf16[256,1024]{1,0:T(8,128)(2,1)S(1)}, bf16[256,1024]{1,0:T(8,128)(2,1)S(1)}, f32[16,256]{1,0:T(8,128)S(1)}, ...) custom-call(s32[12]{0:T(128)S(1)} %copy-done.64, bf16[1024,1024]{1,0:T(8,128)(2,1)} %tok.5, ...), custom_call_target="tpu_custom_call" | custom-call | flops 11000000 | bytes 1000 | tf_op jit(solution)/shard_map/pallas_call | solution.py:90
  97.0 12.0 %shard_map.354 = (bf16[256,1024]{1,0:T(8,128)(2,1)S(1)}, bf16[256,1024]{1,0:T(8,128)(2,1)S(1)}, bf16[256,1024]{1,0:T(8,128)(2,1)S(1)}, bf16[256,1024]{1,0:T(8,12...) custom-call(s32[12]{0:T(128)S(1)} %copy-done.64, ...), custom_call_target="tpu_custom_call" | custom-call | flops 12000000 | bytes 1000 | tf_op jit(solution)/shard_map/pallas_call | solution.py:90
  112.6 11.8 %shard_map.355 = (bf16[256,1024]{1,0:T(8,128)(2,1)S(1)}, bf16[256,1024]{1,0:T(8,128)(2,1)S(1)}, bf16[256,1024]{1,0:T(8,128)(2,1)S(1)}, bf16[256,1024]{1,0:T(8,12...) custom-call(s32[12]{0:T(128)S(1)} %copy-done.64, ...), custom_call_target="tpu_custom_call" | custom-call | flops 12000000 | bytes 1000 | tf_op jit(solution)/shard_map/pallas_call | solution.py:90
  127.9 9.3 %shard_map.356 = bf16[1024,2048]{1,0:T(8,128)(2,1)S(1)} custom-call(s32[12]{0:T(128)S(1)} %copy-done.64, bf16[256,1024]{1,0:T(8,128)(2,1)S(1)} %get-tuple-element.119.h_a.refs_0_, bf16[256,1024]{1,0:T(8,128)(2,1)S(1)} %collective-permute-done.8.h_b.refs_1_, bf16[256,1024]{1,0:T(8,128)(2,1)S(1)} %collective-permute-done.10.h_a.refs_2_, ...), custom_call_target="tpu_custom_call" | custom-call | flops 9000000 | bytes 1000 | tf_op jit(solution)/shard_map/pallas_call | solution.py:90
  142.6 14.7 %shard_map.357 = (bf16[256,1024]{1,0:T(8,128)(2,1)S(1)}, bf16[256,1024]{1,0:T(8,128)(2,1)S(1)}, bf16[256,1024]{1,0:T(8,128)(2,1)S(1)}, f32[256,1024]{1,0:T(8,128...) custom-call(s32[12]{0:T(128)S(1)} %copy-done.64, ...), custom_call_target="tpu_custom_call" | custom-call | flops 15000000 | bytes 1000 | tf_op jit(solution)/shard_map/pallas_call | solution.py:90
  192.8 7.2 %collective-permute-start.31 = (bf16[4,128,512]{2,1,0:T(8,128)(2,1)}, bf16[4,128,512]{2,1,0:T(8,128)(2,1)S(1)}, u32[]{:S(2)}, u32[]{:S(2)}) collective-permute-start(bf16[4,128,512]{2,1,0:T(8,128)(2,1)} %dynamic-slice_bitcast_fusion.1), channel_id=1, source_target_pairs={{0,4},{4,0},{1,5},{5,1},{2,6},{6,2},{3,7},{7,3},{8,12},{12,8},{9,1... | collective-permute-start | bytes 1572872 | tf_op jit(solution)/shard_map/ppermute | solution.py:52
  201.3 36.4 %collective-permute-done.31 = bf16[4,128,512]{2,1,0:T(8,128)(2,1)S(1)} collective-permute-done((bf16[4,128,512]{2,1,0:T(8,128)(2,1)}, bf16[4,128,512]{2,1,0:T(8,128)(2,1)S(1)}, u32[]{:S(2)}, u32[]{:S(2)}) %collective-permute-start.31) | collective-permute-done | bytes 524320 | tf_op jit(solution)/shard_map/ppermute | solution.py:52
  239.7 5.6 %all-to-all-start.2 = ((bf16[4,128,512]{2,1,0:T(8,128)(2,1)}), bf16[4,128,512]{2,1,0:T(8,128)(2,1)}, u32[]{:S(2)}, u32[]{:S(2)}) async-start(bf16[4,128,512]{2,1,0:T(8,128)(2,1)} %fusion.7), calls=%async_computation.2 | async-start | bytes 1048576 | tf_op jit(solution)/shard_map/all_to_all | solution.py:62
  246.7 15.8 %shard_map.361 = (f32[1024,512]{1,0:T(8,128)S(1)}, bf16[1024,256]{1,0:T(8,128)(2,1)S(1)}) custom-call(s32[12]{0:T(128)S(1)} %copy-done.64, bf16[1024,256]{1,0:T(8,128)(2,1)S(1)} %get-tuple-element.106.q, bf16[1024,512]{1,0:T(8,128)(2,1)} %get-tuple-element.102.kv, s32[1,1024]{1,0:T(1,128)S(1)} %copy-done.67, bf16[4,256,256]{2,1,0:T(8,128)(2,1)S(1)} %all-to-all-done.1.grad, ...), custom_call_target="tpu_custom_call" | custom-call | flops 14000000 | bytes 1000 | tf_op jit(solution)/shard_map/pallas_call | solution.py:90
  262.6 4.7 %shard_map.362 = (bf16[1024,512]{1,0:T(8,128)(2,1)S(1)}, bf16[256,1024]{1,0:T(8,128)(2,1)S(1)}, bf16[256,1024]{1,0:T(8,128)(2,1)S(1)}, bf16[2,256,1024]{2,1,0:T(8,128)(2,1)}, f32[2,1024]{1,0:T(2,128)S(1)}) custom-call(s32[12]{0:T(128)S(1)} %copy-done.64, f32[1024,512]{1,0:T(8,128)S(1)} %get-tuple-element.162.dkv, ...), custom_call_target="tpu_custom_call" | custom-call | flops 3000000 | bytes 1000 | tf_op jit(solution)/shard_map/pallas_call | solution.py:90
  274.1 4.3 %all-to-all-start.3 = ((bf16[4,128,256]{2,1,0:T(8,128)(2,1)}), bf16[4,128,256]{2,1,0:T(8,128)(2,1)}, u32[]{:S(2)}, u32[]{:S(2)}) async-start(bf16[4,128,256]{2,1,0:T(8,128)(2,1)} %bitcast.132), calls=%async_computation.3 | async-start | bytes 524288 | tf_op jit(solution)/shard_map/all_to_all | solution.py:892
  287.6 8.5 %collective-permute-done.26.crossed = bf16[256,1024]{1,0:T(8,128)(2,1)S(1)} collective-permute-done((bf16[256,1024]{1,0:T(8,128)(2,1)}, bf16[256,1024]{1,0:T(8,128)(2,1)S(1)}, u32[]{:S(2)}, u32[]{:S(2)}) %collective-permute-start.26) | collective-permute-done | bytes 524320 | tf_op jit(solution)/shard_map/ppermute | solution.py:39
  296.9 5.1 %all-to-all-start.5 = ((f32[8,8,128]{2,1,0:T(8,128)}), f32[8,8,128]{2,1,0:T(8,128)S(1)}, u32[]{:S(2)}, u32[]{:S(2)}) async-start(f32[8,8,128]{2,1,0:T(8,128)} %maximum_bitcast_fusion), calls=%async_computation.5 | async-start | bytes 65536 | tf_op jit(solution)/shard_map/all_to_all | solution.py:929
  302.8 5.8 %all-to-all-done.5 = f32[8,8,128]{2,1,0:T(8,128)S(1)} async-done(((f32[8,8,128]{2,1,0:T(8,128)}), f32[8,8,128]{2,1,0:T(8,128)S(1)}, u32[]{:S(2)}, u32[]{:S(2)}) %all-to-all-start.5) | async-done | bytes 32800 | tf_op jit(solution)/shard_map/all_to_all | solution.py:929
  314.4 16.7 %collective-permute-done.35 = bf16[4,128,768]{2,1,0:T(8,128)(2,1)S(1)} collective-permute-done((bf16[4,128,768]{2,1,0:T(8,128)(2,1)S(1)}, bf16[4,128,768]{2,1,0:T(8,128)(2,1)S(1)}, u32[]{:S(2)}, u32[]{:S(2)}) %collective-permute-start.35) | collective-permute-done | bytes 786464 | tf_op jit(solution)/shard_map/ppermute | solution.py:52
  332.2 4.7 %all-to-all-start.6 = ((bf16[4,128,768]{2,1,0:T(8,128)(2,1)}), bf16[4,128,768]{2,1,0:T(8,128)(2,1)}, u32[]{:S(2)}, u32[]{:S(2)}) async-start(bf16[4,128,768]{2,1,0:T(8,128)(2,1)} %fusion.4), calls=%async_computation.6 | async-start | bytes 1572864 | tf_op jit(solution)/shard_map/all_to_all | solution.py:62
  353.2 9.8 %collective-permute-done.34 = f32[8,128]{1,0:T(8,128)S(1)} collective-permute-done((f32[8,128]{1,0:T(8,128)S(1)}, f32[8,128]{1,0:T(8,128)S(1)}, u32[]{:S(2)}, u32[]{:S(2)}) %collective-permute-start.34) | collective-permute-done | bytes 4128 | tf_op jit(solution)/shard_map/ppermute | solution.py:39
  370.7 5.1 %all-to-all-start.7 = ((bf16[4,128,768]{2,1,0:T(8,128)(2,1)}), bf16[4,128,768]{2,1,0:T(8,128)(2,1)}, u32[]{:S(2)}, u32[]{:S(2)}) async-start(bf16[4,128,768]{2,1,0:T(8,128)(2,1)} %fusion.3), calls=%async_computation.7 | async-start | bytes 1572864 | tf_op jit(solution)/shard_map/all_to_all | solution.py:62
  (314 shorter events, 162.7 us)
Async XLA Ops:
  22.9 46.1 %collective-permute-start.3 = (bf16[768,1024]{1,0:T(8,128)(2,1)}, bf16[768,1024]{1,0:T(8,128)(2,1)}, u32[]{:S(2)}, u32[]{:S(2)}) collective-permute-start(bf16[768,1024]{1,0:T(8,128)(2,1)} %get-tuple-element.104.refs_0_), channel_id=1, source_target_pairs={{0,2},{1,3},{2,0},{3,1},{4,6},{5,7},{6,4},{7,5},{8,10},{9,11},{10,... | collective-permute-start | bytes 4718600 | tf_op jit(solution)/shard_map/ppermute | solution.py:39
  25.8 31.3 %collective-permute-start = (bf16[1024,512]{1,0:T(8,128)(2,1)}, bf16[1024,512]{1,0:T(8,128)(2,1)}, u32[]{:S(2)}, u32[]{:S(2)}) collective-permute-start(bf16[1024,512]{1,0:T(8,128)(2,1)} %get-tuple-element.102.kv), channel_id=1, source_target_pairs={{0,4},{4,8},{8,12},{12,16},{16,20},{20,24},{24,28},{1,5},{5,9},{9,... | collective-permute-start | bytes 3145736 | tf_op jit(solution)/shard_map/ppermute | solution.py:48
  30.2 52.0 %collective-permute-start.2 = (bf16[768,1024]{1,0:T(8,128)(2,1)}, bf16[768,1024]{1,0:T(8,128)(2,1)}, u32[]{:S(2)}, u32[]{:S(2)}) collective-permute-start(bf16[768,1024]{1,0:T(8,128)(2,1)} %get-tuple-element.104.refs_0_), channel_id=1, source_target_pairs={{0,1},{1,0},{2,3},{3,2},{4,5},{5,4},{6,7},{7,6},{8,9},{9,8},{10,11... | collective-permute-start | bytes 4718600 | tf_op jit(solution)/shard_map/ppermute | solution.py:39
  30.2 26.9 %collective-permute-start.1 = (bf16[256,512]{1,0:T(8,128)(2,1)}, bf16[256,512]{1,0:T(8,128)(2,1)}, u32[]{:S(2)}, u32[]{:S(2)}) collective-permute-start(bf16[256,512]{1,0:T(8,128)(2,1)} %get-tuple-element.103), channel_id=1, source_target_pairs={{0,8},{4,12},{8,16},{12,20},{16,24},{20,28},{1,9},{5,13},{9,17},{1... | collective-permute-start | bytes 786440 | tf_op jit(solution)/shard_map/ppermute | solution.py:48
  38.7 30.2 %collective-permute-start.4 = (bf16[384,512]{1,0:T(8,128)(2,1)S(1)}, bf16[384,512]{1,0:T(8,128)(2,1)}, u32[]{:S(2)}, u32[]{:S(2)}) collective-permute-start(bf16[384,512]{1,0:T(8,128)(2,1)S(1)} %shard_map.350.refs_4_), channel_id=1, source_target_pairs={{0,2},{1,3},{2,0},{3,1},{4,6},{5,7},{6,4},{7,5},{8,10},{9,11},{10,... | collective-permute-start | bytes 1179656 | tf_op jit(solution)/shard_map/ppermute | solution.py:39
  95.1 15.5 %collective-permute-start.10 = (bf16[256,1024]{1,0:T(8,128)(2,1)S(1)}, bf16[256,1024]{1,0:T(8,128)(2,1)S(1)}, u32[]{:S(2)}, u32[]{:S(2)}) collective-permute-start(bf16[256,1024]{1,0:T(8,128)(2,1)S(1)} %get-tuple-element.119.h_a.refs_0_), channel_id=1, source_target_pairs={{0,2},{1,3},{2,0},{3,1},{4,6},{5,7},{6,4},{7,5},{8,10},{9,11},{10,... | collective-permute-start | bytes 1572872 | tf_op jit(solution)/shard_map/ppermute | solution.py:39
  161.0 16.5 %all-to-all-start.1 = ((bf16[4,256,256]{2,1,0:T(8,128)(2,1)}), bf16[4,256,256]{2,1,0:T(8,128)(2,1)S(1)}, u32[]{:S(2)}, u32[]{:S(2)}) async-start(bf16[4,256,256]{2,1,0:T(8,128)(2,1)} %get-tuple-element.152), calls=%async_computation.1 | async-start | bytes 1048576 | tf_op jit(solution)/shard_map/all_to_all | solution.py:834
  164.6 235.2 %reduce-scatter.2.cloned.1.call-start = ((), (), s32[]{:S(2)}) async-start(), calls=%async_computation.9 | async-start | bytes 4718592 | tf_op jit(solution)/shard_map/reduce_scatter | solution.py:819
  179.5 101.9 %collective-permute-start.17 = (bf16[2,1024,768]{2,1,0:T(8,128)(2,1)}, bf16[2,1024,768]{2,1,0:T(8,128)(2,1)}, u32[]{:S(2)}, u32[]{:S(2)}) collective-permute-start(bf16[2,1024,768]{2,1,0:T(8,128)(2,1)} %copy-done.80), channel_id=1, source_target_pairs={{0,1},{1,0},{2,3},{3,2},{4,5},{5,4},{6,7},{7,6},{8,9},{9,8},{10,11... | collective-permute-start | bytes 9437192 | tf_op jit(solution)/shard_map/ppermute | solution.py:39
  188.0 74.5 %collective-permute-start.23 = (bf16[1024,512]{1,0:T(8,128)(2,1)}, bf16[1024,512]{1,0:T(8,128)(2,1)}, u32[]{:S(2)}, u32[]{:S(2)}) collective-permute-start(bf16[1024,512]{1,0:T(8,128)(2,1)} %get-tuple-element.163), channel_id=1, source_target_pairs={{4,0},{8,4},{12,8},{16,12},{20,16},{24,20},{28,24},{5,1},{9,5},{13... | collective-permute-start | bytes 3145736 | tf_op jit(solution)/shard_map/ppermute | solution.py:48
  192.8 44.9 %collective-permute-start.31 = (bf16[4,128,512]{2,1,0:T(8,128)(2,1)}, bf16[4,128,512]{2,1,0:T(8,128)(2,1)S(1)}, u32[]{:S(2)}, u32[]{:S(2)}) collective-permute-start(bf16[4,128,512]{2,1,0:T(8,128)(2,1)} %dynamic-slice_bitcast_fusion.1), channel_id=1, source_target_pairs={{0,4},{4,0},{1,5},{5,1},{2,6},{6,2},{3,7},{7,3},{8,12},{12,8},{9,1... | collective-permute-start | bytes 1572872 | tf_op jit(solution)/shard_map/ppermute | solution.py:52
  200.0 62.5 %collective-permute-start.24 = (bf16[256,512]{1,0:T(8,128)(2,1)S(1)}, bf16[256,512]{1,0:T(8,128)(2,1)S(1)}, u32[]{:S(2)}, u32[]{:S(2)}) collective-permute-start(bf16[256,512]{1,0:T(8,128)(2,1)S(1)} %get-tuple-element.164), channel_id=1, source_target_pairs={{8,0},{12,4},{16,8},{20,12},{24,16},{28,20},{9,1},{13,5},{17,9},{2... | collective-permute-start | bytes 786440 | tf_op jit(solution)/shard_map/ppermute | solution.py:48
  239.7 31.8 %all-to-all-start.2 = ((bf16[4,128,512]{2,1,0:T(8,128)(2,1)}), bf16[4,128,512]{2,1,0:T(8,128)(2,1)}, u32[]{:S(2)}, u32[]{:S(2)}) async-start(bf16[4,128,512]{2,1,0:T(8,128)(2,1)} %fusion.7), calls=%async_computation.2 | async-start | bytes 1048576 | tf_op jit(solution)/shard_map/all_to_all | solution.py:62
  279.4 16.7 %collective-permute-start.26 = (bf16[256,1024]{1,0:T(8,128)(2,1)}, bf16[256,1024]{1,0:T(8,128)(2,1)S(1)}, u32[]{:S(2)}, u32[]{:S(2)}) collective-permute-start(bf16[256,1024]{1,0:T(8,128)(2,1)} %fusion.8), channel_id=1, source_target_pairs={{0,2},{1,3},{2,0},{3,1},{4,6},{5,7},{6,4},{7,5},{8,10},{9,11},{10,... | collective-permute-start | bytes 1572872 | tf_op jit(solution)/shard_map/ppermute | solution.py:39
  284.5 52.7 %collective-permute-start.19 = (bf16[1024,768]{1,0:T(8,128)(2,1)}, bf16[1024,768]{1,0:T(8,128)(2,1)}, u32[]{:S(2)}, u32[]{:S(2)}) collective-permute-start(bf16[1024,768]{1,0:T(8,128)(2,1)} %fusion), channel_id=1, source_target_pairs={{0,2},{1,3},{2,0},{3,1},{4,6},{5,7},{6,4},{7,5},{8,10},{9,11},{10,... | collective-permute-start | bytes 4718600 | tf_op jit(solution)/shard_map/ppermute | solution.py:39
  309.6 22.6 %all-to-all-start.4 = ((bf16[4,128,768]{2,1,0:T(8,128)(2,1)}), bf16[4,128,768]{2,1,0:T(8,128)(2,1)}, u32[]{:S(2)}, u32[]{:S(2)}) async-start(bf16[4,128,768]{2,1,0:T(8,128)(2,1)} %broadcast_in_dim.13), calls=%async_computation.4 | async-start | bytes 1572864 | tf_op jit(solution)/shard_map/all_to_all | solution.py:67
  313.9 17.2 %collective-permute-start.35 = (bf16[4,128,768]{2,1,0:T(8,128)(2,1)S(1)}, bf16[4,128,768]{2,1,0:T(8,128)(2,1)S(1)}, u32[]{:S(2)}, u32[]{:S(2)}) collective-permute-start(bf16[4,128,768]{2,1,0:T(8,128)(2,1)S(1)} %fusion.10), channel_id=1, source_target_pairs={{0,4},{4,0},{1,5},{5,1},{2,6},{6,2},{3,7},{7,3},{8,12},{12,8},{9,1... | collective-permute-start | bytes 2359304 | tf_op jit(solution)/shard_map/ppermute | solution.py:52
  332.2 33.0 %all-to-all-start.6 = ((bf16[4,128,768]{2,1,0:T(8,128)(2,1)}), bf16[4,128,768]{2,1,0:T(8,128)(2,1)}, u32[]{:S(2)}, u32[]{:S(2)}) async-start(bf16[4,128,768]{2,1,0:T(8,128)(2,1)} %fusion.4), calls=%async_computation.6 | async-start | bytes 1572864 | tf_op jit(solution)/shard_map/all_to_all | solution.py:62
  342.4 25.8 %collective-permute-start.36 = (bf16[4,128,768]{2,1,0:T(8,128)(2,1)}, bf16[4,128,768]{2,1,0:T(8,128)(2,1)}, u32[]{:S(2)}, u32[]{:S(2)}) collective-permute-start(bf16[4,128,768]{2,1,0:T(8,128)(2,1)} %dynamic-slice_bitcast_fusion), channel_id=1, source_target_pairs={{0,4},{4,0},{1,5},{5,1},{2,6},{6,2},{3,7},{7,3},{8,12},{12,8},{9,1... | collective-permute-start | bytes 2359304 | tf_op jit(solution)/shard_map/ppermute | solution.py:52
  348.4 16.7 %collective-permute-start.28 = (bf16[256,1024]{1,0:T(8,128)(2,1)}, bf16[256,1024]{1,0:T(8,128)(2,1)S(1)}, u32[]{:S(2)}, u32[]{:S(2)}) collective-permute-start(bf16[256,1024]{1,0:T(8,128)(2,1)} %shard_map.363.refs_0_), channel_id=1, source_target_pairs={{0,2},{1,3},{2,0},{3,1},{4,6},{5,7},{6,4},{7,5},{8,10},{9,11},{10,... | collective-permute-start | bytes 1572872 | tf_op jit(solution)/shard_map/ppermute | solution.py:39
  353.1 23.4 %collective-permute-start.27 = (bf16[256,1024]{1,0:T(8,128)(2,1)}, bf16[256,1024]{1,0:T(8,128)(2,1)S(1)}, u32[]{:S(2)}, u32[]{:S(2)}) collective-permute-start(bf16[256,1024]{1,0:T(8,128)(2,1)} %shard_map.363.refs_0_), channel_id=1, source_target_pairs={{0,1},{1,0},{2,3},{3,2},{4,5},{5,4},{6,7},{7,6},{8,9},{9,8},{10,11... | collective-permute-start | bytes 1572872 | tf_op jit(solution)/shard_map/ppermute | solution.py:39
  363.0 19.5 %collective-permute-start.32 = (bf16[4,128,768]{2,1,0:T(8,128)(2,1)}, bf16[4,128,768]{2,1,0:T(8,128)(2,1)}, u32[]{:S(2)}, u32[]{:S(2)}) collective-permute-start(bf16[4,128,768]{2,1,0:T(8,128)(2,1)} %all-to-all-done.4), channel_id=1, source_target_pairs={{0,4},{4,0},{1,5},{5,1},{2,6},{6,2},{3,7},{7,3},{8,12},{12,8},{9,1... | collective-permute-start | bytes 2359304 | tf_op jit(solution)/shard_map/ppermute | solution.py:52
  366.5 18.8 %collective-permute-start.21 = (bf16[256,1024]{1,0:T(8,128)(2,1)S(1)}, bf16[256,1024]{1,0:T(8,128)(2,1)S(1)}, u32[]{:S(2)}, u32[]{:S(2)}) collective-permute-start(bf16[256,1024]{1,0:T(8,128)(2,1)S(1)} %add_convert_fusion.refs_0_), channel_id=1, source_target_pairs={{0,2},{1,3},{2,0},{3,1},{4,6},{5,7},{6,4},{7,5},{8,10},{9,11},{10,... | collective-permute-start | bytes 1572872 | tf_op jit(solution)/shard_map/ppermute | solution.py:39
  370.7 25.7 %all-to-all-start.7 = ((bf16[4,128,768]{2,1,0:T(8,128)(2,1)}), bf16[4,128,768]{2,1,0:T(8,128)(2,1)}, u32[]{:S(2)}, u32[]{:S(2)}) async-start(bf16[4,128,768]{2,1,0:T(8,128)(2,1)} %fusion.3), calls=%async_computation.7 | async-start | bytes 1572864 | tf_op jit(solution)/shard_map/all_to_all | solution.py:62
  (109 other events, 773.8 us)
Sparse Core Ops, SparseCore 0:
  182.2 113.5 reduce-scatter.1

commit v3 on v2

--- a/solution.py
+++ b/solution.py
@@ -48,27 +48,73 @@
     return lax.ppermute(value, SEQ, [(source, source + steps) for source in range(leading, last)])
 
 
-def other_near(value):
-    return lax.ppermute(value, "near", [(0, 1), (1, 0)])
-
-
-def over_shards(blocks):
-    far = lax.axis_size("far")
-    parts = blocks.reshape(far, 2, -1, blocks.shape[-1])
-    own = lax.axis_index("near")
-    sent = other_near(lax.dynamic_index_in_dim(parts, 1 - own, 1, keepdims=False))
-    kept = lax.dynamic_index_in_dim(parts, own, 1, keepdims=False)
-    half = (kept.astype(F32) + sent.astype(F32)).astype(BF)
-    return sum_rows(lax.all_to_all(half, "far", 0, 0))
-
-
-def from_shards(own):
-    far = lax.axis_size("far")
-    mine = lax.all_to_all(jnp.broadcast_to(own[None], (far, *own.shape)), "far", 0, 0)
-    other = other_near(mine)
-    first = lax.axis_index("near") == 0
-    both = jnp.stack([jnp.where(first, mine, other), jnp.where(first, other, mine)], axis=1)
-    return both.reshape(-1, own.shape[-1])
+def shard_bits():
+    return (lax.axis_size("far") * lax.axis_size("near")).bit_length() - 1
+
+
+def across_bit(value, bit):
+    return lax.ppermute(value, SEQ, [(shard, shard ^ (1 << bit)) for shard in range(1 << shard_bits())])
+
+
+def own_bit(bit):
+    return lax.axis_index(SEQ) // (1 << bit) % 2
+
+
+def step_kernel(bit, ids, kept, sent, kept_o, send_o):
+    own = lax.shift_right_logical(ids[0], bit) % 2
+    kept_o[0] = (kept[own].astype(F32) + sent[own].astype(F32)).astype(BF)
+    send_o[0] = (kept[1 - own].astype(F32) + sent[1 - own].astype(F32)).astype(BF)
+
+
+class ShardSum:
+    def __init__(self, kept, send):
+        self.left = list(range(1, shard_bits()))
+        self.kept, self.sent = kept, across_bit(send, 0)
+
+    def step(self, ids, *others):
+        blocks, part, columns = self.kept.shape
+        half = pl.BlockSpec((1, part, columns), lambda j, s: (j, 0, 0))
+        self.kept, send = run(
+            functools.partial(step_kernel, self.left[0]),
+            ids,
+            (self.kept, after(self.sent, *others)),
+            [shaped((blocks // 2, part, columns), BF)] * 2,
+            grid=(blocks // 2,),
+            in_specs=[pl.BlockSpec((2, part, columns), lambda j, s: (j, 0, 0))] * 2,
+            out_specs=[half, half],
+            micros=2,
+        )
+        self.sent = across_bit(send, self.left[0])
+        self.left = self.left[1:]
+
+    def last(self, ids, *others):
+        while self.left:
+            self.step(ids, *others)
+        rows = lambda value: value.reshape(-1, value.shape[-1])
+        return rows(self.kept), rows(after(self.sent, *others))
+
+
+def double(value, have, bit):
+    other = across_bit(value, bit)
+    dim = sorted([*have, bit], reverse=True).index(bit)
+    low = own_bit(bit) == 0
+    return jnp.stack([jnp.where(low, value, other), jnp.where(low, other, value)], axis=dim)
+
+
+def to_all(own):
+    have = []
+    value = own
+    for bit in reversed(range(shard_bits())):
+        value = double(value, have, bit)
+        have.append(bit)
+    return value.reshape(-1, own.shape[-1])
+
+
+def added(*terms):
+    total = terms[0].astype(F32)
+    for term in terms[1:]:
+        total = total + term.astype(F32)
+    return total.astype(BF)
 
 
 def whole(array):
@@ -85,7 +131,6 @@
     out_specs = out_specs or [None] * len(outs)
     in_specs = [whole(a) if s is None else s for a, s in zip(args, in_specs)]
     out_specs = [whole(a) if s is None else s for a, s in zip(outs, out_specs)]
-    moved = sum(a.size * a.dtype.itemsize for a in list(args) + list(outs))
     prefetch = () if ids is None else (ids,)
     return pl.pallas_call(
         functools.partial(kernel, None) if ids is None else kernel,
@@ -98,7 +143,7 @@
             scratch_shapes=list(scratch),
         ),
         compiler_params=pltpu.CompilerParams(vmem_limit_bytes=vmem * MIB),
-        cost_estimate=pl.CostEstimate(flops=int(micros * 1e6), transcendentals=0, bytes_accessed=1000),
+        cost_estimate=pl.CostEstimate(flops=int(micros * 0.5e9), transcendentals=0, bytes_accessed=1000),
     )(*prefetch, *args)
 
 
@@ -133,9 +178,10 @@
     items = lens.shape[0]
     offset = place[0] * rows
     own_first = offset + place[1] * (rows // 4)
-    positions = offset + lax.broadcasted_iota(jnp.int32, (1, rows), 1)
-    found = jnp.zeros((1, rows), jnp.int32)
-    lows = [jnp.int32(0)] * (rows // BLOCK)
+    reach = begin.shape[1]
+    positions = offset + lax.broadcasted_iota(jnp.int32, (1, reach), 1)
+    found = jnp.zeros((1, reach), jnp.int32)
+    lows = [jnp.int32(0)] * (reach // BLOCK)
     begun = base = own_base = jnp.int32(0)
     for item in range(items):
         found = jnp.where(positions >= begun, begun, found)
@@ -143,7 +189,8 @@
         begun = begun + lens[item]
         base = base + jnp.where(begun <= offset, 1, 0)
         own_base = own_base + jnp.where(begun <= own_first, 1, 0)
-    begin[...] = found - offset
+    begin[...] = jnp.where(positions >= begun, begun, found) - offset
+    lows = [jnp.where(offset + block * BLOCK >= begun, begun, low) for block, low in enumerate(lows)]
     base = jnp.minimum(base, items - 3)
     own_base = jnp.minimum(own_base, items - 2)
     begun = bound = jnp.int32(0)
@@ -162,14 +209,15 @@
         ids[8 + block] = low - offset
 
 
-def entry_kernel(ids, tok, gain, bias, wq, wk, wv, merge, pq, pm, hid, q, kv, tail, pack):
+def pack_kernel(ids, merge, pq, pm, pack):
+    width = pq.shape[1]
+    pack[:width, :] = merge[...]
+    pack[width : 2 * width, :] = pq[...].T
+    pack[2 * width :, :] = pm[...]
+
+
+def entry_kernel(ids, tok, gain, bias, wq, wk, wv, hid, q, kv, tail):
     width = wq.shape[1]
-    for part, source in enumerate((merge, pq, pm)):
-
-        @pl.when(pl.program_id(0) == part)
-        def _():
-            pack[part * width : (part + 1) * width, :] = source[...].T if part == 1 else source[...]
-
     normed, _ = ln_rows(tok[...].astype(F32))
     hidden = (normed * gain[...] + bias[...]).astype(BF)
     hid[...] = hidden
@@ -235,7 +283,7 @@
     total_o[0] = total[...]
 
 
-def attend_remote_kernel(ids, q, kv, tail, begin, acc_i, top_i, total_i, out, low_out, lse, vt, acc, top, total):
+def attend_remote_kernel(ids, q, kv, tail, begin, acc_i, top_i, total_i, out, low_out, lse, ship_a, ship_b, ship0, vt, acc, top, total):
     step = pl.program_id(0)
     width = q.shape[1]
     heads = width // HD
@@ -266,29 +314,60 @@
         row = pl.multiple_of((b - 1) * BLOCK, BLOCK)
         attend_block(kv[pl.ds(row, BLOCK), :width], vt[b], queries, bias_of(b), top, total, acc)
 
-    lse[0] = top[...] + jnp.log(total[...])
+    sums = top[...] + jnp.log(total[...])
+    lse[0] = sums
+    high = sums.astype(BF).astype(F32)
+    both = jnp.concatenate([high, sums - high], axis=1)
     stacked = jnp.concatenate([acc[h] * (1.0 / total[h : h + 1, :]) for h in range(heads)], axis=0)
     rows = stacked.T
     out[0] = rows
     low_out[0] = rows.astype(BF)
-
-
-def back_block(keys, values, keys_t, queries, grads, bias, lse, delta, dq):
+    half = pl.num_programs(0) // 2
+
+    def put(ship):
+        ship[:BLOCK, :width] = q[...]
+        ship[:BLOCK, width:] = rows.astype(BF)
+        ship[BLOCK:, :] = jnp.concatenate([both, jnp.zeros((16 - heads, 2 * BLOCK), F32)], axis=0).astype(BF)
+
+    @pl.when(step < half)
+    def _():
+        put(ship_a.at[0])
+
+    @pl.when(step >= half)
+    def _():
+        put(ship_b.at[0])
+
+    @pl.when(step == 0)
+    def _():
+        ship0[0] = ship_a[0]
+
+
+def back_block(keys, values, keys_t, queries, grads, bias, lse, delta, dq, dkv):
+    width = keys.shape[1]
     key_sum = value_sum = None
     for head, (query, grad) in enumerate(zip(queries, grads)):
         row = slice(head, head + 1)
         probs = jnp.exp(nt(keys, query) + bias - lse[row, :])
         score_grad = (probs * (nt(values, grad) - delta[row, :])).astype(BF)
-        low_probs = probs.astype(BF)
-        key_term = nn(score_grad, query)
-        value_term = nn(low_probs, grad)
-        key_sum = key_term if key_sum is None else key_sum + key_term
-        value_sum = value_term if value_sum is None else value_sum + value_term
-        dq[head] += nn(keys_t[head * HD : (head + 1) * HD, :], score_grad)
-    return key_sum, value_sum
-
-
-def back_remote_kernel(ids, q, kv, tail, begin, grad, out, lse, dkv_o, dtail_o, dq_o, delta_o, kt, dkv, dq):
+        if dkv is not None:
+            key_term = nn(score_grad, query)
+            value_term = nn(probs.astype(BF), grad)
+            key_sum = key_term if key_sum is None else key_sum + key_term
+            value_sum = value_term if value_sum is None else value_sum + value_term
+        if dq is not None:
+            dq[head] += nn(keys_t[head * HD : (head + 1) * HD, :], score_grad)
+    if dkv is not None:
+        dkv[:, :width] += key_sum
+        dkv[:, width:] += value_sum
+
+
+def put_delta(delta, grad, out):
+    products = (grad.astype(F32) * out.astype(F32)).T
+    for head in range(delta.shape[0]):
+        delta[head : head + 1, :] = jnp.sum(products[head * HD : (head + 1) * HD, :], axis=0, keepdims=True)
+
+
+def back_local_kernel(ids, q, kv, begin, grad, out, lse, dkv_o, dq_o, delta_o, kt, dkv):
     step = pl.program_id(0)
     width = q.shape[1]
     heads = width // HD
@@ -297,61 +376,11 @@
     @pl.when(step == 0)
     def _():
         dkv[...] = jnp.zeros_like(dkv)
-        kt[0] = tail[:, :width].T
-        for b in range(blocks):
-            kt[b + 1] = kv[b * BLOCK : (b + 1) * BLOCK, :width].T
-
-    products = (grad[0].astype(F32) * out[0]).T
-    for head in range(heads):
-        delta_o[0, head : head + 1, :] = jnp.sum(products[head * HD : (head + 1) * HD, :], axis=0, keepdims=True)
-    dq[...] = jnp.zeros_like(dq)
-    span = (blocks + 1) * BLOCK
-    low = lax.shift_right_logical(jnp.maximum(ids[8 + step] + span, 0), 8)
-
-    @pl.when(low <= blocks)
-    def _():
-        queries = by_head(q[...], heads)
-        grads = by_head(grad[0], heads)
-
-        def one(b, pair):
-            bias = window_bias(b * BLOCK - span, step * BLOCK, begin[...])
-            key_sum, value_sum = back_block(
-                pair[:, :width], pair[:, width:], kt[b], queries, grads, bias, lse.at[0], delta_o.at[0], dq
-            )
-            dkv[b, :, :width] += key_sum
-            dkv[b, :, width:] += value_sum
-
-        @pl.when(low == 0)
-        def _():
-            one(0, tail[...])
-
-        @pl.loop(jnp.maximum(low, 1), blocks + 1)
-        def _(b):
-            row = pl.multiple_of((b - 1) * BLOCK, BLOCK)
-            one(b, kv[pl.ds(row, BLOCK), :])
-
-    dq_o[0] = dq[...]
-
-    @pl.when(step == pl.num_programs(0) - 1)
-    def _():
-        dtail_o[...] = dkv[0].astype(BF)
-        for b in range(blocks):
-            dkv_o[b * BLOCK : (b + 1) * BLOCK, :] = dkv[b + 1].astype(BF)
-
-
-def back_local_kernel(ids, q, kv, begin, grad, lse, delta, dq_i, dkv_o, dq_o, kt, dkv, dq):
-    step = pl.program_id(0)
-    width = q.shape[1]
-    heads = width // HD
-    blocks = kv.shape[0] // BLOCK
-
-    @pl.when(step == 0)
-    def _():
-        dkv[...] = jnp.zeros_like(dkv)
         for b in range(blocks):
             kt[b] = kv[b * BLOCK : (b + 1) * BLOCK, :width].T
 
-    dq[...] = dq_i[0]
+    put_delta(delta_o.at[0], grad[0], out[0])
+    dq_o[...] = jnp.zeros_like(dq_o)
     queries = by_head(q[...], heads)
     grads = by_head(grad[0], heads)
     low = lax.shift_right_logical(jnp.maximum(ids[8 + step], 0), 8)
@@ -361,19 +390,96 @@
         row = pl.multiple_of(b * BLOCK, BLOCK)
         pair = kv[pl.ds(row, BLOCK), :]
         bias = window_bias(row, step * BLOCK, begin[...])
-        key_sum, value_sum = back_block(
-            pair[:, :width], pair[:, width:], kt[b], queries, grads, bias, lse.at[0], delta.at[0], dq
+        back_block(
+            pair[:, :width], pair[:, width:], kt[b], queries, grads, bias, lse.at[0], delta_o.at[0], dq_o.at[0], dkv.at[b]
         )
-        dkv[b, :, :width] += key_sum
-        dkv[b, :, width:] += value_sum
+
+    @pl.when(step == pl.num_programs(0) - 1)
+    def _():
+        for b in range(blocks):
+            dkv_o[b * BLOCK : (b + 1) * BLOCK, :] = dkv[b]
+
+
+def back_query_kernel(ids, q, kv, tail, begin, grad, lse, delta, dq_i, dq_o, kt, dq):
+    step = pl.program_id(0)
+    width = q.shape[1]
+    heads = width // HD
+    blocks = kv.shape[0] // BLOCK
+
+    @pl.when(step == 0)
+    def _():
+        kt[0] = tail[:, :width].T
+        for b in range(blocks):
+            kt[b + 1] = kv[b * BLOCK : (b + 1) * BLOCK, :width].T
+
+    dq[...] = dq_i[0]
+    span = (blocks + 1) * BLOCK
+    low = lax.shift_right_logical(jnp.maximum(ids[8 + step] + span, 0), 8)
+
+    @pl.when(low <= blocks)
+    def _():
+        queries = by_head(q[...], heads)
+        grads = by_head(grad[0], heads)
+
+        def one(b, pair):
+            bias = window_bias(b * BLOCK - span, step * BLOCK, begin[...])
+            back_block(pair[:, :width], pair[:, width:], kt[b], queries, grads, bias, lse.at[0], delta.at[0], dq, None)
+
+        @pl.when(low == 0)
+        def _():
+            one(0, tail[...])
+
+        @pl.loop(jnp.maximum(low, 1), blocks + 1)
+        def _(b):
+            row = pl.multiple_of((b - 1) * BLOCK, BLOCK)
+            one(b, kv[pl.ds(row, BLOCK), :])
 
     stacked = jnp.concatenate([dq[h] for h in range(heads)], axis=0)
     dq_o[...] = (stacked.T * SCALE).astype(BF)
 
-    @pl.when(step == pl.num_programs(0) - 1)
+
+def back_key_kernel(ids, kv, begin, ship_low, ship_high, grad_n, ship_f, grad_f, dkv_i, dkv_o, delta, lse, dkv):
+    step = pl.program_id(0)
+    width = kv.shape[1] // 2
+    heads = width // HD
+    blocks = kv.shape[0] // BLOCK
+
+    @pl.when(step == 0)
     def _():
         for b in range(blocks):
-            dkv_o[b * BLOCK : (b + 1) * BLOCK, :] = dkv[b]
+            dkv[b] = dkv_i[b * BLOCK : (b + 1) * BLOCK, :]
+
+    low = lax.shift_right_logical(jnp.maximum(ids[8 + blocks + step], 0), 8)
+
+    def all_keys(ship, grad):
+        put_delta(delta, grad, ship[:BLOCK, width:])
+        parts = ship[BLOCK:, :].astype(F32)
+        lse[...] = parts[:heads, :BLOCK] + parts[:heads, BLOCK:]
+        queries, grads = by_head(ship[:BLOCK, :width], heads), by_head(grad, heads)
+
+        @pl.loop(low, blocks)
+        def _(b):
+            row = pl.multiple_of(b * BLOCK, BLOCK)
+            pair = kv[pl.ds(row, BLOCK), :]
+            bias = window_bias(row, blocks * BLOCK + step * BLOCK, begin[...])
+            back_block(pair[:, :width], pair[:, width:], None, queries, grads, bias, lse, delta, None, dkv.at[b])
+
+    @pl.when((low < blocks) & (step < blocks // 2))
+    def _():
+        all_keys(ship_low.at[0], grad_n[0])
+
+    @pl.when((low < blocks) & (step >= blocks // 2) & (step < blocks))
+    def _():
+        all_keys(ship_high.at[0], grad_n[0])
+
+    @pl.when((low < blocks) & (step == blocks))
+    def _():
+        all_keys(ship_f.at[0], grad_f[0])
+
+    @pl.when(step == blocks)
+    def _():
+        for b in range(blocks):
+            dkv_o[b * BLOCK : (b + 1) * BLOCK, :] = dkv[b].astype(BF)
 
 
 def cross_bias(ids, prompt_rows, rows):
@@ -549,6 +655,14 @@
     )
 
 
+def spread(ids, rows, kept, send):
+    far, part, _ = kept.shape
+    own = ids[0] % 2
+    for block in range(far):
+        kept[block] = rows[pl.ds(pl.multiple_of((2 * block + own) * part, part), part), :]
+        send[block] = rows[pl.ds(pl.multiple_of((2 * block + 1 - own) * part, part), part), :]
+
+
 def feed_weights_kernel(ids, *refs):
     threes, pres, lows = refs[:4], refs[4:8], refs[8:12]
     og, out, turned = refs[12:]
@@ -593,6 +707,7 @@
         out_specs=[pl.BlockSpec((model, chunk), lambda j, s: (0, j))],
         scratch=[pltpu.VMEM((model, 4 * rows), BF)],
         micros=9,
+        vmem=60,
     )[0]
 
 
@@ -607,20 +722,16 @@
         out[:, 2 * width :] = nn(slg_t, low[rank ^ d]).astype(BF)
 
 
-def key_sum_kernel(ids, dkv, near, far, hid, dq, wq, wk, wv, gain, bias, kvg_o, keep0, keep1, send, norms):
-    rows, width2 = dkv.shape
+def one_grad_kernel(ids, kvg, hid, dq, wq, wk, wv, gain, bias, keep0, keep1, send, norms):
+    rows, width2 = kvg.shape
     width = width2 // 2
     quarter = rows // 4
     rank = ids[1]
-    kvg_o[: rows - BLOCK, :] = (dkv[: rows - BLOCK, :] + near[: rows - BLOCK, :].astype(F32)).astype(BF)
-    kvg_o[rows - BLOCK :, :] = (
-        dkv[rows - BLOCK :, :] + near[rows - BLOCK :, :].astype(F32) + far[...].astype(F32)
-    ).astype(BF)
     product = total = None
     for d in (1, 3, 2, 0):
         own = pl.ds(pl.multiple_of((rank ^ d) * quarter, quarter), quarter)
         part = (
-            nt(dq[own, :], wq[...]) + nt(kvg_o[own, :width], wk[...]) + nt(kvg_o[own, width:], wv[...])
+            nt(dq[own, :], wq[...]) + nt(kvg[own, :width], wk[...]) + nt(kvg[own, width:], wv[...])
         )
         hidden = hid[own, :].astype(F32)
         term = jnp.sum(part * hidden, axis=0, keepdims=True)
@@ -632,6 +743,47 @@
     norms[1:2, :] = total
 
 
+def text_kernel(ids, own, pk, pv, keep0, keep1, send):
+    width = own.shape[1] // 2
+    rank = ids[1]
+    for d, out in enumerate((keep0, send.at[0], keep1, send.at[1])):
+        columns = pl.ds(pl.multiple_of((rank ^ d) * width, width), width)
+        out[...] = (nt(own[:, :width], pk[columns, :]) + nt(own[:, width:], pv[columns, :])).astype(BF)
+
+
+def entry_weights_kernel(ids, hid, dq, kvg, entry_norms, norms, kept, send, rows):
+    width = dq.shape[1]
+    model = hid.shape[1]
+    turned = hid[...].T
+    rows[:, :width] = nn(turned, dq[...]).astype(BF)
+    rows[:, width : 3 * width] = nn(turned, kvg[...]).astype(BF)
+    sums = jnp.concatenate([entry_norms[...], norms[...], jnp.zeros((122, model), F32)], axis=0)
+    rows[:, 3 * width :] = sums.T.astype(BF)
+    spread(ids, rows, kept, send)
+
+
+def arrived_kernel(ids, *refs):
+    feed, head, entry, (expand, shrink, pq, pm, merge, wq, wk, wv, norms) = refs[:1], refs[1:2], refs[2:4], refs[4:]
+
+    def total(terms, width, index):
+        columns = slice(index * width, (index + 1) * width)
+        value = terms[0][:, columns].astype(F32)
+        for term in terms[1:]:
+            value = value + term[:, columns].astype(F32)
+        return value
+
+    hidden, width = expand.shape[1], pq.shape[1]
+    expand[...] = total(feed, hidden, 0)
+    shrink[...] = total(feed, hidden, 1).T
+    pq[...] = total(head, width, 0)
+    pm[...] = total(head, width, 1).T
+    merge[...] = total(head, width, 2).T
+    wq[...] = total(entry, width, 0)
+    wk[...] = total(entry, width, 1)
+    wv[...] = total(entry, width, 2)
+    norms[...] = total(entry, 128, 3 * width // 128).T[:8, :]
+
+
 def entry_back_kernel(ids, keep, sent, crossed, tok, gain, resid, out):
     grad = keep[...].astype(F32) + sent[0].astype(F32) + crossed[...].astype(F32)
     normed, inverse = ln_rows(tok[...].astype(F32))
@@ -656,7 +808,7 @@
         [shaped((4 * rows, model), dtype)],
         grid=(4,),
         out_specs=[pl.BlockSpec((rows, model), lambda i, s: (i, 0))],
-        micros=4,
+        micros=3,
     )[0]
 
 
@@ -664,10 +816,6 @@
     across = partner(own, 2)
     near = partner(own, 1)
     return own, near, across, partner(across, 1)
-
-
-def sum_rows(blocks):
-    return jnp.sum(blocks.astype(F32), axis=0)
 
 
 def body(
@@ -708,7 +856,7 @@
     scalars = pl.BlockSpec(memory_space=pltpu.SMEM)
     ids, begin = pl.pallas_call(
         functools.partial(layout_kernel, rows),
-        out_shape=[shaped((8 + steps,), jnp.int32), shaped((1, rows), jnp.int32)],
+        out_shape=[shaped((9 + 2 * steps + 7,), jnp.int32), shaped((1, 2 * rows + BLOCK), jnp.int32)],
         in_specs=[scalars] * 3,
         out_specs=[scalars, pl.BlockSpec(memory_space=pltpu.VMEM)],
     )(item_lengths, prompt_lengths, place)
@@ -718,21 +866,23 @@
     own_rows = lambda columns: pl.BlockSpec((quarter, columns), lambda *g: (g[-1][1], 0))
 
     block_rows = lambda columns: pl.BlockSpec((BLOCK, columns), lambda i, *s: (i, 0))
-    hidden_one, q, kv, kv_tail, pack = run(
+    pack = run(pack_kernel, None, (merge_weight, prompt_query, prompt_merge), [shaped((3 * width, model), BF)], vmem=60)[0]
+    pack_near, pack_across = partner(pack, 1), partner(pack, 2)
+    hidden_one, q, kv, kv_tail = run(
         entry_kernel,
         None,
-        (tokens, row(entry_gain), row(entry_bias), query_weight, key_weight, value_weight, merge_weight, prompt_query, prompt_merge),
+        (after(tokens, pack), row(entry_gain), row(entry_bias), query_weight, key_weight, value_weight),
         [
             shaped((rows, model), BF),
             shaped((rows, width), BF),
             shaped((rows, 2 * width), BF),
             shaped((BLOCK, 2 * width), BF),
-            shaped((3 * width, model), BF),
         ],
         grid=(steps,),
-        in_specs=[block_rows(model)] + [None] * 8,
-        out_specs=[block_rows(model), block_rows(width), block_rows(2 * width), None, None],
-        micros=5,
+        in_specs=[block_rows(model)] + [None] * 5,
+        out_specs=[block_rows(model), block_rows(width), block_rows(2 * width), None],
+        micros=2,
+        vmem=60,
     )
     kv_near = from_behind(kv, 1)
     kv_far = from_behind(kv_tail, 2)
@@ -740,16 +890,15 @@
     pair = run(
         prompt_kernel,
         ids,
-        (after(text_states, kv), prompt_key, prompt_value),
+        (after(text_states, kv, pack_near), prompt_key, prompt_value),
         [shaped((3 * prompt_rows, 2 * width), BF)],
         grid=(3,),
         in_specs=[pl.BlockSpec((1, prompt_rows, model), lambda i, s: (s[2] + i, 0, 0)), None, None],
         out_specs=[pl.BlockSpec((prompt_rows, 2 * width), lambda i, s: (i, 0))],
         micros=1.5,
     )[0]
-    pack_near, pack_across = partner(pack, 1), partner(pack, 2)
-    pair_near, pair_across = partner(pair, 1), partner(after(pair, pack), 2)
-    hidden_grad = nt(after(output_grad, kv, pack), shrink_weight).astype(BF)
+    pair_near, pair_across = partner(pair, 1), partner(pair, 2)
+    hidden_grad = nt(after(output_grad, kv, pair), shrink_weight).astype(BF)
 
     state = [shaped((steps, heads, HD, BLOCK), F32), shaped((steps, heads, BLOCK), F32), shaped((steps, heads, BLOCK), F32)]
     state_specs = [
@@ -765,25 +914,31 @@
     acc, top, total = run(
         attend_local_kernel,
         ids,
-        (after(q, pack, pair), kv, begin),
+        (after(q, pair_near), kv, begin),
         state,
         grid=(steps,),
         in_specs=[q_spec, None, begin_spec],
         out_specs=state_specs,
         scratch=[turned(steps)] + state_scratch,
-        micros=12,
+        micros=13,
     )
     kv_near, kv_far = lax.optimization_barrier((kv_near, kv_far, acc, hidden_grad))[:2]
-    self_out, self_low, lse = run(
+    def ship_spec(side):
+        half = steps // 2
+        index = (lambda i: jnp.maximum(i - half, 0)) if side else (lambda i: jnp.minimum(i, half - 1))
+        return pl.BlockSpec((1, BLOCK + 16, 2 * width), lambda i, s: (index(jnp.minimum(i, steps - 1)), 0, 0))
+
+    self_out, self_low, lse, ship_low, ship_high, ship_first = run(
         attend_remote_kernel,
         ids,
         (q, kv_near, kv_far, begin, acc, top, total),
-        [shaped((steps, BLOCK, width), F32), shaped((steps, BLOCK, width), BF), shaped((steps, heads, BLOCK), F32)],
+        [shaped((steps, BLOCK, width), F32), shaped((steps, BLOCK, width), BF), shaped((steps, heads, BLOCK), F32)]
+        + [shaped((blocks, BLOCK + 16, 2 * width), BF) for blocks in (steps // 2, steps // 2, 1)],
         grid=(steps,),
         in_specs=[q_spec, None, None, begin_spec] + state_specs,
-        out_specs=[piece_spec, piece_spec, state_specs[1]],
+        out_specs=[piece_spec, piece_spec, state_specs[1], ship_spec(0), ship_spec(1), None],
         scratch=[turned(steps + 1)] + state_scratch,
-        micros=10,
+        micros=9,
     )
     low_rows = lax.all_to_all(self_low, "mp", 0, 0)
     pack_across, pair_across = lax.optimization_barrier((pack_across, pair_across, self_low))[:2]
@@ -802,20 +957,25 @@
         micros=11,
     )
 
+    ship_low, ship_high, ship_f = after((ship_low, ship_high, ship_first), hidden_three)
+    ship_low, ship_f = from_behind(ship_low, -1), from_behind(ship_f, -2)
+
     three_near, three_across = partner(hidden_three, 1), partner(hidden_three, 2)
     low0, pre0, out0, part0, low1, pre1, out1, part1 = feed(
         ids, 0, hidden_three, three_near, hidden_grad, expand_weight, shrink_weight
     )
-    three_across = after(three_across, part1)
+    three_across, ship_low, ship_f = after((three_across, ship_low, ship_f), part1)
+    ship_high = from_behind(after(ship_high, ship_low), -1)
     threes = (hidden_three, three_near, three_across, partner(three_across, 1))
     sent1, out_sent1 = partner(part1, 1), partner(out1, 1)
     low2, pre2, out2, part2, low3, pre3, out3, part3 = feed(
         ids, 2, threes[2], threes[3], hidden_grad, expand_weight, shrink_weight
     )
+    part3, sent1, out_sent1, ship_high = after((part3, sent1, out_sent1, ship_high), part2)
     partial = (part2.astype(F32) + partner(part3, 1).astype(F32)).astype(BF)
     across = partner(partial, 2)
     out_partial = (out2.astype(F32) + partner(after(out3, partial), 1).astype(F32)).astype(BF)
-    feed_grads = feed_weights(ids, threes, (pre0, pre1, pre2, pre3), (low0, low1, low2, low3), after(output_grad, partial))
+    feed_grads = feed_weights(ids, threes, after((pre0, pre1, pre2, pre3), partial), (low0, low1, low2, low3), output_grad)
     feed_sum = lax.psum_scatter(feed_grads, SEQ, scatter_dimension=0, tiled=True)
     across = after(across, feed_grads, out_partial)
     out_across = partner(after(out_partial, across), 2)
@@ -833,125 +993,159 @@
     )
     self_grad = lax.all_to_all(shg, "mp", 0, 0)
 
+    pair_sent = partner(pair_send, 1)
     pieces = shaped((model, 3 * width), BF)
     head_keep0, head_keep1, head_send = run(
         head_weights_kernel,
         ids,
         (hidden_two, cqg, cog, cross_out, slg, low_rows),
         [pieces, pieces, shaped((2, *pieces.shape), BF)],
-        micros=4,
-    )
-
-    def added(*terms):
-        total = terms[0].astype(F32)
-        for term in terms[1:]:
-            total = total + term.astype(F32)
-        return total.astype(BF)
-
-    pair_sent, head_sent = partner(pair_send, 1), partner(head_send, 1)
+        micros=5,
+        vmem=60,
+    )
+    head_sent = partner(head_send, 1)
+    head_half = added(head_keep1, head_sent[1])
+    self_grad, out_across, pair_sent, head_half = after((self_grad, out_across, pair_sent, head_half), head_keep0)
+    head_across = partner(head_half, 2)
+    grad_n, grad_f = from_behind(self_grad, -1), from_behind(self_grad[:1], -2)
     pair_half = added(pair_keep1, pair_sent[1])
-    self_grad = after(self_grad, head_keep0, pair_half)
-    pair_across = partner(after(pair_half, self_grad), 2)
-    head_across = partner(after(added(head_keep1, head_sent[1]), self_grad), 2)
+    pair_across = partner(pair_half, 2)
 
     lse_spec = state_specs[1]
     stat4 = shaped((steps, heads, BLOCK), F32)
-    dkv_near, dkv_far, dq_part, delta = run(
-        back_remote_kernel,
-        ids,
-        (q, kv_near, kv_far, begin, self_grad, self_out, lse),
-        [shaped((rows, 2 * width), BF), shaped((BLOCK, 2 * width), BF), state[0], stat4],
+    dkv, dq_part, delta = run(
+        back_local_kernel,
+        ids,
+        (q, kv, begin, after(self_grad, pair_half), self_out, lse),
+        [shaped((rows, 2 * width), F32), state[0], stat4],
         grid=(steps,),
-        in_specs=[q_spec, None, None, begin_spec, piece_spec, piece_spec, lse_spec],
-        out_specs=[None, None, state_specs[0], lse_spec],
-        scratch=[turned(steps + 1), pltpu.VMEM((steps + 1, BLOCK, 2 * width), F32), state_scratch[0]],
-        micros=10,
-    )
-    from_near = from_behind(dkv_near, -1)
-    from_far = from_behind(dkv_far, -2)
-
+        in_specs=[q_spec, None, begin_spec, piece_spec, piece_spec, lse_spec],
+        out_specs=[None, state_specs[0], lse_spec],
+        scratch=[turned(steps), pltpu.VMEM((steps, BLOCK, 2 * width), F32)],
+        micros=15,
+    )
+    pair_across, grad_n, grad_f = after((pair_across, grad_n, grad_f), dq_part)
     pair_sum = added(pair_keep0, pair_sent[0], pair_across).reshape(3, prompt_rows, 2 * width)
     placed = lax.dynamic_update_slice_in_dim(jnp.zeros((items, prompt_rows, 2 * width), BF), pair_sum, base, 0)
-    placed = after(placed, dkv_near).reshape(items * prompt_rows, 2 * width)
-    dq_part = after(dq_part, placed)
-    own_pair = over_shards(placed).astype(BF)
-
-    dkv, dq = run(
-        back_local_kernel,
-        ids,
-        (q, kv, begin, self_grad, lse, delta, dq_part),
-        [shaped((rows, 2 * width), F32), shaped((rows, width), BF)],
+    placed = placed.reshape(shards // 2, 2, -1, 2 * width)
+    own = own_bit(0)
+    text_sum = ShardSum(
+        lax.dynamic_index_in_dim(placed, own, 1, keepdims=False), lax.dynamic_index_in_dim(placed, 1 - own, 1, keepdims=False)
+    )
+    dq = run(
+        back_query_kernel,
+        ids,
+        (q, kv_near, kv_far, begin, self_grad, lse, delta, after(dq_part, text_sum.kept)),
+        [shaped((rows, width), BF)],
         grid=(steps,),
-        in_specs=[q_spec, None, begin_spec, piece_spec, lse_spec, lse_spec, state_specs[0]],
-        out_specs=[None, q_spec],
-        scratch=[turned(steps), pltpu.VMEM((steps, BLOCK, 2 * width), F32), state_scratch[0]],
-        micros=14,
-    )
-    text_part = nt(own_pair[:, :width], prompt_key) + nt(own_pair[:, width:], prompt_value)
-    text_blocks = jnp.swapaxes(text_part.astype(BF).reshape(-1, ranks, width), 0, 1)
-    text_own = sum_rows(lax.all_to_all(text_blocks, "mp", 0, 0)).astype(BF)
-
-    head_rows = added(head_keep0, head_sent[0], head_across)
-    out_rows = added(after_cross, out0, out_sent1, out_across)
-    layer_output = assemble(ids, gather(after(out_rows, head_rows)), BF)
-
-    from_near, from_far = lax.optimization_barrier((from_near, from_far, dq))[:2]
+        in_specs=[q_spec, None, None, begin_spec, piece_spec, lse_spec, lse_spec, state_specs[0]],
+        out_specs=[q_spec],
+        scratch=[turned(steps + 1), state_scratch[0]],
+        micros=7,
+    )[0]
+    text_sum.step(ids, dq)
+    far = shards // 2
+    spread_out = [shaped((far, model // shards, 3 * width + 128), BF)] * 2
+    grad_n, grad_f = after((grad_n, grad_f), dq, text_sum.kept)
+    held = lambda i: jnp.minimum(i, steps - 1)
+    near_piece = pl.BlockSpec((1, BLOCK, width), lambda i, s: (held(i), 0, 0))
+    kvg = run(
+        back_key_kernel,
+        ids,
+        (kv, begin, ship_low, ship_high, grad_n, ship_f, grad_f, dkv),
+        [shaped((rows, 2 * width), BF)],
+        grid=(steps + 1,),
+        in_specs=[None, pl.BlockSpec((1, BLOCK), lambda i, s: (0, steps + i)), ship_spec(0), ship_spec(1), near_piece] + [None] * 3,
+        scratch=[pltpu.VMEM((heads, BLOCK), F32)] * 2 + [pltpu.VMEM((steps, BLOCK, 2 * width), F32)],
+        micros=8,
+    )[0]
+
     quarter_out = shaped((quarter, model), BF)
-    kvg, one_keep0, one_keep1, one_send, entry_norms = run(
-        key_sum_kernel,
-        ids,
-        (dkv, from_near, from_far, hidden_one, dq, query_weight, key_weight, value_weight, row(entry_gain), row(entry_bias)),
-        [shaped((rows, 2 * width), BF), quarter_out, quarter_out, shaped((2, *quarter_out.shape), BF), shaped((2, model), F32)],
+    one_keep0, one_keep1, one_send, entry_norms = run(
+        one_grad_kernel,
+        ids,
+        (kvg, hidden_one, dq, query_weight, key_weight, value_weight, row(entry_gain), row(entry_bias)),
+        [quarter_out, quarter_out, shaped((2, *quarter_out.shape), BF), shaped((2, model), F32)],
         micros=3,
     )
     one_sent = partner(one_send, 1)
-    one_across = partner(added(one_keep1, one_sent[1]), 2)
-    head_sum = over_shards(after(head_rows, from_near, from_far))
-    entry_grads = jnp.concatenate([tn(hidden_one, dq), tn(hidden_one, kvg)], axis=1).astype(BF)
-    one_across = after(one_across, entry_grads)
-    entry_sum = over_shards(entry_grads)
+    entry_rows = run(
+        entry_weights_kernel,
+        ids,
+        (hidden_one, after(dq, one_send), kvg, entry_norms, norm_grads),
+        spread_out,
+        scratch=[pltpu.VMEM((model, 3 * width + 128), BF)],
+        micros=4,
+    )
+    entry_sum = ShardSum(*entry_rows)
+    head_rows = added(head_keep0, head_sent[0], after(head_across, kvg))
+    one_half = added(one_keep1, after(one_sent, entry_rows[0], head_rows)[1])
+    one_across = partner(one_half, 2)
+    own_pair = added(*text_sum.last(ids, one_half))
+    text_out = shaped((prompt_rows * items // shards, width), BF)
+    text_keep0, text_keep1, text_send = run(
+        text_kernel, ids, (own_pair, prompt_key, prompt_value), [text_out, text_out, shaped((2, *text_out.shape), BF)], micros=1
+    )
+    text_sent = partner(text_send, 1)
+    text_half = added(text_keep1, text_sent[1])
+    text_across = partner(text_half, 2)
+    one_across = after(one_across, text_half, head_rows, feed_sum)
+    head_sum = lax.psum_scatter(after(head_rows, feed_sum), SEQ, scatter_dimension=0, tiled=True)
     grad_rows = run(
         entry_back_kernel,
         ids,
         (one_keep0, one_sent, one_across, tokens, row(entry_gain), resid),
         [wide(BF)],
         in_specs=[None] * 3 + [own_rows(model)] + [None] * 2,
+        micros=2,
+        vmem=60,
+    )[0]
+    grad_pieces = gather(grad_rows)
+
+    text_own = added(text_keep0, text_sent[0], after(text_across, grad_rows))
+    entry_sum.step(ids, grad_rows)
+    prompt_all = to_all(jnp.concatenate([own_pair, text_own], axis=1))
+    flat_text = text_states.reshape(items * prompt_rows, model)
+    key_prompt, value_prompt = tn(flat_text, prompt_all[:, :width]), tn(flat_text, prompt_all[:, width : 2 * width])
+    text_grad = prompt_all[:, 2 * width :].astype(F32).reshape(items, prompt_rows, width)
+
+    tokens_grad = assemble(ids, grad_pieces, F32)
+    out_rows = added(after_cross, out0, out_sent1, out_across)
+    out_pieces = gather(after(out_rows, grad_rows))
+    layer_output = assemble(ids, out_pieces, BF)
+
+    part = model // shards
+    square, turned_square = shaped((part, width), F32), shaped((width, part), F32)
+    expand_grad, shrink_grad, pq_grad, pm_grad, merge_grad, wq_grad, wk_grad, wv_grad, norm_sum = run(
+        arrived_kernel,
+        None,
+        (feed_sum, head_sum, *entry_sum.last(ids, grad_rows)),
+        [shaped((part, hidden_units), F32), shaped((hidden_units, part), F32)]
+        + [square, turned_square, turned_square, square, square, square, shaped((8, part), F32)],
         micros=3,
-    )[0]
-    tokens_grad = assemble(ids, gather(grad_rows), F32)
-
-    prompt_all = from_shards(jnp.concatenate([own_pair, text_own], axis=1))
-    prompt_grads = tn(text_states.reshape(items * prompt_rows, model), prompt_all[:, : 2 * width])
-    text_grad = prompt_all[:, 2 * width :].astype(F32).reshape(items, prompt_rows, width)
-
-    norm_rows = jnp.concatenate([after(entry_norms, one_across), norm_grads[2:4], norm_grads[0:2], jnp.zeros((2, model), F32)])
-    norm_blocks = jnp.swapaxes(norm_rows.reshape(8, shards, model // shards), 0, 1)
-    norm_sum = jnp.sum(lax.all_to_all(norm_blocks, SEQ, 0, 0), axis=0)
+    )
     norm_sum = norm_sum + partner(norm_sum, 1)
     norm_sum = norm_sum + partner(norm_sum, 2)
-
-    cut = lambda array, index: array[:, index * width : (index + 1) * width]
-    feed_sum = feed_sum.astype(F32)
     return (
         layer_output,
         tokens_grad,
         text_grad,
         norm_sum[0],
         norm_sum[1],
+        norm_sum[4],
+        norm_sum[5],
         norm_sum[2],
         norm_sum[3],
-        norm_sum[4],
-        norm_sum[5],
-        cut(entry_sum, 0),
-        cut(entry_sum, 1),
-        cut(entry_sum, 2),
-        cut(head_sum, 2).T,
-        cut(head_sum, 0),
-        prompt_grads[:, :width],
-        prompt_grads[:, width:],
-        cut(head_sum, 1).T,
-        feed_sum[:, :hidden_units],
-        feed_sum[:, hidden_units:].T,
+        wq_grad,
+        wk_grad,
+        wv_grad,
+        merge_grad,
+        pq_grad,
+        key_prompt,
+        value_prompt,
+        pm_grad,
+        expand_grad,
+        shrink_grad,
     )
 
 

time: 418 us -> 384 us (0.919)
  Pallas kernels: 118 us -> 145 us
  local copies, waits for them, and re-layouts: 59 us -> 39.6 us
  starting transfers between devices: 71.6 us -> 55.9 us
  other arithmetic: 32.5 us -> 20.5 us
  waiting for transfers between devices: 102 us -> 91.5 us
    all_to_all x6 -> x0, starting transfers between devices: 29 us -> none  [the longest x3 15.5 us: over_shards(): return sum_rows(lax.all_to_all(half, 'far', 0, 0))]
    pallas_call x16 -> x25, Pallas kernels: 117 us -> 143 us  [run(): pl.pallas_call(functools.partial(kernel, None) if ids is None else kernel...]
    ppermute x29 -> x31, waiting for transfers between devices: 31.7 us -> 8.26 us  [partner(): lax.ppermute(value, 'mp', [(rank, rank ^ step) for rank in range(count)])]
    unnamed x179 -> x198, local copies, waits for them, and re-layouts: 50.8 us -> 37 us
    ppermute x4 -> x7, waiting for transfers between devices: 0.01 us -> 11 us  [from_behind(): lax.ppermute(value, SEQ, [(source, source + steps) for source in range(le...]
    all_to_all x1, waiting for transfers between devices: 0.01 us -> 9.74 us  [body(): self_grad = lax.all_to_all(shg, 'mp', 0, 0)]
    all_to_all x6 -> x0, waiting for transfers between devices: 7.38 us -> none  [the longest x1 5.83 us: body(): norm_sum = jnp.sum(lax.all_to_all(norm_blocks, SEQ, 0, 0), axis=0)]
    convert_element_type x4 -> x0, other arithmetic: 6.72 us -> none  [the longest x3 5.51 us: over_shards(): half = (kept.astype(F32) + sent.astype(F32)).astype(BF)]
  transfers between devices with their start and end apart: 46 -> 51, of which waited for: 15 -> 16; matrix products, arithmetic and copies ran while one was open for 13% -> 8% of each run, Pallas kernels for 18% -> 35%
where the time goes in v3:
time: 384 us; the launch traced here: 377 us
  Pallas kernels  145 us (38%)
  waiting for transfers between devices  91.5 us (24%)
  starting transfers between devices  55.9 us (15%)
  local copies, waits for them, and re-layouts  39.6 us (10%)
  other arithmetic  20.5 us (5%)
  between operations  17.4 us (5%)
  matrix products  7.71 us (2%)
    pallas_call x25, Pallas kernels, run(): pl.pallas_call(functools.partial(kernel, None) if ids is None else kernel...  143 us
    ppermute x9, waiting for transfers between devices, across_bit(): lax.ppermute(value, SEQ, [(shard, shard ^ 1 << bit) for shard in range(1...  54 us
    unnamed x198, local copies, waits for them, and re-layouts  37 us
    ppermute x31, starting transfers between devices, partner(): lax.ppermute(value, 'mp', [(rank, rank ^ step) for rank in range(count)])  18.9 us
    ppermute x9, starting transfers between devices, across_bit(): lax.ppermute(value, SEQ, [(shard, shard ^ 1 << bit) for shard in range(1...  15.2 us
    ppermute x7, starting transfers between devices, from_behind(): lax.ppermute(value, SEQ, [(source, source + steps) for source in range(le...  14.6 us
    convert_element_type x9, other arithmetic, added(): return total.astype(BF)  13.2 us
    ppermute x7, waiting for transfers between devices, from_behind(): lax.ppermute(value, SEQ, [(source, source + steps) for source in range(le...  11 us
  transfers between devices with their start and end apart: 51, of which 16 were waited for; matrix products, arithmetic and copies ran while one was open for 8% of the time, Pallas kernels for 35%

profile of v3, /device:TPU:0, one launch (start us, length us, event | category | flops | bytes accessed | tf_op | source)
XLA Modules:
  0.0 377.3 jit_solution(13750890274148086906)
XLA Ops:
  13.0 6.6 %shard_map.350 = (bf16[1024,1024]{1,0:T(8,128)(2,1)}, bf16[1024,256]{1,0:T(8,128)(2,1)}, bf16[1024,512]{1,0:T(8,128)(2,1)}, bf16[256,512]{1,0:T(8,128)(2,1)}) custom-call(bf16[1024,1024]{1,0:T(8,128)(2,1)} %tok.4, f32[1,1024]{1,0:T(1,128)} %bitcast.86, f32[1,1024]{1,0:T(1,128)} %bitcast.96, bf16[1024,256]{1,0:T(8,128)(2,1)} %wq.3, bf16[1024,256]{1,0:T(8,128)(2,1)} %wk.3, ...), custom_call_target="tpu_custom_call" | custom-call | flops 1000000000 | bytes 1000 | tf_op jit(solution)/shard_map/pallas_call | solution.py:135
  19.6 4.4 %collective-permute-start = (bf16[1024,512]{1,0:T(8,128)(2,1)}, bf16[1024,512]{1,0:T(8,128)(2,1)}, u32[]{:S(2)}, u32[]{:S(2)}) collective-permute-start(bf16[1024,512]{1,0:T(8,128)(2,1)} %get-tuple-element.151.kv), channel_id=1, source_target_pairs={{0,4},{4,8},{8,12},{12,16},{16,20},{20,24},{24,28},{1,5},{5,9},{9,... | collective-permute-start | bytes 3145736 | tf_op jit(solution)/shard_map/ppermute | solution.py:48
  32.5 5.3 %convolution_convert_fusion.dh_a.dh_b = bf16[1024,1024]{1,0:T(8,128)(2,1)} fusion(bf16[1024,1024]{1,0:T(8,128)(2,1)} %og.1, bf16[1024,1024]{1,0:T(8,128)(2,1)S(1)} %copy-done.21), kind=kOutput, calls=%fused_computation.5 | convolution fusion | flops 2148532224 | bytes 6291456 | tf_op jit(solution)/shard_map/dot_general | solution.py:22
  37.8 12.0 %shard_map.352 = (f32[4,4,64,256]{3,2,1,0:T(8,128)S(1)}, f32[4,4,256]{2,1,0:T(4,128)S(1)}, f32[4,4,256]{2,1,0:T(4,128)S(1)}) custom-call(s32[24]{0:T(128)S(1)} %copy-done.16, bf16[1024,256]{1,0:T(8,128)(2,1)S(1)} %copy-done.63, bf16[1024,512]{1,0:T(8,128)(2,1)S(1)} %copy-done.24, s32[1,2304]{1,0:T(1,128)S(1)} %copy-done.61), custom_call_target="tpu_custom_call" | custom-call | flops 6499999744 | bytes 1000 | tf_op jit(solution)/shard_map/pallas_call | solution.py:135
  61.6 8.5 %all-to-all-done.low = bf16[4,256,256]{2,1,0:T(8,128)(2,1)S(1)} async-done(((bf16[4,256,256]{2,1,0:T(8,128)(2,1)}), bf16[4,256,256]{2,1,0:T(8,128)(2,1)S(1)}, u32[]{:S(2)}, u32[]{:S(2)}) %all-to-all-start) | async-done | bytes 524320 | tf_op jit(solution)/shard_map/all_to_all | solution.py:943
  71.7 10.3 %shard_map.354 = (f32[256,1024]{1,0:T(8,128)S(1)}, bf16[256,1024]{1,0:T(8,128)(2,1)S(1)}, bf16[256,1024]{1,0:T(8,128)(2,1)S(1)}, f32[16,256]{1,0:T(8,128)S(1)}, ...) custom-call(s32[24]{0:T(128)S(1)} %copy-done.16, bf16[1024,1024]{1,0:T(8,128)(2,1)} %tok.4, ...), custom_call_target="tpu_custom_call" | custom-call | flops 5500000256 | bytes 1000 | tf_op jit(solution)/shard_map/pallas_call | solution.py:135
  88.7 11.0 %shard_map.355 = (bf16[256,1024]{1,0:T(8,128)(2,1)S(1)}, bf16[256,1024]{1,0:T(8,128)(2,1)S(1)}, bf16[256,1024]{1,0:T(8,128)(2,1)S(1)}, bf16[256,1024]{1,0:T(8,12...) custom-call(s32[24]{0:T(128)S(1)} %copy-done.16, ...), custom_call_target="tpu_custom_call" | custom-call | flops 6000000000 | bytes 1000 | tf_op jit(solution)/shard_map/pallas_call | solution.py:135
  104.6 10.8 %collective-permute-done.11.ship_f = bf16[1,272,512]{2,1,0:T(8,128)(2,1)S(1)} collective-permute-done((bf16[1,272,512]{2,1,0:T(8,128)(2,1)S(1)}, bf16[1,272,512]{2,1,0:T(8,128)(2,1)S(1)}, u32[]{:S(2)}, u32[]{:S(2)}) %collective-permute-start.11) | collective-permute-done | bytes 278560 | tf_op jit(solution)/shard_map/ppermute | solution.py:48
  118.6 11.8 %shard_map.356 = (bf16[256,1024]{1,0:T(8,128)(2,1)S(1)}, bf16[256,1024]{1,0:T(8,128)(2,1)S(1)}, bf16[256,1024]{1,0:T(8,128)(2,1)S(1)}, bf16[256,1024]{1,0:T(8,12...) custom-call(s32[24]{0:T(128)S(1)} %copy-done.16, ...), custom_call_target="tpu_custom_call" | custom-call | flops 6000000000 | bytes 1000 | tf_op jit(solution)/shard_map/pallas_call | solution.py:135
  138.7 12.6 %shard_map.357 = bf16[1024,2048]{1,0:T(8,128)(2,1)} custom-call(s32[24]{0:T(128)} %get-tuple-element.148.ids, bf16[256,1024]{1,0:T(8,128)(2,1)} %copy-done.39, bf16[256,1024]{1,0:T(8,128)(2,1)} %copy-done.42, bf16[256,1024]{1,0:T(8,128)(2,1)} %copy-done.43, bf16[256,1024]{1,0:T(8,128)(2,1)} %copy-done.44, bf16[256,1024]{1,0:T(8,128)(2,1)} %copy-done.68, ...), custom_call_target="tpu_custom_call" | custom-call | flops 4499999744 | bytes 1000 | tf_op jit(solution)/shard_map/pallas_call | solution.py:135
  159.4 15.0 %shard_map.358 = (bf16[256,1024]{1,0:T(8,128)(2,1)S(1)}, bf16[256,1024]{1,0:T(8,128)(2,1)S(1)}, bf16[256,1024]{1,0:T(8,128)(2,1)S(1)}, f32[256,1024]{1,0:T(8,128...) custom-call(s32[24]{0:T(128)S(1)} %copy-done.17, ...), custom_call_target="tpu_custom_call" | custom-call | flops 7500000256 | bytes 1000 | tf_op jit(solution)/shard_map/pallas_call | solution.py:135
  176.8 6.5 %shard_map.359 = (bf16[1024,768]{1,0:T(8,128)(2,1)}, bf16[1024,768]{1,0:T(8,128)(2,1)}, bf16[2,1024,768]{2,1,0:T(8,128)(2,1)}) custom-call(s32[24]{0:T(128)} %get-tuple-element.148.ids, bf16[256,1024]{1,0:T(8,128)(2,1)} %copy-done.76, bf16[256,1024]{1,0:T(8,128)(2,1)} %copy-done.79, bf16[256,1024]{1,0:T(8,128)(2,1)} %copy-done.78, ...), custom_call_target="tpu_custom_call" | custom-call | flops 2500000000 | bytes 1000 | tf_op jit(solution)/shard_map/pallas_call | solution.py:135
  193.8 9.7 %all-to-all-done.1.grad = bf16[4,256,256]{2,1,0:T(8,128)(2,1)S(1)} async-done(((bf16[4,256,256]{2,1,0:T(8,128)(2,1)}), bf16[4,256,256]{2,1,0:T(8,128)(2,1)S(1)}, u32[]{:S(2)}, u32[]{:S(2)}) %all-to-all-start.1) | async-done | bytes 524320 | tf_op jit(solution)/shard_map/all_to_all | solution.py:994
  211.1 14.5 %shard_map.360 = (f32[1024,512]{1,0:T(8,128)S(1)}, f32[4,4,64,256]{3,2,1,0:T(8,128)S(1)}, f32[4,4,256]{2,1,0:T(4,128)S(1)}) custom-call(s32[24]{0:T(128)S(1)} %copy-done.18, bf16[1024,256]{1,0:T(8,128)(2,1)S(1)} %copy-done.64, bf16[1024,512]{1,0:T(8,128)(2,1)S(1)} %copy-done.25, s32[1,2304]{1,0:T(1,128)S(1)} %copy-done.61, ...), custom_call_target="tpu_custom_call" | custom-call | flops 7500000256 | bytes 1000 | tf_op jit(solution)/shard_map/pallas_call | solution.py:135
  227.1 4.1 %collective-permute-start.25 = (bf16[4,128,512]{2,1,0:T(8,128)(2,1)S(1)}, bf16[4,128,512]{2,1,0:T(8,128)(2,1)S(1)}, u32[]{:S(2)}, u32[]{:S(2)}) collective-permute-start(bf16[4,128,512]{2,1,0:T(8,128)(2,1)S(1)} %get-tuple-element.317), channel_id=1, source_target_pairs={{0,4},{4,0},{8,12},{12,8},{16,20},{20,16},{24,28},{28,24},{1,5},{5... | collective-permute-start | bytes 1572872 | tf_op jit(solution)/shard_map/ppermute | solution.py:56
  235.3 12.5 %collective-permute-done.25.sent = bf16[4,128,512]{2,1,0:T(8,128)(2,1)S(1)} collective-permute-done((bf16[4,128,512]{2,1,0:T(8,128)(2,1)S(1)}, bf16[4,128,512]{2,1,0:T(8,128)(2,1)S(1)}, u32[]{:S(2)}, u32[]{:S(2)}) %collective-permute-start.25) | collective-permute-done | bytes 524320 | tf_op jit(solution)/shard_map/ppermute | solution.py:56
  248.6 6.0 %shard_map.363.kvg = bf16[1024,512]{1,0:T(8,128)(2,1)S(1)} custom-call(s32[24]{0:T(128)S(1)} %copy-done.18, bf16[1024,512]{1,0:T(8,128)(2,1)S(1)} %copy-done.26, s32[1,2304]{1,0:T(1,128)S(1)} %copy-done.61, bf16[2,272,512]{2,1,0:T(8,128)(2,1)S(1)} %copy-done.28, bf16[2,272,512]{2,1,0:T(8,128)(2,1)S(1)} %copy-done.30, ...), custom_call_target="tpu_custom_call" | custom-call | flops 4000000000 | bytes 1000 | tf_op jit(solution)/shard_map/pallas_call | solution.py:135
  271.9 5.4 %collective-permute-start.30 = (bf16[1,128,512]{2,1,0:T(8,128)(2,1)S(1)}, bf16[1,128,512]{2,1,0:T(8,128)(2,1)S(1)}, u32[]{:S(2)}, u32[]{:S(2)}) collective-permute-start(bf16[1,128,512]{2,1,0:T(8,128)(2,1)S(1)} %get-tuple-element.250), channel_id=1, source_target_pairs={{0,16},{4,20},{8,24},{12,28},{16,0},{20,4},{24,8},{28,12},{1,17},{... | collective-permute-start | bytes 393224 | tf_op jit(solution)/shard_map/ppermute | solution.py:56
  290.4 4.4 %shard_map.368.refs_0_ = bf16[256,1024]{1,0:T(8,128)(2,1)} custom-call(s32[24]{0:T(128)} %get-tuple-element.148.ids, bf16[256,1024]{1,0:T(8,128)(2,1)} %copy-done.12, bf16[2,256,1024]{2,1,0:T(8,128)(2,1)} %collective-permute-done.26.sent, bf16[256,1024]{1,0:T(8,128)(2,1)} %copy-done.97, bf16[1024,1024]{1,0:T(8,128)(2,1)} %tok.4, f32[1,1024]{1,0:T(1,128)} %bitcast.87, ...), custom_call_target="tpu_custom_call" | custom-call | flops 1000000000 | bytes 1000 | tf_op jit(solution)/shard_map/pallas_call | solution.py:135
  303.9 6.7 %collective-permute-done.39 = bf16[128,768]{1,0:T(8,128)(2,1)S(1)} collective-permute-done((bf16[128,768]{1,0:T(8,128)(2,1)S(1)}, bf16[128,768]{1,0:T(8,128)(2,1)S(1)}, u32[]{:S(2)}, u32[]{:S(2)}) %collective-permute-start.39) | collective-permute-done | bytes 196640 | tf_op jit(solution)/shard_map/ppermute | solution.py:56
  314.0 10.0 %collective-permute-done.43.sent = bf16[2,128,896]{2,1,0:T(8,128)(2,1)S(1)} collective-permute-done((bf16[2,128,896]{2,1,0:T(8,128)(2,1)S(1)}, bf16[2,128,896]{2,1,0:T(8,128)(2,1)S(1)}, u32[]{:S(2)}, u32[]{:S(2)}) %collective-permute-start.43) | collective-permute-done | bytes 458784 | tf_op jit(solution)/shard_map/ppermute | solution.py:56
  325.1 9.7 %collective-permute-done.40 = bf16[2,128,768]{2,1,0:T(8,128)(2,1)S(1)} collective-permute-done((bf16[2,128,768]{2,1,0:T(8,128)(2,1)S(1)}, bf16[2,128,768]{2,1,0:T(8,128)(2,1)S(1)}, u32[]{:S(2)}, u32[]{:S(2)}) %collective-permute-start.40) | collective-permute-done | bytes 393248 | tf_op jit(solution)/shard_map/ppermute | solution.py:56
  337.5 4.2 %shard_map.370 = f32[1024,1024]{1,0:T(8,128)} custom-call(s32[24]{0:T(128)S(1)} %copy-done.19, bf16[256,1024]{1,0:T(8,128)(2,1)S(1)} %copy-done.1, bf16[256,1024]{1,0:T(8,128)(2,1)} %collective-permute-done.35.refs_1_, bf16[256,1024]{1,0:T(8,128)(2,1)S(1)} %collective-permute-done.36.refs_2_, bf16[256,1024]{1,0:T(8,128)(2,1)} %collective-permute-done.37.refs_3_), custom_call_target="tpu_custom_call" | custom-call | flops 1500000000 | bytes 1000 | tf_op jit(solution)/shard_map/pallas_call | solution.py:135
  345.6 10.5 %collective-permute-done.41 = bf16[2,2,128,768]{3,2,0,1:T(8,128)(2,1)} collective-permute-done((bf16[2,2,128,768]{3,2,0,1:T(8,128)(2,1)}, bf16[2,2,128,768]{3,2,0,1:T(8,128)(2,1)}, u32[]{:S(2)}, u32[]{:S(2)}) %collective-permute-start.41) | collective-permute-done | bytes 786464 | tf_op jit(solution)/shard_map/ppermute | solution.py:56
  (337 shorter events, 147.1 us)
Async XLA Ops:
  10.4 46.9 %collective-permute-start.4 = (bf16[768,1024]{1,0:T(8,128)(2,1)}, bf16[768,1024]{1,0:T(8,128)(2,1)}, u32[]{:S(2)}, u32[]{:S(2)}) collective-permute-start(bf16[768,1024]{1,0:T(8,128)(2,1)} %shard_map.349.refs_0_), channel_id=1, source_target_pairs={{0,2},{1,3},{2,0},{3,1},{4,6},{5,7},{6,4},{7,5},{8,10},{9,11},{10,... | collective-permute-start | bytes 4718600 | tf_op jit(solution)/shard_map/ppermute | solution.py:39
  19.6 30.2 %collective-permute-start = (bf16[1024,512]{1,0:T(8,128)(2,1)}, bf16[1024,512]{1,0:T(8,128)(2,1)}, u32[]{:S(2)}, u32[]{:S(2)}) collective-permute-start(bf16[1024,512]{1,0:T(8,128)(2,1)} %get-tuple-element.151.kv), channel_id=1, source_target_pairs={{0,4},{4,8},{8,12},{12,16},{16,20},{20,24},{24,28},{1,5},{5,9},{9,... | collective-permute-start | bytes 3145736 | tf_op jit(solution)/shard_map/ppermute | solution.py:48
  24.0 25.8 %collective-permute-start.1 = (bf16[256,512]{1,0:T(8,128)(2,1)}, bf16[256,512]{1,0:T(8,128)(2,1)}, u32[]{:S(2)}, u32[]{:S(2)}) collective-permute-start(bf16[256,512]{1,0:T(8,128)(2,1)} %get-tuple-element.152), channel_id=1, source_target_pairs={{0,8},{4,12},{8,16},{12,20},{16,24},{20,28},{1,9},{5,13},{9,17},{1... | collective-permute-start | bytes 786440 | tf_op jit(solution)/shard_map/ppermute | solution.py:48
  31.6 25.7 %collective-permute-start.5 = (bf16[384,512]{1,0:T(8,128)(2,1)S(1)}, bf16[384,512]{1,0:T(8,128)(2,1)}, u32[]{:S(2)}, u32[]{:S(2)}) collective-permute-start(bf16[384,512]{1,0:T(8,128)(2,1)S(1)} %shard_map.351.refs_4_), channel_id=1, source_target_pairs={{0,2},{1,3},{2,0},{3,1},{4,6},{5,7},{6,4},{7,5},{8,10},{9,11},{10,... | collective-permute-start | bytes 1179656 | tf_op jit(solution)/shard_map/ppermute | solution.py:39
  61.3 221.6 %reduce-scatter.3.cloned.1.call-start = ((), (), s32[]{:S(2)}) async-start(), calls=%async_computation.4 | async-start | bytes 4718592 | tf_op jit(solution)/shard_map/reduce_scatter | solution.py:979
  85.6 30.6 %collective-permute-start.9 = (bf16[256,1024]{1,0:T(8,128)(2,1)S(1)}, bf16[256,1024]{1,0:T(8,128)(2,1)S(1)}, u32[]{:S(2)}, u32[]{:S(2)}) collective-permute-start(bf16[256,1024]{1,0:T(8,128)(2,1)S(1)} %get-tuple-element.166.h_a.refs_0_), channel_id=1, source_target_pairs={{0,2},{1,3},{2,0},{3,1},{4,6},{5,7},{6,4},{7,5},{8,10},{9,11},{10,... | collective-permute-start | bytes 1572872 | tf_op jit(solution)/shard_map/ppermute | solution.py:39
  85.9 30.2 %collective-permute-start.10 = (bf16[2,272,512]{2,1,0:T(8,128)(2,1)S(1)}, bf16[2,272,512]{2,1,0:T(8,128)(2,1)S(1)}, u32[]{:S(2)}, u32[]{:S(2)}) collective-permute-start(bf16[2,272,512]{2,1,0:T(8,128)(2,1)S(1)} %copy-done.34), channel_id=1, source_target_pairs={{4,0},{8,4},{12,8},{16,12},{20,16},{24,20},{28,24},{5,1},{9,5},{13... | collective-permute-start | bytes 1671176 | tf_op jit(solution)/shard_map/ppermute | solution.py:48
  87.4 28.1 %collective-permute-start.11 = (bf16[1,272,512]{2,1,0:T(8,128)(2,1)S(1)}, bf16[1,272,512]{2,1,0:T(8,128)(2,1)S(1)}, u32[]{:S(2)}, u32[]{:S(2)}) collective-permute-start(bf16[1,272,512]{2,1,0:T(8,128)(2,1)S(1)} %copy-done.52), channel_id=1, source_target_pairs={{8,0},{12,4},{16,8},{20,12},{24,16},{28,20},{9,1},{13,5},{17,9},{2... | collective-permute-start | bytes 835592 | tf_op jit(solution)/shard_map/ppermute | solution.py:48
  183.3 20.2 %collective-permute-start.20 = (bf16[2,384,512]{2,1,0:T(8,128)(2,1)}, bf16[2,384,512]{2,1,0:T(8,128)(2,1)}, u32[]{:S(2)}, u32[]{:S(2)}) collective-permute-start(bf16[2,384,512]{2,1,0:T(8,128)(2,1)} %get-tuple-element.206), channel_id=1, source_target_pairs={{0,1},{1,0},{2,3},{3,2},{4,5},{5,4},{6,7},{7,6},{8,9},{9,8},{10,11... | collective-permute-start | bytes 2359304 | tf_op jit(solution)/shard_map/ppermute | solution.py:39
  183.8 19.7 %collective-permute-start.19 = (bf16[256,1024]{1,0:T(8,128)(2,1)}, bf16[256,1024]{1,0:T(8,128)(2,1)}, u32[]{:S(2)}, u32[]{:S(2)}) collective-permute-start(bf16[256,1024]{1,0:T(8,128)(2,1)} %add_convert_fusion.1), channel_id=1, source_target_pairs={{0,2},{1,3},{2,0},{3,1},{4,6},{5,7},{6,4},{7,5},{8,10},{9,11},{10,... | collective-permute-start | bytes 1572872 | tf_op jit(solution)/shard_map/ppermute | solution.py:39
  184.1 19.4 %all-to-all-start.1 = ((bf16[4,256,256]{2,1,0:T(8,128)(2,1)}), bf16[4,256,256]{2,1,0:T(8,128)(2,1)S(1)}, u32[]{:S(2)}, u32[]{:S(2)}) async-start(bf16[4,256,256]{2,1,0:T(8,128)(2,1)} %get-tuple-element.204), calls=%async_computation.1 | async-start | bytes 1048576 | tf_op jit(solution)/shard_map/all_to_all | solution.py:994
  187.6 171.2 %reduce-scatter.5.cloned.1.call-start = ((), (), s32[]{:S(2)}) async-start(), calls=%async_computation.5 | async-start | bytes 1769472 | tf_op jit(solution)/shard_map/reduce_scatter | solution.py:1093
  204.6 21.0 %collective-permute-start.22 = (bf16[384,512]{1,0:T(8,128)(2,1)S(1)}, bf16[384,512]{1,0:T(8,128)(2,1)S(1)}, u32[]{:S(2)}, u32[]{:S(2)}) collective-permute-start(bf16[384,512]{1,0:T(8,128)(2,1)S(1)} %fusion.6), channel_id=1, source_target_pairs={{0,2},{1,3},{2,0},{3,1},{4,6},{5,7},{6,4},{7,5},{8,10},{9,11},{10,... | collective-permute-start | bytes 1179656 | tf_op jit(solution)/shard_map/ppermute | solution.py:39
  205.0 20.7 %collective-permute-start.23 = (bf16[4,256,256]{2,1,0:T(8,128)(2,1)S(1)}, bf16[4,256,256]{2,1,0:T(8,128)(2,1)S(1)}, u32[]{:S(2)}, u32[]{:S(2)}) collective-permute-start(bf16[4,256,256]{2,1,0:T(8,128)(2,1)S(1)} %all-to-all-done.1.grad), channel_id=1, source_target_pairs={{4,0},{8,4},{12,8},{16,12},{20,16},{24,20},{28,24},{5,1},{9,5},{13... | collective-permute-start | bytes 1572872 | tf_op jit(solution)/shard_map/ppermute | solution.py:48
  206.3 19.4 %collective-permute-start.24 = (bf16[1,256,256]{2,1,0:T(8,128)(2,1)S(1)}, bf16[1,256,256]{2,1,0:T(8,128)(2,1)S(1)}, u32[]{:S(2)}, u32[]{:S(2)}) collective-permute-start(bf16[1,256,256]{2,1,0:T(8,128)(2,1)S(1)} %slice.56), channel_id=1, source_target_pairs={{8,0},{12,4},{16,8},{20,12},{24,16},{28,20},{9,1},{13,5},{17,9},{2... | collective-permute-start | bytes 393224 | tf_op jit(solution)/shard_map/ppermute | solution.py:48
  227.1 20.7 %collective-permute-start.25 = (bf16[4,128,512]{2,1,0:T(8,128)(2,1)S(1)}, bf16[4,128,512]{2,1,0:T(8,128)(2,1)S(1)}, u32[]{:S(2)}, u32[]{:S(2)}) collective-permute-start(bf16[4,128,512]{2,1,0:T(8,128)(2,1)S(1)} %get-tuple-element.317), channel_id=1, source_target_pairs={{0,4},{4,0},{8,12},{12,8},{16,20},{20,16},{24,28},{28,24},{1,5},{5... | collective-permute-start | bytes 1572872 | tf_op jit(solution)/shard_map/ppermute | solution.py:56
  231.2 34.9 %collective-permute-start.27 = (bf16[1024,768]{1,0:T(8,128)(2,1)S(1)}, bf16[1024,768]{1,0:T(8,128)(2,1)S(1)}, u32[]{:S(2)}, u32[]{:S(2)}) collective-permute-start(bf16[1024,768]{1,0:T(8,128)(2,1)S(1)} %copy-done.94), channel_id=1, source_target_pairs={{0,2},{1,3},{2,0},{3,1},{4,6},{5,7},{6,4},{7,5},{8,10},{9,11},{10,... | collective-permute-start | bytes 4718600 | tf_op jit(solution)/shard_map/ppermute | solution.py:39
  277.3 22.2 %collective-permute-start.42 = (bf16[4,128,896]{2,1,0:T(8,128)(2,1)}, bf16[4,128,896]{2,1,0:T(8,128)(2,1)}, u32[]{:S(2)}, u32[]{:S(2)}) collective-permute-start(bf16[4,128,896]{2,1,0:T(8,128)(2,1)} %get-tuple-element.260), channel_id=1, source_target_pairs={{0,4},{4,0},{8,12},{12,8},{16,20},{20,16},{24,28},{28,24},{1,5},{5... | collective-permute-start | bytes 2752520 | tf_op jit(solution)/shard_map/ppermute | solution.py:56
  295.2 29.9 %collective-permute-start.36 = (bf16[256,1024]{1,0:T(8,128)(2,1)}, bf16[256,1024]{1,0:T(8,128)(2,1)S(1)}, u32[]{:S(2)}, u32[]{:S(2)}) collective-permute-start(bf16[256,1024]{1,0:T(8,128)(2,1)} %shard_map.368.refs_0_), channel_id=1, source_target_pairs={{0,2},{1,3},{2,0},{3,1},{4,6},{5,7},{6,4},{7,5},{8,10},{9,11},{10,... | collective-permute-start | bytes 1572872 | tf_op jit(solution)/shard_map/ppermute | solution.py:39
  302.5 21.6 %collective-permute-start.43 = (bf16[2,128,896]{2,1,0:T(8,128)(2,1)S(1)}, bf16[2,128,896]{2,1,0:T(8,128)(2,1)S(1)}, u32[]{:S(2)}, u32[]{:S(2)}) collective-permute-start(bf16[2,128,896]{2,1,0:T(8,128)(2,1)S(1)} %get-tuple-element.263), channel_id=1, source_target_pairs={{0,8},{4,12},{8,0},{12,4},{16,24},{20,28},{24,16},{28,20},{1,9},{5... | collective-permute-start | bytes 1376264 | tf_op jit(solution)/shard_map/ppermute | solution.py:56
  310.8 24.0 %collective-permute-start.40 = (bf16[2,128,768]{2,1,0:T(8,128)(2,1)S(1)}, bf16[2,128,768]{2,1,0:T(8,128)(2,1)S(1)}, u32[]{:S(2)}, u32[]{:S(2)}) collective-permute-start(bf16[2,128,768]{2,1,0:T(8,128)(2,1)S(1)} %pad_maximum_fusion.2), channel_id=1, source_target_pairs={{0,8},{4,12},{8,0},{12,4},{16,24},{20,28},{24,16},{28,20},{1,9},{5... | collective-permute-start | bytes 1179656 | tf_op jit(solution)/shard_map/ppermute | solution.py:56
  313.0 24.4 %collective-permute-start.35 = (bf16[256,1024]{1,0:T(8,128)(2,1)S(1)}, bf16[256,1024]{1,0:T(8,128)(2,1)}, u32[]{:S(2)}, u32[]{:S(2)}) collective-permute-start(bf16[256,1024]{1,0:T(8,128)(2,1)S(1)} %copy-done.1), channel_id=1, source_target_pairs={{0,1},{1,0},{2,3},{3,2},{4,5},{5,4},{6,7},{7,6},{8,9},{9,8},{10,11... | collective-permute-start | bytes 1572872 | tf_op jit(solution)/shard_map/ppermute | solution.py:39
  313.0 23.8 %collective-permute-start.33 = (bf16[256,1024]{1,0:T(8,128)(2,1)}, bf16[256,1024]{1,0:T(8,128)(2,1)}, u32[]{:S(2)}, u32[]{:S(2)}) collective-permute-start(bf16[256,1024]{1,0:T(8,128)(2,1)} %add_convert_fusion.refs_0_), channel_id=1, source_target_pairs={{0,2},{1,3},{2,0},{3,1},{4,6},{5,7},{6,4},{7,5},{8,10},{9,11},{10,... | collective-permute-start | bytes 1572872 | tf_op jit(solution)/shard_map/ppermute | solution.py:39
  335.9 20.3 %collective-permute-start.41 = (bf16[2,2,128,768]{3,2,0,1:T(8,128)(2,1)}, bf16[2,2,128,768]{3,2,0,1:T(8,128)(2,1)}, u32[]{:S(2)}, u32[]{:S(2)}) collective-permute-start(bf16[2,2,128,768]{3,2,0,1:T(8,128)(2,1)} %pad_maximum_fusion.1), channel_id=1, source_target_pairs={{0,4},{4,0},{8,12},{12,8},{16,20},{20,16},{24,28},{28,24},{1,5},{5... | collective-permute-start | bytes 2359304 | tf_op jit(solution)/shard_map/ppermute | solution.py:56
  (125 other events, 997.0 us)
Sparse Core Ops, SparseCore 0:
  151.5 100.5 reduce-scatter.2
  283.0 73.0 reduce-scatter.4
